TPU v7x, 32 devices: a whole 2x2x4 slice. The times are simulated.
32 devices in a mesh: group: 2 (over y), member: 4 (over z), strip: 2 (over x), sub: 2 (over core).
Axes of the slice: x: 2, y: 2, z: 4, core: 2. Of those that a mesh axis runs over, the one named last changes fastest.
Arguments:
- noisy: bfloat16 [8, 128, 128, 256], P(('group', 'member'), None, 'strip', 'sub'), parts along dimension 0, may hold values from -6 to 6
- condition: bfloat16 [24, 128, 256], P('group', ('strip', 'member'), 'sub'), parts along dimension 0, may hold values from -6 to 6
- levels: int32 [8], P(('group', 'member')), parts along dimension 0, may hold values from 0 to 17
- enc_w1: bfloat16 [9, 128, 12], replicated, may hold values from -0.625 to 0.625
- enc_b1: float32 [128], replicated, may hold values from -4 to 4
- enc_w2: bfloat16 [9, 128, 128], replicated, may hold values from -0.1875 to 0.1875
- enc_b2: float32 [128], replicated, may hold values from -4 to 4
- den_wa: bfloat16 [9, 128, 256], replicated, may hold values from -0.125 to 0.125
- den_ba: float32 [128], replicated, may hold values from -4 to 4
- noise_gain: float32 [128], replicated, may hold values from -6 to 6
- den_wb: bfloat16 [9, 128, 128], replicated, may hold values from -0.1875 to 0.1875
Outputs:
- denoised: bfloat16 [8, 128, 128, 256], P(('group', 'member'), None, 'strip', 'sub'), parts along dimension 0
There are 2 independent parts, one for each index of `group`. A program takes and returns all parts, laid end to end along the dimension named above; an argument that names none is the same for every part. Nothing has to cross between parts.
All inputs are finite; a program needn't handle non-finite values.
Results may differ from a plain program's by a relative error of at most 0.0043.
The roundings to bfloat16 on the way count: a program that leaves them out, or rounds other values in their place, can miss the bound.
Values may be sent and summed in bfloat16 or wider, within the bound.
No kernel may reach another device: no remote copies, remote signals or barrier semaphores. Data moves between devices by JAX's collectives and lax.ppermute only.
A program may use at most 64 MiB of HBM per device.

v0:
```python
import functools

import jax
import jax.numpy as jnp
from jax import lax
from jax.experimental import pallas as pl
from jax.experimental.pallas import tpu as pltpu
from jax.sharding import PartitionSpec as P

LEVELS = 18
SIGMA_DATA = 0.5
SIG_LOW = 0.25
SIG_HIGH = 4.0

BF16 = jnp.bfloat16
F32 = jnp.float32
NT = (((1,), (1,)), ((), ()))
NN = (((1,), (0,)), ((), ()))
VMEM_LIMIT = 48 * 2**20

BASE = 8
HALO = 4
EDGE = 8
SLOT = 16


def prep_kernel(scale_ref, field_ref, pairs_ref, left_ref, right_ref, buf, *, pitch):
    chans, rows, cols = field_ref.shape
    buf[...] = field_ref[...].astype(F32).reshape(chans * rows, cols)
    c_in = scale_ref[0]
    for q in range(rows // 2):
        for h in range(2):
            row = buf[pl.ds(2 * q + h, chans, stride=rows), :]
            cells = (c_in * row.T).astype(BF16)
            lanes = slice(h * chans, (h + 1) * chans)
            pairs_ref[q * pitch + 2:q * pitch + 2 + cols, lanes] = cells
            left_ref[2 * q:2 * q + 2, lanes] = cells[:2]
            right_ref[2 * q:2 * q + 2, lanes] = cells[cols - 2:]


def pack_kernel(*refs, geo, block_count):
    top_ref, bottom_ref, left_ref, right_ref = refs[:4]
    blocks = refs[4:4 + block_count]
    outs = list(refs[4 + block_count:])
    n_strip, n_sub, n_member = geo["n_strip"], geo["n_sub"], geo["n_member"]
    pitch, cols, rows, cin = geo["pitch"], geo["cols"], geo["rows"], geo["cin"]
    half = cin // 2
    member = lax.axis_index("member")
    strip = lax.axis_index("strip")
    sub = lax.axis_index("sub")

    whole = outs[0]
    edge_rows = rows
    for k, block in enumerate(blocks):
        tall = block.shape[1]
        if block_count == 1:
            at = 0
        else:
            at = pl.multiple_of(lax.rem(member - k + n_member, n_member) * tall, tall)
        for c in range(cin):
            lanes = slice((c // half) * cols, (c // half + 1) * cols)
            start = 2 * (rows // 2) + (c % half) * rows + at
            if block_count != 1:
                start = pl.multiple_of(start, 16)
            whole[pl.ds(start, tall), lanes] = block[c]
    noisy_rows = 2 * (rows // 2)
    whole_left = left_ref[...]
    whole_right = right_ref[...]

    def cond_edge(c, top):
        lanes = slice((c // half) * cols, (c // half + 1) * cols)
        start = noisy_rows + (c % half) * rows
        if top:
            return whole[start:start + EDGE, lanes]
        return whole[start + rows - EDGE:start + rows, lanes]

    def pick(flag, a, b):
        return jnp.where(flag, a.astype(F32), b.astype(F32)).astype(BF16)

    def pair_edge(top):
        if top:
            return top_ref[2:2 + cols, :]
        return bottom_ref[pitch + 2:pitch + 2 + cols, :]

    if n_sub == 2:
        whole[:noisy_rows, :] = pick(sub == 0, whole_right, whole_left)
        rest = outs[1:]
    else:
        whole[:noisy_rows, :] = whole_left
        other = outs[1]
        other[noisy_rows:, :] = whole[noisy_rows:, :]
        other[:noisy_rows, :] = whole_right
        rest = outs[2:]
    tops = [None] if n_strip == 2 else [True, False]
    lefts = [None] if n_sub == 2 else [True, False]
    at = 0
    for top in tops:
        if top is None:
            pair = pick(strip == 0, pair_edge(False), pair_edge(True))
        else:
            pair = pair_edge(top)
        strip_out = rest[at]
        at += 1
        strip_out[:cols, :] = pair
        for c in range(cin):
            lanes = slice((c // half) * cols, (c // half + 1) * cols)
            if top is None:
                cells = pick(strip == 0, cond_edge(c, False), cond_edge(c, True))
            else:
                cells = cond_edge(c, top)
            start = cols + (c % half) * EDGE
            strip_out[start:start + EDGE, lanes] = cells
        for left in lefts:
            corner_out = rest[at]
            at += 1
            if left is None:
                corner = pick(sub == 0, pair[cols - 2:], pair[:2])
            else:
                corner = pair[:2] if left else pair[cols - 2:]
            corner_out[:2, :] = corner
            corner_out[16:, :] = strip_out[cols:, :]


def main_kernel(*refs, geo, n_strip_in, n_sub_in):
    it = iter(refs)
    scal = next(it)
    field_hbm = next(it)
    pairs_hbm = next(it)
    own = next(it)
    sub_in = [next(it) for _ in range(n_sub_in)]
    strip_in = []
    diag_in = []
    for _ in range(n_strip_in):
        strip_in.append(next(it))
        diag_in.append([next(it) for _ in range(n_sub_in)])
    w1, b1, w2, b2, wa, ba, gain, wb = [next(it) for _ in range(8)]
    out_hbm = next(it)
    (xe, xn, xf, xh, m1, m2, mn, mf, mb, cr, ch, lw, field, out, obuf, sems) = list(it)

    n_strip, n_sub = geo["n_strip"], geo["n_sub"]
    pitch, cols, rows, cin = geo["pitch"], geo["cols"], geo["rows"], geo["cin"]
    chans = 128
    half = cin // 2
    npair = rows // 2
    noisy_rows = 2 * npair
    strip = lax.axis_index("strip")
    sub = lax.axis_index("sub")
    above, below = strip > 0, strip < n_strip - 1
    before, after = sub > 0, sub < n_sub - 1

    get_pairs = pltpu.make_async_copy(
        pairs_hbm, xn.at[pl.ds(BASE + pitch, npair * pitch), :], sems.at[0])
    get_pairs.start()
    get_field = pltpu.make_async_copy(field_hbm, field, sems.at[1])
    get_field.start()

    def keep(flag, cells):
        return jnp.where(flag, cells.astype(F32), 0.0)

    def blocks_of(dst, src, lanes):
        zero = jnp.zeros((chans, chans), BF16)
        for b in range(3):
            a0 = b * 2 * chans
            b0 = (3 + b) * 2 * chans
            taps = [src[3 * a + b, :, lanes] for a in range(3)]
            dst[:chans, a0:a0 + chans] = taps[0]
            dst[:chans, a0 + chans:a0 + 2 * chans] = taps[1]
            dst[chans:, a0:a0 + chans] = zero
            dst[chans:, a0 + chans:a0 + 2 * chans] = taps[0]
            dst[:chans, b0:b0 + chans] = taps[2]
            dst[:chans, b0 + chans:b0 + 2 * chans] = zero
            dst[chans:, b0:b0 + chans] = taps[1]
            dst[chans:, b0 + chans:b0 + 2 * chans] = taps[2]

    blocks_of(m2, w2, slice(0, chans))
    blocks_of(mn, wa, slice(0, chans))
    blocks_of(mf, wa, slice(chans, 2 * chans))
    blocks_of(mb, wb, slice(0, chans))
    m1[...] = jnp.zeros_like(m1)
    for b in range(3):
        for n in range(6):
            for a in range(3):
                at = b * 8 * SLOT + (n + a) * SLOT
                m1[at:at + cin, n * chans:(n + 1) * chans] = w1[3 * a + b]

    cr[...] = jnp.zeros_like(cr)
    ch[...] = jnp.zeros_like(ch)

    def lanes_of(c):
        return slice((c // half) * cols, (c // half + 1) * cols)

    def fill(dst, body, tops):
        for c in range(cin):
            at = noisy_rows + (c % half) * rows
            dst[pl.ds(HALO * SLOT + c, rows, stride=SLOT), :] = (
                body[at:at + rows, lanes_of(c)].astype(F32))
            for source, flag, is_top, first in tops:
                at = first + (c % half) * EDGE
                cells = source[at:at + EDGE, lanes_of(c)].astype(F32)
                if is_top:
                    dst[pl.ds(c, HALO, stride=SLOT), :] = keep(flag, cells[EDGE - HALO:])
                else:
                    dst[pl.ds((HALO + rows) * SLOT + c, HALO, stride=SLOT), :] = keep(flag, cells[:HALO])

    strip_top, strip_bottom = strip_in[0], strip_in[-1]
    diag_top, diag_bottom = diag_in[0], diag_in[-1]
    fill(cr, own, [(strip_top, above, True, cols), (strip_bottom, below, False, cols)])
    windows = geo["windows"]
    for w in range(windows):
        cells = cr[6 * SLOT * w:6 * SLOT * w + 8 * SLOT, :].T
        at = BASE - HALO + w * pitch
        lw[at + HALO:at + HALO + cols, :] = cells.astype(BF16)
    for k in range(n_sub_in):
        fill(ch, sub_in[k], [(diag_top[k], above, True, 16), (diag_bottom[k], below, False, 16)])
        for w in range(windows):
            cells = ch[6 * SLOT * w:6 * SLOT * w + 8 * SLOT, :].T
            at = BASE - HALO + w * pitch
            if k == 0:
                lw[at:at + HALO, :] = keep(before, cells[cols - HALO:]).astype(BF16)
            if k == n_sub_in - 1:
                lw[at + HALO + cols:at + 2 * HALO + cols, :] = keep(after, cells[:HALO]).astype(BF16)

    def inside(y, left, right, first, count, low_row):
        y = y.reshape(count, pitch, 2 * chans)
        col = lax.broadcasted_iota(jnp.int32, (count, 8, 2 * chans), 1)
        head = jnp.where((col >= left) | before, y[:, :8], 0.0)
        tail = jnp.where((col < right - (pitch - 8)) | after, y[:, pitch - 8:], 0.0)
        y = jnp.concatenate([head, y[:, 8:pitch - 8], tail], axis=1)
        parts = []
        for i in range(count):
            halves = []
            for h in range(2):
                row = 2 * (first + i) + h - low_row
                cells = y[i, :, h * chans:(h + 1) * chans]
                if row < 0:
                    cells = jnp.where(above, cells, 0.0)
                elif row >= rows:
                    cells = jnp.where(below, cells, 0.0)
                halves.append(cells)
            parts.append(jnp.concatenate(halves, axis=1))
        return parts

    def silu(v):
        return v * (0.5 * jnp.tanh(0.5 * v) + 0.5)

    def twice(v):
        return jnp.concatenate([v, v], axis=1)

    bias1 = twice(b1[...])
    per = 4
    for w0 in range(0, windows, per):
        count = min(per, windows - w0)
        span = count * pitch
        at = BASE - HALO + w0 * pitch
        lhs = jnp.concatenate([lw[at + b:at + b + span, :] for b in range(3)], axis=1)
        y = lax.dot_general(lhs, m1[...], NN, preferred_element_type=F32)
        for p in range(3):
            z = silu(y[:, p * 2 * chans:(p + 1) * 2 * chans] + bias1)
            for i in range(count):
                j = 3 * (w0 + i) + p
                if j < npair + 3:
                    cells = inside(z[i * pitch:(i + 1) * pitch], 3, 3 + cols, j, 1, 3)[0]
                    xe[BASE + j * pitch:BASE + (j + 1) * pitch, :] = cells.astype(BF16)

    def conv(src, weight, first, count):
        span = count * pitch
        at = BASE + first * pitch
        lhs = jnp.concatenate(
            [src[at + p * pitch + b:at + p * pitch + b + span, :] for p in range(2) for b in range(3)],
            axis=1)
        return lax.dot_general(lhs, weight[...], NT, preferred_element_type=F32)

    def chunks(total, size):
        return [(at, min(size, total - at)) for at in range(0, total, size)]

    bias2 = twice(b2[...])
    for first, count in chunks(npair + 2, 9):
        parts = inside(conv(xe, m2, first, count) + bias2, 2, 2 + cols, first, count, 2)
        for i, cells in enumerate(parts):
            at = BASE + (first + i) * pitch
            xf[at:at + pitch, :] = cells.astype(BF16)

    get_pairs.wait()
    for k in range(n_sub_in):
        for q in range(npair):
            at = BASE + (q + 1) * pitch
            cells = sub_in[k][2 * q:2 * q + 2, :]
            if k == 0:
                xn[at:at + 2, :] = keep(before, cells).astype(BF16)
            if k == n_sub_in - 1:
                xn[at + 2 + cols:at + 4 + cols, :] = keep(after, cells).astype(BF16)
    for source, corners, flag, j in (
        (strip_top, diag_top, above, 0), (strip_bottom, diag_bottom, below, npair + 1)):
        at = BASE + j * pitch
        xn[at + 2:at + 2 + cols, :] = keep(flag, source[:cols, :]).astype(BF16)
        xn[at:at + 2, :] = keep(flag & before, corners[0][:2, :]).astype(BF16)
        xn[at + 2 + cols:at + 4 + cols, :] = keep(flag & after, corners[-1][:2, :]).astype(BF16)

    offset = twice(ba[...] + scal[3] * gain[...])
    for first, count in chunks(npair + 1, 9):
        y = conv(xn, mn, first, count) + conv(xf, mf, first, count) + offset
        parts = inside(silu(y), 1, 1 + cols, first, count, 1)
        for i, cells in enumerate(parts):
            at = BASE + (first + i) * pitch
            xh[at:at + pitch, :] = cells.astype(BF16)

    get_field.wait()
    c_skip, c_out = scal[1], scal[2]
    group = 8
    puts = []
    for first, count in chunks(npair, group):
        y = conv(xh, mb, first, count)
        tall = 2 * count
        for i in range(count):
            for h in range(2):
                cells = y[i * pitch:i * pitch + cols, h * chans:(h + 1) * chans]
                obuf[pl.ds(2 * i + h, chans, stride=tall), :] = cells.T
        update = obuf[...].reshape(chans, tall, cols)
        r0 = 2 * first
        skip = field[:, r0:r0 + tall, :].astype(F32)
        out[:, r0:r0 + tall, :] = (c_skip * skip + c_out * update).astype(BF16)
        put = pltpu.make_async_copy(
            out.at[:, pl.ds(r0, tall), :], out_hbm.at[:, pl.ds(r0, tall), :],
            sems.at[2 + first // group])
        put.start()
        puts.append(put)
    for put in puts:
        put.wait()


def local(
    noisy, condition, levels, enc_w1, enc_b1, enc_w2, enc_b2, den_wa, den_ba, noise_gain, den_wb
):
    field = noisy[0]
    chans, rows, cols = field.shape
    cin = condition.shape[0]
    n_member = lax.axis_size("member")
    n_strip = lax.axis_size("strip")
    n_sub = lax.axis_size("sub")
    pitch = cols + 2 * HALO
    npair = rows // 2
    geo = dict(n_strip=n_strip, n_sub=n_sub, n_member=n_member, pitch=pitch, cols=cols, rows=rows,
               cin=cin, windows=-(-(rows + 6) // 6))

    if n_member <= 4:
        blocks = [condition]
        for k in range(1, n_member):
            blocks.append(
                lax.ppermute(condition, "member", [(i, (i + k) % n_member) for i in range(n_member)]))
    else:
        blocks = [lax.all_gather(condition, "member", axis=1, tiled=True)]

    level_value = levels[0].astype(F32)
    noise_sigma = SIG_LOW * (SIG_HIGH / SIG_LOW) ** (level_value / (LEVELS - 1))
    spread = noise_sigma * noise_sigma + SIGMA_DATA * SIGMA_DATA
    c_in = 1.0 / jnp.sqrt(spread)
    c_skip = SIGMA_DATA * SIGMA_DATA / spread
    c_out = noise_sigma * SIGMA_DATA / jnp.sqrt(spread)
    c_noise = jnp.log(noise_sigma) / 4.0
    scal = jnp.stack([c_in, c_skip, c_out, c_noise])

    tall = 16
    steps = rows // tall
    pairs, left, right = pl.pallas_call(
        functools.partial(prep_kernel, pitch=pitch),
        grid=(steps,),
        out_shape=[
            jax.ShapeDtypeStruct((npair * pitch, 2 * chans), BF16),
            jax.ShapeDtypeStruct((2 * npair, 2 * chans), BF16),
            jax.ShapeDtypeStruct((2 * npair, 2 * chans), BF16),
        ],
        in_specs=[
            pl.BlockSpec(memory_space=pltpu.SMEM),
            pl.BlockSpec((chans, tall, cols), lambda i: (0, i, 0)),
        ],
        out_specs=[
            pl.BlockSpec((npair * pitch // steps, 2 * chans), lambda i: (i, 0)),
            pl.BlockSpec((2 * npair // steps, 2 * chans), lambda i: (i, 0)),
            pl.BlockSpec((2 * npair // steps, 2 * chans), lambda i: (i, 0)),
        ],
        scratch_shapes=[pltpu.VMEM((chans * tall, cols), F32)],
        compiler_params=pltpu.CompilerParams(vmem_limit_bytes=VMEM_LIMIT),
        cost_estimate=pl.CostEstimate(flops=0, bytes_accessed=16 * 2**20, transcendentals=0),
        name="prep",
    )(scal, field)

    whole_shape = jax.ShapeDtypeStruct((2 * npair + cin // 2 * rows, 2 * cols), BF16)
    strip_shape = jax.ShapeDtypeStruct((cols + cin // 2 * EDGE, 2 * cols), BF16)
    diag_shape = jax.ShapeDtypeStruct((16 + cin // 2 * EDGE, 2 * cols), BF16)
    n_sub_out = 1 if n_sub == 2 else 2
    n_strip_out = 1 if n_strip == 2 else 2
    out_shape = [whole_shape] * n_sub_out
    for _ in range(n_strip_out):
        out_shape += [strip_shape] + [diag_shape] * n_sub_out
    last = npair // 2 - 1
    vmem = pl.BlockSpec(memory_space=pltpu.VMEM)
    packed = pl.pallas_call(
        functools.partial(pack_kernel, geo=geo, block_count=len(blocks)),
        grid=(1,),
        out_shape=out_shape,
        in_specs=[
            pl.BlockSpec((2 * pitch, 2 * chans), lambda i: (0, 0)),
            pl.BlockSpec((2 * pitch, 2 * chans), lambda i: (last, 0)),
        ] + [vmem] * (2 + len(blocks)),
        out_specs=[vmem] * len(out_shape),
        compiler_params=pltpu.CompilerParams(vmem_limit_bytes=VMEM_LIMIT),
        name="pack",
    )(pairs, pairs, left, right, *blocks)

    def up(n):
        return [(i, i - 1) for i in range(1, n)]

    def down(n):
        return [(i, i + 1) for i in range(n - 1)]

    sub_moves = [up(n_sub) + down(n_sub)] if n_sub == 2 else [up(n_sub), down(n_sub)]
    strip_moves = [up(n_strip) + down(n_strip)] if n_strip == 2 else [up(n_strip), down(n_strip)]
    rest = packed[n_sub_out:]
    strip_in = []
    at = 0
    for move in strip_moves:
        got = [lax.ppermute(rest[at], "strip", move)]
        at += 1
        corners = []
        for side in sub_moves:
            pairs_of = [(i * n_sub + j, k * n_sub + l) for i, k in move for j, l in side]
            corners.append(lax.ppermute(rest[at], ("strip", "sub"), pairs_of))
            at += 1
        strip_in.append(got + corners[::-1])
    strip_in = [x for one in strip_in[::-1] for x in one]
    sub_in = [lax.ppermute(x, "sub", move) for x, move in zip(packed[:n_sub_out], sub_moves)][::-1]

    flat = BASE + (npair + 3) * pitch + 16
    windows = geo["windows"]
    any_spec = pl.BlockSpec(memory_space=pl.ANY)
    smem = pl.BlockSpec(memory_space=pltpu.SMEM)
    steps_out = -(-npair // 8)
    result = pl.pallas_call(
        functools.partial(main_kernel, geo=geo, n_strip_in=n_strip_out, n_sub_in=n_sub_out),
        out_shape=jax.ShapeDtypeStruct((chans, rows, cols), BF16),
        in_specs=[smem, any_spec, any_spec] + [vmem] * (1 + n_sub_out + len(strip_in) + 8),
        out_specs=any_spec,
        scratch_shapes=[
            pltpu.VMEM((flat, 2 * chans), BF16),
            pltpu.VMEM((flat, 2 * chans), BF16),
            pltpu.VMEM((flat, 2 * chans), BF16),
            pltpu.VMEM((flat, 2 * chans), BF16),
            pltpu.VMEM((3 * 8 * SLOT, 6 * chans), BF16),
            pltpu.VMEM((2 * chans, 12 * chans), BF16),
            pltpu.VMEM((2 * chans, 12 * chans), BF16),
            pltpu.VMEM((2 * chans, 12 * chans), BF16),
            pltpu.VMEM((2 * chans, 12 * chans), BF16),
            pltpu.VMEM(((6 * windows + 2) * SLOT, cols), F32),
            pltpu.VMEM(((6 * windows + 2) * SLOT, cols), F32),
            pltpu.VMEM((BASE + windows * pitch + 16, 8 * SLOT), BF16),
            pltpu.VMEM((chans, rows, cols), BF16),
            pltpu.VMEM((chans, rows, cols), BF16),
            pltpu.VMEM((chans * 16, cols), F32),
            pltpu.SemaphoreType.DMA((2 + steps_out,)),
        ],
        compiler_params=pltpu.CompilerParams(vmem_limit_bytes=VMEM_LIMIT),
        name="denoise",
    )(scal, field, pairs, packed[0], *sub_in, *strip_in, jnp.swapaxes(enc_w1, 1, 2),
      enc_b1[None], enc_w2, enc_b2[None], den_wa, den_ba[None], noise_gain[None], den_wb)
    return result[None]


def solution(mesh):
    return jax.shard_map(
        local,
        mesh=mesh,
        in_specs=(
            P(("group", "member"), None, "strip", "sub"),
            P("group", ("strip", "member"), "sub"),
            P(("group", "member")),
            P(),
            P(),
            P(),
            P(),
            P(),
            P(),
            P(),
            P(),
        ),
        out_specs=P(("group", "member"), None, "strip", "sub"),
        check_vma=False,
    )
```

profile of v0, /device:TPU:0, one launch (start us, length us, event | category | flops | bytes accessed | tf_op | source)
XLA Modules:
  0.0 41.7 jit_solution(1317323592157085104)
XLA Ops:
  0.0 4.0 %collective-permute-start.1 = (bf16[12,16,128]{2,1,0:T(8,128)(2,1)}, bf16[12,16,128]{2,1,0:T(8,128)(2,1)S(1)}, u32[]{:S(2)}, u32[]{:S(2)}) collective-permute-start(bf16[12,16,128]{2,1,0:T(8,128)(2,1)} %refs_4_.1), channel_id=1, source_target_pairs={{0,8},{4,12},{8,0},{12,4},{1,9},{5,13},{9,1},{13,5},{2,10},{6,14},... | collective-permute-start | bytes 147464 | tf_op jit(solution)/shard_map/ppermute | solution.py:349
  4.0 1.6 %collective-permute-start = (bf16[12,16,128]{2,1,0:T(8,128)(2,1)}, bf16[12,16,128]{2,1,0:T(8,128)(2,1)S(1)}, u32[]{:S(2)}, u32[]{:S(2)}) collective-permute-start(bf16[12,16,128]{2,1,0:T(8,128)(2,1)} %refs_4_.1), channel_id=1, source_target_pairs={{0,4},{4,8},{8,12},{12,0},{1,5},{5,9},{9,13},{13,1},{2,6},{6,10},{... | collective-permute-start | bytes 147464 | tf_op jit(solution)/shard_map/ppermute | solution.py:349
  5.6 2.2 %collective-permute-start.2 = (bf16[12,16,128]{2,1,0:T(8,128)(2,1)}, bf16[12,16,128]{2,1,0:T(8,128)(2,1)S(1)}, u32[]{:S(2)}, u32[]{:S(2)}) collective-permute-start(bf16[12,16,128]{2,1,0:T(8,128)(2,1)} %refs_4_.1), channel_id=1, source_target_pairs={{0,12},{4,0},{8,4},{12,8},{1,13},{5,1},{9,5},{13,9},{2,14},{6,2},{... | collective-permute-start | bytes 147464 | tf_op jit(solution)/shard_map/ppermute | solution.py:349
  8.8 0.1 pad_maximum_fusion.scale_ref.refs_0_
  8.8 1.6 %copy-done = bf16[1,128,64,128]{3,2,1,0:T(8,128)(2,1)S(1)} copy-done((bf16[1,128,64,128]{3,2,1,0:T(8,128)(2,1)S(1)}, bf16[1,128,64,128]{3,2,1,0:T(8,128)(2,1)}, u32[]{:S(2)}) %copy-start) | copy-done | bytes 2097176
  10.4 2.8 %prep.1 = (bf16[4352,256]{1,0:T(8,128)(2,1)S(1)}, bf16[64,256]{1,0:T(8,128)(2,1)S(1)}, bf16[64,256]{1,0:T(8,128)(2,1)S(1)}) custom-call(f32[4]{0:T(128)S(1)} %pad_maximum_fusion.scale_ref.refs_0_, bf16[128,64,128]{2,1,0:T(8,128)(2,1)S(1)} %bitcast.7), custom_call_target="tpu_custom_call" | custom-call | bytes 16777216 | tf_op jit(solution)/shard_map/prep/pallas_call | solution.py:364
  13.2 0.0 collective-permute-done.1.refs_6_
  13.2 0.0 collective-permute-done.refs_5_
  13.3 0.0 collective-permute-done.2.refs_7_
  13.3 0.0 copy-start.1
  13.3 0.0 copy-start.2
  13.3 0.0 copy-start.3
  13.3 0.0 copy-start.5
  13.3 0.0 copy-start.6
  13.3 0.0 copy-start.7
  13.3 0.0 copy-start.8
  13.4 0.0 copy-start.9
  13.4 0.1 pack.1
  13.5 0.1 collective-permute-start.3
  13.5 1.6 %collective-permute-start.4 = (bf16[176,256]{1,0:T(8,128)(2,1)S(1)}, bf16[176,256]{1,0:T(8,128)(2,1)S(1)}, u32[]{:S(2)}, u32[]{:S(2)}) collective-permute-start(bf16[176,256]{1,0:T(8,128)(2,1)S(1)} %get-tuple-element.15), channel_id=1, source_target_pairs={{2,0},{0,2},{3,1},{1,3},{6,4},{4,6},{7,5},{5,7},{10,8},{8,10},{11,... | collective-permute-start | bytes 270344 | tf_op jit(solution)/shard_map/ppermute | solution.py:422
  15.1 0.3 collective-permute-start.5
  15.4 3.4 %collective-permute-done.5.refs_6_ = bf16[64,256]{1,0:T(8,128)(2,1)S(1)} collective-permute-done((bf16[64,256]{1,0:T(8,128)(2,1)S(1)}, bf16[64,256]{1,0:T(8,128)(2,1)S(1)}, u32[]{:S(2)}, u32[]{:S(2)}) %collective-permute-start.5) | collective-permute-done | bytes 32800 | tf_op jit(solution)/shard_map/ppermute | solution.py:427
  18.8 0.1 collective-permute-done.4.refs_5_
  19.0 22.6 %denoise.1 = bf16[128,64,128]{2,1,0:T(8,128)(2,1)} custom-call(f32[4]{0:T(128)S(1)} %pad_maximum_fusion.scale_ref.refs_0_, bf16[128,64,128]{2,1,0:T(8,128)(2,1)S(1)} %bitcast.8, bf16[4352,256]{1,0:T(8,128)(2,1)S(1)} %get-tuple-element.11.refs_0_.refs_1_.refs_2_, bf16[448,256]{1,0:T(8,128)(2,1)S(1)} %get-tuple-element.14.refs_3_, ...), custom_call_target="tpu_custom_call" | custom-call | tf_op jit(solution)/shard_map/denoise/pallas_call | solution.py:438
  (12 shorter events, 0.0 us)
Async XLA Ops:
  0.0 13.2 %collective-permute-start.1 = (bf16[12,16,128]{2,1,0:T(8,128)(2,1)}, bf16[12,16,128]{2,1,0:T(8,128)(2,1)S(1)}, u32[]{:S(2)}, u32[]{:S(2)}) collective-permute-start(bf16[12,16,128]{2,1,0:T(8,128)(2,1)} %refs_4_.1), channel_id=1, source_target_pairs={{0,8},{4,12},{8,0},{12,4},{1,9},{5,13},{9,1},{13,5},{2,10},{6,14},... | collective-permute-start | bytes 147464 | tf_op jit(solution)/shard_map/ppermute | solution.py:349
  4.0 9.2 %collective-permute-start = (bf16[12,16,128]{2,1,0:T(8,128)(2,1)}, bf16[12,16,128]{2,1,0:T(8,128)(2,1)S(1)}, u32[]{:S(2)}, u32[]{:S(2)}) collective-permute-start(bf16[12,16,128]{2,1,0:T(8,128)(2,1)} %refs_4_.1), channel_id=1, source_target_pairs={{0,4},{4,8},{8,12},{12,0},{1,5},{5,9},{9,13},{13,1},{2,6},{6,10},{... | collective-permute-start | bytes 147464 | tf_op jit(solution)/shard_map/ppermute | solution.py:349
  5.6 7.6 %collective-permute-start.2 = (bf16[12,16,128]{2,1,0:T(8,128)(2,1)}, bf16[12,16,128]{2,1,0:T(8,128)(2,1)S(1)}, u32[]{:S(2)}, u32[]{:S(2)}) collective-permute-start(bf16[12,16,128]{2,1,0:T(8,128)(2,1)} %refs_4_.1), channel_id=1, source_target_pairs={{0,12},{4,0},{8,4},{12,8},{1,13},{5,1},{9,5},{13,9},{2,14},{6,2},{... | collective-permute-start | bytes 147464 | tf_op jit(solution)/shard_map/ppermute | solution.py:349
  8.8 1.6 %copy-start = (bf16[1,128,64,128]{3,2,1,0:T(8,128)(2,1)S(1)}, bf16[1,128,64,128]{3,2,1,0:T(8,128)(2,1)}, u32[]{:S(2)}) copy-start(bf16[1,128,64,128]{3,2,1,0:T(8,128)(2,1)} %param.11) | copy-start | bytes 6291460
  10.4 2.8 %copy-start.4 = (bf16[12,16,128]{2,1,0:T(8,128)(2,1)S(1)}, bf16[12,16,128]{2,1,0:T(8,128)(2,1)}, u32[]{:S(2)}) copy-start(bf16[12,16,128]{2,1,0:T(8,128)(2,1)} %refs_4_.1) | copy-start | bytes 147460
  13.3 5.7 %copy-start.1 = (bf16[9,128,256]{2,1,0:T(8,128)(2,1)S(1)}, bf16[9,128,256]{2,1,0:T(8,128)(2,1)}, u32[]{:S(2)}) copy-start(bf16[9,128,256]{2,1,0:T(8,128)(2,1)} %refs_11_.1) | copy-start | bytes 1769476
  13.3 5.7 %copy-start.2 = (bf16[9,128,128]{2,1,0:T(8,128)(2,1)S(1)}, bf16[9,128,128]{2,1,0:T(8,128)(2,1)}, u32[]{:S(2)}) copy-start(bf16[9,128,128]{2,1,0:T(8,128)(2,1)} %refs_9_.1) | copy-start | bytes 884740
  13.3 5.7 %copy-start.3 = (bf16[9,128,128]{2,1,0:T(8,128)(2,1)S(1)}, bf16[9,128,128]{2,1,0:T(8,128)(2,1)}, u32[]{:S(2)}) copy-start(bf16[9,128,128]{2,1,0:T(8,128)(2,1)} %refs_14_.1) | copy-start | bytes 884740
  13.3 5.6 %copy-start.5 = (bf16[9,128,12]{1,2,0:T(8,128)(2,1)S(1)}, bf16[9,128,12]{1,2,0:T(8,128)(2,1)}, u32[]{:S(2)}) copy-start(bf16[9,128,12]{1,2,0:T(8,128)(2,1)} %param.14) | copy-start | bytes 82948
  13.3 5.6 %copy-start.6 = (f32[128]{0:T(128)S(1)}, f32[128]{0:T(128)}, u32[]{:S(2)}) copy-start(f32[128]{0:T(128)} %param.15) | copy-start | bytes 1540
  13.3 5.6 %copy-start.7 = (f32[128]{0:T(128)S(1)}, f32[128]{0:T(128)}, u32[]{:S(2)}) copy-start(f32[128]{0:T(128)} %param.17) | copy-start | bytes 1540
  13.3 5.6 %copy-start.8 = (f32[128]{0:T(128)S(1)}, f32[128]{0:T(128)}, u32[]{:S(2)}) copy-start(f32[128]{0:T(128)} %param.19) | copy-start | bytes 1540
  13.4 5.6 %copy-start.9 = (f32[128]{0:T(128)S(1)}, f32[128]{0:T(128)}, u32[]{:S(2)}) copy-start(f32[128]{0:T(128)} %param.20) | copy-start | bytes 1540
  13.5 5.5 %collective-permute-start.3 = (bf16[448,256]{1,0:T(8,128)(2,1)S(1)}, bf16[448,256]{1,0:T(8,128)(2,1)S(1)}, u32[]{:S(2)}, u32[]{:S(2)}) collective-permute-start(bf16[448,256]{1,0:T(8,128)(2,1)S(1)} %get-tuple-element.14.refs_3_), channel_id=1, source_target_pairs={{1,0},{0,1},{3,2},{2,3},{5,4},{4,5},{7,6},{6,7},{9,8},{8,9},{11,10... | collective-permute-start | bytes 688136 | tf_op jit(solution)/shard_map/ppermute | solution.py:431
  13.5 5.4 %collective-permute-start.4 = (bf16[176,256]{1,0:T(8,128)(2,1)S(1)}, bf16[176,256]{1,0:T(8,128)(2,1)S(1)}, u32[]{:S(2)}, u32[]{:S(2)}) collective-permute-start(bf16[176,256]{1,0:T(8,128)(2,1)S(1)} %get-tuple-element.15), channel_id=1, source_target_pairs={{2,0},{0,2},{3,1},{1,3},{6,4},{4,6},{7,5},{5,7},{10,8},{8,10},{11,... | collective-permute-start | bytes 270344 | tf_op jit(solution)/shard_map/ppermute | solution.py:422
  15.1 3.7 %collective-permute-start.5 = (bf16[64,256]{1,0:T(8,128)(2,1)S(1)}, bf16[64,256]{1,0:T(8,128)(2,1)S(1)}, u32[]{:S(2)}, u32[]{:S(2)}) collective-permute-start(bf16[64,256]{1,0:T(8,128)(2,1)S(1)} %get-tuple-element.16), channel_id=1, source_target_pairs={{3,0},{2,1},{1,2},{0,3},{7,4},{6,5},{5,6},{4,7},{11,8},{10,9},{9,1... | collective-permute-start | bytes 98312 | tf_op jit(solution)/shard_map/ppermute | solution.py:427
where the time goes:
time: 41.9 us; the launch traced here: 41.7 us
  Pallas kernels  25.4 us (61%)
  starting transfers between devices  9.79 us (23%)
  waiting for transfers between devices  3.53 us (8%)
  local copies, waits for them, and re-layouts  1.65 us (4%)
  between operations  1.23 us (3%)
    pallas_call x1, Pallas kernels, local(): pl.pallas_call(functools.partial(main_kernel, geo=geo, n_strip_in=n_strip...  22.6 us
    ppermute x3, starting transfers between devices, local(): lax.ppermute(condition, 'member', [(i, (i + k) % n_member) for i in range...  7.86 us
    ppermute x1, waiting for transfers between devices, local(): corners.append(lax.ppermute(rest[at], ('strip', 'sub'), pairs_of))  3.42 us
    pallas_call x1, Pallas kernels, local(): pl.pallas_call(functools.partial(prep_kernel, pitch=pitch), grid=(steps,)...  2.79 us
    unnamed x20, local copies, waits for them, and re-layouts  1.65 us
    ppermute x1, starting transfers between devices, local(): got = [lax.ppermute(rest[at], 'strip', move)]  1.56 us
  transfers between devices with their start and end apart: 6, of which 2 were waited for; matrix products, arithmetic and copies ran while one was open for 0% of the time, Pallas kernels for 7%

commit v1 on v0

--- a/solution.py
+++ b/solution.py
@@ -1,4 +1,5 @@
 import functools
+import math
 
 import jax
 import jax.numpy as jnp
@@ -16,26 +17,42 @@
 F32 = jnp.float32
 NT = (((1,), (1,)), ((), ()))
 NN = (((1,), (0,)), ((), ()))
-VMEM_LIMIT = 48 * 2**20
 
 BASE = 8
 HALO = 4
 EDGE = 8
+GROUP = 8
 SLOT = 16
 
 
-def prep_kernel(scale_ref, field_ref, pairs_ref, left_ref, right_ref, buf, *, pitch):
-    chans, rows, cols = field_ref.shape
-    buf[...] = field_ref[...].astype(F32).reshape(chans * rows, cols)
-    c_in = scale_ref[0]
-    for q in range(rows // 2):
-        for h in range(2):
-            row = buf[pl.ds(2 * q + h, chans, stride=rows), :]
-            cells = (c_in * row.T).astype(BF16)
-            lanes = slice(h * chans, (h + 1) * chans)
-            pairs_ref[q * pitch + 2:q * pitch + 2 + cols, lanes] = cells
-            left_ref[2 * q:2 * q + 2, lanes] = cells[:2]
-            right_ref[2 * q:2 * q + 2, lanes] = cells[cols - 2:]
+def plan(level_ref):
+    level = jnp.full((1, 128), level_ref[0].astype(F32))
+    sigma = SIG_LOW * jnp.exp(level * (math.log(SIG_HIGH / SIG_LOW) / (LEVELS - 1)))
+    spread = sigma * sigma + SIGMA_DATA * SIGMA_DATA
+    root = jnp.sqrt(spread)
+    return 1.0 / root, SIGMA_DATA * SIGMA_DATA / spread, sigma * SIGMA_DATA / root, jnp.log(sigma) / 4.0
+
+
+def prep_kernel(level_ref, field_hbm, pairs_ref, left_ref, right_ref, raw, buf, sems, *, pitch):
+    steps, chans, tall, cols = raw.shape
+    gets = []
+    for s in range(steps):
+        get = pltpu.make_async_copy(field_hbm.at[:, pl.ds(s * tall, tall), :], raw.at[s], sems.at[s])
+        get.start()
+        gets.append(get)
+    c_in = plan(level_ref)[0]
+    for s in range(steps):
+        gets[s].wait()
+        buf[...] = raw[s].astype(F32).reshape(chans * tall, cols)
+        for q in range(tall // 2):
+            at = s * (tall // 2) + q
+            for h in range(2):
+                row = buf[pl.ds(2 * q + h, chans, stride=tall), :]
+                cells = (c_in * row.T).astype(BF16)
+                lanes = slice(h * chans, (h + 1) * chans)
+                pairs_ref[at * pitch + 2:at * pitch + 2 + cols, lanes] = cells
+                left_ref[2 * at:2 * at + 2, lanes] = cells[:2]
+                right_ref[2 * at:2 * at + 2, lanes] = cells[cols - 2:]
 
 
 def pack_kernel(*refs, geo, block_count):
@@ -56,7 +73,7 @@
         if block_count == 1:
             at = 0
         else:
-            at = pl.multiple_of(lax.rem(member - k + n_member, n_member) * tall, tall)
+            at = pl.multiple_of(jnp.bitwise_xor(member, k) * tall, tall)
         for c in range(cin):
             lanes = slice((c // half) * cols, (c // half + 1) * cols)
             start = 2 * (rows // 2) + (c % half) * rows + at
@@ -121,21 +138,75 @@
             corner_out[16:, :] = strip_out[cols:, :]
 
 
+def conv(src, weight, at, span, pitch):
+    lo, hi = slice(0, 128), slice(128, 256)
+    parts = []
+    for b in range(3):
+        parts.append(src[at + b:at + b + span, hi])
+        parts.append(src[at + pitch + b:at + pitch + b + span, lo])
+    y = lax.dot_general(
+        jnp.concatenate(parts, axis=1), weight[:, :768], NT, preferred_element_type=F32)
+    more = span + 8
+    upper = jnp.concatenate([src[at + b:at + b + more, lo] for b in range(2)], axis=1)
+    upper = lax.dot_general(upper, weight[:, 768:1024], NT, preferred_element_type=F32)
+    lower = jnp.concatenate(
+        [src[at + pitch + b:at + pitch + b + more, hi] for b in range(2)], axis=1)
+    lower = lax.dot_general(lower, weight[:, 1024:], NT, preferred_element_type=F32)
+    return y + jnp.concatenate(
+        [upper[:span, lo] + upper[1:span + 1, hi], lower[:span, lo] + lower[1:span + 1, hi]], axis=1)
+
+
+def tiles_of(dst, src, lanes):
+    zero = jnp.zeros((128, 128), BF16)
+    tap = [[src[3 * a + b, :, lanes] for b in range(3)] for a in range(3)]
+
+    def put(at, blocks):
+        for n in range(2):
+            for k in range(2):
+                dst[n * 128:(n + 1) * 128, at + k * 128:at + (k + 1) * 128] = blocks[n][k]
+
+    for b in range(3):
+        put(b * 256, [[tap[1][b], tap[2][b]], [tap[0][b], tap[1][b]]])
+    put(768, [[tap[0][0], tap[0][1]], [zero, tap[0][2]]])
+    put(1024, [[tap[2][0], tap[2][1]], [zero, tap[2][2]]])
+
+
+def chunks(total, size):
+    return [(at, min(size, total - at)) for at in range(0, total, size)]
+
+
+def noisy_kernel(pairs, w1, w2, wa, wb, part, m1, m2, mn, mf, mb, *, geo):
+    pitch, npair, cin = geo["pitch"], geo["rows"] // 2, geo["cin"]
+    chans = 128
+    tiles_of(mn, wa, slice(0, chans))
+    for first, count in chunks(npair - 1, GROUP):
+        part[first * pitch:(first + count) * pitch, :] = conv(
+            pairs, mn, first * pitch, count * pitch, pitch)
+    tiles_of(m2, w2, slice(0, chans))
+    tiles_of(mf, wa, slice(chans, 2 * chans))
+    tiles_of(mb, wb, slice(0, chans))
+    m1[...] = jnp.zeros_like(m1)
+    for b in range(3):
+        for n in range(6):
+            for a in range(3):
+                at = b * 8 * SLOT + (n + a) * SLOT
+                m1[at:at + cin, n * chans:(n + 1) * chans] = w1[3 * a + b]
+
+
 def main_kernel(*refs, geo, n_strip_in, n_sub_in):
     it = iter(refs)
-    scal = next(it)
-    field_hbm = next(it)
-    pairs_hbm = next(it)
-    own = next(it)
+    level_ref = next(it)
+    field = next(it)
+    part, pairs_top, pairs_bottom, left, right, own = [next(it) for _ in range(6)]
     sub_in = [next(it) for _ in range(n_sub_in)]
     strip_in = []
     diag_in = []
     for _ in range(n_strip_in):
         strip_in.append(next(it))
         diag_in.append([next(it) for _ in range(n_sub_in)])
-    w1, b1, w2, b2, wa, ba, gain, wb = [next(it) for _ in range(8)]
+    m1, m2, mn, mf, mb, b1, b2, ba, gain = [next(it) for _ in range(9)]
     out_hbm = next(it)
-    (xe, xn, xf, xh, m1, m2, mn, mf, mb, cr, ch, lw, field, out, obuf, sems) = list(it)
+    (xe, xf, xh, xt, xb, xc, yc, cr, ch, lw, out, obuf, sems) = list(it)
 
     n_strip, n_sub = geo["n_strip"], geo["n_sub"]
     pitch, cols, rows, cin = geo["pitch"], geo["cols"], geo["rows"], geo["cin"]
@@ -148,40 +219,10 @@
     above, below = strip > 0, strip < n_strip - 1
     before, after = sub > 0, sub < n_sub - 1
 
-    get_pairs = pltpu.make_async_copy(
-        pairs_hbm, xn.at[pl.ds(BASE + pitch, npair * pitch), :], sems.at[0])
-    get_pairs.start()
-    get_field = pltpu.make_async_copy(field_hbm, field, sems.at[1])
-    get_field.start()
+    _, c_skip, c_out, c_noise = plan(level_ref)
 
     def keep(flag, cells):
         return jnp.where(flag, cells.astype(F32), 0.0)
-
-    def blocks_of(dst, src, lanes):
-        zero = jnp.zeros((chans, chans), BF16)
-        for b in range(3):
-            a0 = b * 2 * chans
-            b0 = (3 + b) * 2 * chans
-            taps = [src[3 * a + b, :, lanes] for a in range(3)]
-            dst[:chans, a0:a0 + chans] = taps[0]
-            dst[:chans, a0 + chans:a0 + 2 * chans] = taps[1]
-            dst[chans:, a0:a0 + chans] = zero
-            dst[chans:, a0 + chans:a0 + 2 * chans] = taps[0]
-            dst[:chans, b0:b0 + chans] = taps[2]
-            dst[:chans, b0 + chans:b0 + 2 * chans] = zero
-            dst[chans:, b0:b0 + chans] = taps[1]
-            dst[chans:, b0 + chans:b0 + 2 * chans] = taps[2]
-
-    blocks_of(m2, w2, slice(0, chans))
-    blocks_of(mn, wa, slice(0, chans))
-    blocks_of(mf, wa, slice(chans, 2 * chans))
-    blocks_of(mb, wb, slice(0, chans))
-    m1[...] = jnp.zeros_like(m1)
-    for b in range(3):
-        for n in range(6):
-            for a in range(3):
-                at = b * 8 * SLOT + (n + a) * SLOT
-                m1[at:at + cin, n * chans:(n + 1) * chans] = w1[3 * a + b]
 
     cr[...] = jnp.zeros_like(cr)
     ch[...] = jnp.zeros_like(ch)
@@ -262,54 +303,63 @@
                     cells = inside(z[i * pitch:(i + 1) * pitch], 3, 3 + cols, j, 1, 3)[0]
                     xe[BASE + j * pitch:BASE + (j + 1) * pitch, :] = cells.astype(BF16)
 
-    def conv(src, weight, first, count):
-        span = count * pitch
-        at = BASE + first * pitch
-        lhs = jnp.concatenate(
-            [src[at + p * pitch + b:at + p * pitch + b + span, :] for p in range(2) for b in range(3)],
-            axis=1)
-        return lax.dot_general(lhs, weight[...], NT, preferred_element_type=F32)
-
-    def chunks(total, size):
-        return [(at, min(size, total - at)) for at in range(0, total, size)]
-
     bias2 = twice(b2[...])
-    for first, count in chunks(npair + 2, 9):
-        parts = inside(conv(xe, m2, first, count) + bias2, 2, 2 + cols, first, count, 2)
+    for first, count in chunks(npair + 2, GROUP):
+        y = conv(xe, m2, BASE + first * pitch, count * pitch, pitch) + bias2
+        parts = inside(y, 2, 2 + cols, first, count, 2)
         for i, cells in enumerate(parts):
             at = BASE + (first + i) * pitch
             xf[at:at + pitch, :] = cells.astype(BF16)
 
-    get_pairs.wait()
-    for k in range(n_sub_in):
-        for q in range(npair):
-            at = BASE + (q + 1) * pitch
-            cells = sub_in[k][2 * q:2 * q + 2, :]
-            if k == 0:
-                xn[at:at + 2, :] = keep(before, cells).astype(BF16)
-            if k == n_sub_in - 1:
-                xn[at + 2 + cols:at + 4 + cols, :] = keep(after, cells).astype(BF16)
-    for source, corners, flag, j in (
-        (strip_top, diag_top, above, 0), (strip_bottom, diag_bottom, below, npair + 1)):
-        at = BASE + j * pitch
-        xn[at + 2:at + 2 + cols, :] = keep(flag, source[:cols, :]).astype(BF16)
-        xn[at:at + 2, :] = keep(flag & before, corners[0][:2, :]).astype(BF16)
-        xn[at + 2 + cols:at + 4 + cols, :] = keep(flag & after, corners[-1][:2, :]).astype(BF16)
-
-    offset = twice(ba[...] + scal[3] * gain[...])
-    for first, count in chunks(npair + 1, 9):
-        y = conv(xn, mn, first, count) + conv(xf, mf, first, count) + offset
+    def halo_cells(q):
+        return (keep(before, sub_in[0][2 * q:2 * q + 2, :]).astype(BF16),
+                keep(after, sub_in[-1][2 * q:2 * q + 2, :]).astype(BF16))
+
+    strip_rows = (
+        (xt, strip_top, diag_top, above, 0, pairs_top[:pitch, :], 0, 1),
+        (xb, strip_bottom, diag_bottom, below, 1, pairs_bottom[pitch:, :], npair - 1, 0))
+    for dst, source, corners, flag, at, inner, q, inner_at in strip_rows:
+        at = BASE + at * pitch
+        dst[at + 2:at + 2 + cols, :] = keep(flag, source[:cols, :]).astype(BF16)
+        dst[at:at + 2, :] = keep(flag & before, corners[0][:2, :]).astype(BF16)
+        dst[at + 2 + cols:at + 4 + cols, :] = keep(flag & after, corners[-1][:2, :]).astype(BF16)
+        at = BASE + inner_at * pitch
+        dst[at:at + pitch, :] = inner
+        dst[at:at + 2, :], dst[at + 2 + cols:at + 4 + cols, :] = halo_cells(q)
+    for q in range(npair):
+        at = 8 * q
+        xc[at:at + 2, :], xc[at + 6:at + 8, :] = halo_cells(q)
+        xc[at + 2:at + 4, :] = left[2 * q:2 * q + 2, :]
+        xc[at + 4:at + 6, :] = right[2 * q:2 * q + 2, :]
+    yc[...] = conv(xc, mn, 0, 8 * (npair - 1), 8)
+
+    offset = twice(ba[...] + c_noise * gain[...])
+    first_cols = lax.broadcasted_iota(jnp.int32, (8, 2 * chans), 0) < 2
+    for first, count in chunks(npair + 1, GROUP):
+        y = conv(xf, mf, BASE + first * pitch, count * pitch, pitch) + offset
+        noisy = []
+        for j in range(first, first + count):
+            if j == 0:
+                noisy.append(conv(xt, mn, BASE, pitch, pitch))
+            elif j == npair:
+                noisy.append(conv(xb, mn, BASE, pitch, pitch))
+            else:
+                at = (j - 1) * pitch
+                edge = yc[8 * (j - 1):8 * j, :]
+                noisy.append(jnp.where(first_cols, edge, part[at:at + 8, :]))
+                noisy.append(part[at + 8:at + cols, :])
+                noisy.append(jnp.where(
+                    first_cols, pltpu.roll(edge, 4, 0), part[at + cols:at + cols + 8, :]))
+        y = y + jnp.concatenate(noisy, axis=0)
         parts = inside(silu(y), 1, 1 + cols, first, count, 1)
         for i, cells in enumerate(parts):
             at = BASE + (first + i) * pitch
             xh[at:at + pitch, :] = cells.astype(BF16)
 
-    get_field.wait()
-    c_skip, c_out = scal[1], scal[2]
-    group = 8
+    c_skip, c_out = c_skip.reshape(1, 1, cols), c_out.reshape(1, 1, cols)
     puts = []
-    for first, count in chunks(npair, group):
-        y = conv(xh, mb, first, count)
+    for first, count in chunks(npair, 8):
+        y = conv(xh, mb, BASE + first * pitch, count * pitch, pitch)
         tall = 2 * count
         for i in range(count):
             for h in range(2):
@@ -321,7 +371,7 @@
         out[:, r0:r0 + tall, :] = (c_skip * skip + c_out * update).astype(BF16)
         put = pltpu.make_async_copy(
             out.at[:, pl.ds(r0, tall), :], out_hbm.at[:, pl.ds(r0, tall), :],
-            sems.at[2 + first // group])
+            sems.at[first // 8])
         put.start()
         puts.append(put)
     for put in puts:
@@ -342,47 +392,37 @@
     geo = dict(n_strip=n_strip, n_sub=n_sub, n_member=n_member, pitch=pitch, cols=cols, rows=rows,
                cin=cin, windows=-(-(rows + 6) // 6))
 
-    if n_member <= 4:
+    if n_member in (1, 2, 4):
         blocks = [condition]
         for k in range(1, n_member):
             blocks.append(
-                lax.ppermute(condition, "member", [(i, (i + k) % n_member) for i in range(n_member)]))
+                lax.ppermute(condition, "member", [(i, i ^ k) for i in range(n_member)]))
     else:
         blocks = [lax.all_gather(condition, "member", axis=1, tiled=True)]
 
-    level_value = levels[0].astype(F32)
-    noise_sigma = SIG_LOW * (SIG_HIGH / SIG_LOW) ** (level_value / (LEVELS - 1))
-    spread = noise_sigma * noise_sigma + SIGMA_DATA * SIGMA_DATA
-    c_in = 1.0 / jnp.sqrt(spread)
-    c_skip = SIGMA_DATA * SIGMA_DATA / spread
-    c_out = noise_sigma * SIGMA_DATA / jnp.sqrt(spread)
-    c_noise = jnp.log(noise_sigma) / 4.0
-    scal = jnp.stack([c_in, c_skip, c_out, c_noise])
-
     tall = 16
     steps = rows // tall
+    any_spec = pl.BlockSpec(memory_space=pl.ANY)
+    smem = pl.BlockSpec(memory_space=pltpu.SMEM)
+    vmem = pl.BlockSpec(memory_space=pltpu.VMEM)
     pairs, left, right = pl.pallas_call(
         functools.partial(prep_kernel, pitch=pitch),
-        grid=(steps,),
         out_shape=[
-            jax.ShapeDtypeStruct((npair * pitch, 2 * chans), BF16),
+            jax.ShapeDtypeStruct((npair * pitch + 16, 2 * chans), BF16),
             jax.ShapeDtypeStruct((2 * npair, 2 * chans), BF16),
             jax.ShapeDtypeStruct((2 * npair, 2 * chans), BF16),
         ],
-        in_specs=[
-            pl.BlockSpec(memory_space=pltpu.SMEM),
-            pl.BlockSpec((chans, tall, cols), lambda i: (0, i, 0)),
+        in_specs=[smem, pl.BlockSpec(memory_space=pltpu.HBM)],
+        out_specs=[vmem] * 3,
+        scratch_shapes=[
+            pltpu.VMEM((steps, chans, tall, cols), BF16),
+            pltpu.VMEM((chans * tall, cols), F32),
+            pltpu.SemaphoreType.DMA((steps,)),
         ],
-        out_specs=[
-            pl.BlockSpec((npair * pitch // steps, 2 * chans), lambda i: (i, 0)),
-            pl.BlockSpec((2 * npair // steps, 2 * chans), lambda i: (i, 0)),
-            pl.BlockSpec((2 * npair // steps, 2 * chans), lambda i: (i, 0)),
-        ],
-        scratch_shapes=[pltpu.VMEM((chans * tall, cols), F32)],
-        compiler_params=pltpu.CompilerParams(vmem_limit_bytes=VMEM_LIMIT),
+        compiler_params=pltpu.CompilerParams(vmem_limit_bytes=12 * 2**20),
         cost_estimate=pl.CostEstimate(flops=0, bytes_accessed=16 * 2**20, transcendentals=0),
         name="prep",
-    )(scal, field)
+    )(levels, pltpu.with_memory_space_constraint(field, pltpu.HBM))
 
     whole_shape = jax.ShapeDtypeStruct((2 * npair + cin // 2 * rows, 2 * cols), BF16)
     strip_shape = jax.ShapeDtypeStruct((cols + cin // 2 * EDGE, 2 * cols), BF16)
@@ -393,7 +433,6 @@
     for _ in range(n_strip_out):
         out_shape += [strip_shape] + [diag_shape] * n_sub_out
     last = npair // 2 - 1
-    vmem = pl.BlockSpec(memory_space=pltpu.VMEM)
     packed = pl.pallas_call(
         functools.partial(pack_kernel, geo=geo, block_count=len(blocks)),
         grid=(1,),
@@ -403,7 +442,7 @@
             pl.BlockSpec((2 * pitch, 2 * chans), lambda i: (last, 0)),
         ] + [vmem] * (2 + len(blocks)),
         out_specs=[vmem] * len(out_shape),
-        compiler_params=pltpu.CompilerParams(vmem_limit_bytes=VMEM_LIMIT),
+        compiler_params=pltpu.CompilerParams(vmem_limit_bytes=8 * 2**20),
         name="pack",
     )(pairs, pairs, left, right, *blocks)
 
@@ -430,38 +469,53 @@
     strip_in = [x for one in strip_in[::-1] for x in one]
     sub_in = [lax.ppermute(x, "sub", move) for x, move in zip(packed[:n_sub_out], sub_moves)][::-1]
 
+    mat = jax.ShapeDtypeStruct((2 * chans, 10 * chans), BF16)
+    part, *mats = pl.pallas_call(
+        functools.partial(noisy_kernel, geo=geo),
+        out_shape=[
+            jax.ShapeDtypeStruct(((npair - 1) * pitch, 2 * chans), F32),
+            jax.ShapeDtypeStruct((3 * 8 * SLOT, 6 * chans), BF16),
+            mat, mat, mat, mat,
+        ],
+        in_specs=[vmem] * 5,
+        out_specs=[vmem] * 6,
+        compiler_params=pltpu.CompilerParams(vmem_limit_bytes=16 * 2**20),
+        cost_estimate=pl.CostEstimate(
+            flops=2 * 9 * chans * chans * rows * cols, bytes_accessed=8 * 2**20, transcendentals=0),
+        name="noisy",
+    )(pairs, jnp.swapaxes(enc_w1, 1, 2), enc_w2, den_wa, den_wb)
+
     flat = BASE + (npair + 3) * pitch + 16
     windows = geo["windows"]
-    any_spec = pl.BlockSpec(memory_space=pl.ANY)
-    smem = pl.BlockSpec(memory_space=pltpu.SMEM)
-    steps_out = -(-npair // 8)
+    field_scratch = pltpu.VMEM((flat, 2 * chans), BF16)
+    edge_scratch = pltpu.VMEM((BASE + 2 * pitch + 16, 2 * chans), BF16)
+    cond_scratch = pltpu.VMEM(((6 * windows + 2) * SLOT, cols), F32)
+    whole_scratch = pltpu.VMEM((chans, rows, cols), BF16)
+    inputs = [part, pairs, pairs, left, right, packed[0], *sub_in, *strip_in, *mats,
+              enc_b1[None], enc_b2[None], den_ba[None], noise_gain[None]]
+    in_specs = [vmem] * len(inputs)
+    in_specs[1] = pl.BlockSpec((2 * pitch, 2 * chans), lambda i: (0, 0))
+    in_specs[2] = pl.BlockSpec((2 * pitch, 2 * chans), lambda i: (last, 0))
     result = pl.pallas_call(
         functools.partial(main_kernel, geo=geo, n_strip_in=n_strip_out, n_sub_in=n_sub_out),
+        grid=(1,),
         out_shape=jax.ShapeDtypeStruct((chans, rows, cols), BF16),
-        in_specs=[smem, any_spec, any_spec] + [vmem] * (1 + n_sub_out + len(strip_in) + 8),
+        in_specs=[smem, vmem] + in_specs,
         out_specs=any_spec,
         scratch_shapes=[
-            pltpu.VMEM((flat, 2 * chans), BF16),
-            pltpu.VMEM((flat, 2 * chans), BF16),
-            pltpu.VMEM((flat, 2 * chans), BF16),
-            pltpu.VMEM((flat, 2 * chans), BF16),
-            pltpu.VMEM((3 * 8 * SLOT, 6 * chans), BF16),
-            pltpu.VMEM((2 * chans, 12 * chans), BF16),
-            pltpu.VMEM((2 * chans, 12 * chans), BF16),
-            pltpu.VMEM((2 * chans, 12 * chans), BF16),
-            pltpu.VMEM((2 * chans, 12 * chans), BF16),
-            pltpu.VMEM(((6 * windows + 2) * SLOT, cols), F32),
-            pltpu.VMEM(((6 * windows + 2) * SLOT, cols), F32),
+            field_scratch, field_scratch, field_scratch,
+            edge_scratch, edge_scratch,
+            pltpu.VMEM((8 * npair + 16, 2 * chans), BF16),
+            pltpu.VMEM((8 * (npair - 1), 2 * chans), F32),
+            cond_scratch, cond_scratch,
             pltpu.VMEM((BASE + windows * pitch + 16, 8 * SLOT), BF16),
-            pltpu.VMEM((chans, rows, cols), BF16),
-            pltpu.VMEM((chans, rows, cols), BF16),
+            whole_scratch,
             pltpu.VMEM((chans * 16, cols), F32),
-            pltpu.SemaphoreType.DMA((2 + steps_out,)),
+            pltpu.SemaphoreType.DMA((-(-npair // 8),)),
         ],
-        compiler_params=pltpu.CompilerParams(vmem_limit_bytes=VMEM_LIMIT),
+        compiler_params=pltpu.CompilerParams(vmem_limit_bytes=28 * 2**20),
         name="denoise",
-    )(scal, field, pairs, packed[0], *sub_in, *strip_in, jnp.swapaxes(enc_w1, 1, 2),
-      enc_b1[None], enc_w2, enc_b2[None], den_wa, den_ba[None], noise_gain[None], den_wb)
+    )(levels, field, *inputs)
     return result[None]
 
 

time: 41.9 us -> 35.1 us (0.84)
  Pallas kernels: 25.4 us -> 22.3 us
  starting transfers between devices: 9.79 us -> 7.83 us
  local copies, waits for them, and re-layouts: 1.65 us -> 0.84 us
  waiting for transfers between devices: 3.53 us -> 2.95 us
    pallas_call x1, Pallas kernels: 22.6 us -> 15.8 us  [local(): pl.pallas_call(functools.partial(main_kernel, geo=geo, n_strip_in=n_strip...]
    pallas_call x1 -> x2, Pallas kernels: 2.79 us -> 6.44 us  [the longest x1 3.41 us: local(): pl.pallas_call(functools.partial(noisy_kernel, geo=geo), out_shape=[jax.S...]
    ppermute x1, waiting for transfers between devices: 3.42 us -> 0.01 us  [local(): corners.append(lax.ppermute(rest[at], ('strip', 'sub'), pairs_of))]
    ppermute x3, waiting for transfers between devices: 0.01 us -> 2.39 us  [local(): lax.ppermute(condition, 'member', [(i, i ^ k) for i in range(n_member)])]
    ppermute x3, starting transfers between devices: 7.86 us -> 5.62 us  [local(): lax.ppermute(condition, 'member', [(i, i ^ k) for i in range(n_member)])]
    ppermute x1, starting transfers between devices: 0.31 us -> 1.61 us  [local(): corners.append(lax.ppermute(rest[at], ('strip', 'sub'), pairs_of))]
    ppermute x1, starting transfers between devices: 1.56 us -> 0.53 us  [local(): got = [lax.ppermute(rest[at], 'strip', move)]]
    unnamed x20, local copies, waits for them, and re-layouts: 1.65 us -> 0.84 us
  transfers between devices with their start and end apart: 6 -> 6, of which waited for: 2 -> 2; matrix products, arithmetic and copies ran while one was open for 0% -> 0% of each run, Pallas kernels for 7% -> 18%
where the time goes in v1:
time: 35.1 us; the launch traced here: 34.9 us
  Pallas kernels  22.3 us (64%)
  starting transfers between devices  7.83 us (22%)
  waiting for transfers between devices  2.95 us (8%)
  between operations  0.95 us (3%)
  local copies, waits for them, and re-layouts  0.84 us (2%)
    pallas_call x1, Pallas kernels, local(): pl.pallas_call(functools.partial(main_kernel, geo=geo, n_strip_in=n_strip...  15.8 us
    ppermute x3, starting transfers between devices, local(): lax.ppermute(condition, 'member', [(i, i ^ k) for i in range(n_member)])  5.62 us
    pallas_call x1, Pallas kernels, local(): pl.pallas_call(functools.partial(noisy_kernel, geo=geo), out_shape=[jax.S...  3.41 us
    pallas_call x1, Pallas kernels, local(): pl.pallas_call(functools.partial(prep_kernel, pitch=pitch), out_shape=[ja...  3.03 us
    ppermute x3, waiting for transfers between devices, local(): lax.ppermute(condition, 'member', [(i, i ^ k) for i in range(n_member)])  2.39 us
    ppermute x1, starting transfers between devices, local(): corners.append(lax.ppermute(rest[at], ('strip', 'sub'), pairs_of))  1.61 us
    unnamed x20, local copies, waits for them, and re-layouts  0.84 us
  transfers between devices with their start and end apart: 6, of which 2 were waited for; matrix products, arithmetic and copies ran while one was open for 0% of the time, Pallas kernels for 18%

profile of v1, /device:TPU:0, one launch (start us, length us, event | category | flops | bytes accessed | tf_op | source)
XLA Modules:
  0.0 34.9 jit_solution(5859964994371407573)
XLA Ops:
  0.0 4.0 %collective-permute-start.1 = (bf16[12,16,128]{2,1,0:T(8,128)(2,1)}, bf16[12,16,128]{2,1,0:T(8,128)(2,1)S(1)}, u32[]{:S(2)}, u32[]{:S(2)}) collective-permute-start(bf16[12,16,128]{2,1,0:T(8,128)(2,1)} %refs_4_.1), channel_id=1, source_target_pairs={{0,8},{4,12},{8,0},{12,4},{1,9},{5,13},{9,1},{13,5},{2,10},{6,14},... | collective-permute-start | bytes 147464 | tf_op jit(solution)/shard_map/ppermute | solution.py:399
  4.0 1.6 %collective-permute-start = (bf16[12,16,128]{2,1,0:T(8,128)(2,1)}, bf16[12,16,128]{2,1,0:T(8,128)(2,1)S(1)}, u32[]{:S(2)}, u32[]{:S(2)}) collective-permute-start(bf16[12,16,128]{2,1,0:T(8,128)(2,1)} %refs_4_.1), channel_id=1, source_target_pairs={{0,4},{4,0},{8,12},{12,8},{1,5},{5,1},{9,13},{13,9},{2,6},{6,2},{1... | collective-permute-start | bytes 147464 | tf_op jit(solution)/shard_map/ppermute | solution.py:399
  5.6 0.0 collective-permute-start.2
  6.3 3.0 %prep.1 = (bf16[4368,256]{1,0:T(8,128)(2,1)S(1)}, bf16[64,256]{1,0:T(8,128)(2,1)S(1)}, bf16[64,256]{1,0:T(8,128)(2,1)S(1)}) custom-call(s32[1]{0:T(128)S(6)} %copy.12.level_ref.refs_0_, bf16[128,64,128]{2,1,0:T(8,128)(2,1)} %bitcast.7), custom_call_target="tpu_custom_call" | custom-call | bytes 16777216 | tf_op jit(solution)/shard_map/prep/pallas_call | solution.py:408
  9.3 0.0 collective-permute-done.1.refs_6_
  9.3 0.0 collective-permute-done.refs_5_
  9.3 2.4 %collective-permute-done.2.refs_7_ = bf16[12,16,128]{2,1,0:T(8,128)(2,1)S(1)} collective-permute-done((bf16[12,16,128]{2,1,0:T(8,128)(2,1)}, bf16[12,16,128]{2,1,0:T(8,128)(2,1)S(1)}, u32[]{:S(2)}, u32[]{:S(2)}) %collective-permute-start.2) | collective-permute-done | bytes 49184 | tf_op jit(solution)/shard_map/ppermute | solution.py:399
  11.7 0.8 %copy-done.1 = bf16[12,16,128]{2,1,0:T(8,128)(2,1)S(1)} copy-done((bf16[12,16,128]{2,1,0:T(8,128)(2,1)S(1)}, bf16[12,16,128]{2,1,0:T(8,128)(2,1)}, u32[]{:S(2)}) %copy-start.1) | copy-done | bytes 49176
  12.5 0.1 pack.1
  12.6 0.1 collective-permute-start.3
  12.7 1.6 %collective-permute-start.5 = (bf16[64,256]{1,0:T(8,128)(2,1)S(1)}, bf16[64,256]{1,0:T(8,128)(2,1)S(1)}, u32[]{:S(2)}, u32[]{:S(2)}) collective-permute-start(bf16[64,256]{1,0:T(8,128)(2,1)S(1)} %get-tuple-element.23), channel_id=1, source_target_pairs={{3,0},{2,1},{1,2},{0,3},{7,4},{6,5},{5,6},{4,7},{11,8},{10,9},{9,1... | collective-permute-start | bytes 98312 | tf_op jit(solution)/shard_map/ppermute | solution.py:466
  14.3 0.5 %collective-permute-start.4 = (bf16[176,256]{1,0:T(8,128)(2,1)S(1)}, bf16[176,256]{1,0:T(8,128)(2,1)S(1)}, u32[]{:S(2)}, u32[]{:S(2)}) collective-permute-start(bf16[176,256]{1,0:T(8,128)(2,1)S(1)} %get-tuple-element.22), channel_id=1, source_target_pairs={{2,0},{0,2},{3,1},{1,3},{6,4},{4,6},{7,5},{5,7},{10,8},{8,10},{11,... | collective-permute-start | bytes 270344 | tf_op jit(solution)/shard_map/ppermute | solution.py:461
  14.8 0.0 copy-done.7
  14.9 0.0 copy-done.9
  14.9 0.0 copy-start
  14.9 0.0 copy-start.2
  14.9 0.0 copy-start.3
  14.9 0.0 copy-start.4
  14.9 0.0 copy-start.5
  14.9 3.4 %noisy.1 = (f32[4216,256]{1,0:T(8,128)S(1)}, bf16[384,768]{1,0:T(8,128)(2,1)S(1)}, bf16[256,1280]{1,0:T(8,128)(2,1)S(1)}, bf16[256,1280]{1,0:T(8,128)(2,1)S(1)},...) custom-call(bf16[4368,256]{1,0:T(8,128)(2,1)S(1)} %get-tuple-element.17.pairs.refs_0_.refs_1_.refs_3_.refs_4_, ...), custom_call_target="tpu_custom_call" | custom-call | flops 2415919104 | bytes 8388608 | tf_op jit(solution)/shard_map/noisy/pallas_call | solution.py:473
  18.3 0.0 collective-permute-done.5.refs_10_
  18.3 0.5 %collective-permute-done.4.refs_9_ = bf16[176,256]{1,0:T(8,128)(2,1)S(1)} collective-permute-done((bf16[176,256]{1,0:T(8,128)(2,1)S(1)}, bf16[176,256]{1,0:T(8,128)(2,1)S(1)}, u32[]{:S(2)}, u32[]{:S(2)}) %collective-permute-start.4) | collective-permute-done | bytes 90144 | tf_op jit(solution)/shard_map/ppermute | solution.py:461
  18.9 0.0 collective-permute-done.3.refs_8_
  18.9 15.8 %denoise.1 = bf16[128,64,128]{2,1,0:T(8,128)(2,1)} custom-call(s32[1]{0:T(128)S(6)} %copy.12.level_ref.refs_0_, bf16[128,64,128]{2,1,0:T(8,128)(2,1)S(1)} %bitcast.8, f32[4216,256]{1,0:T(8,128)S(1)} %get-tuple-element.18.refs_2_, bf16[4368,256]{1,0:T(8,128)(2,1)S(1)} %get-tuple-element.17.pairs.refs_0_.refs_1_.refs_3_.refs_4_, ...), custom_call_target="tpu_custom_call" | custom-call | tf_op jit(solution)/shard_map/denoise/pallas_call | solution.py:499
  (12 shorter events, 0.0 us)
Async XLA Ops:
  0.0 9.3 %collective-permute-start.1 = (bf16[12,16,128]{2,1,0:T(8,128)(2,1)}, bf16[12,16,128]{2,1,0:T(8,128)(2,1)S(1)}, u32[]{:S(2)}, u32[]{:S(2)}) collective-permute-start(bf16[12,16,128]{2,1,0:T(8,128)(2,1)} %refs_4_.1), channel_id=1, source_target_pairs={{0,8},{4,12},{8,0},{12,4},{1,9},{5,13},{9,1},{13,5},{2,10},{6,14},... | collective-permute-start | bytes 147464 | tf_op jit(solution)/shard_map/ppermute | solution.py:399
  4.0 5.3 %collective-permute-start = (bf16[12,16,128]{2,1,0:T(8,128)(2,1)}, bf16[12,16,128]{2,1,0:T(8,128)(2,1)S(1)}, u32[]{:S(2)}, u32[]{:S(2)}) collective-permute-start(bf16[12,16,128]{2,1,0:T(8,128)(2,1)} %refs_4_.1), channel_id=1, source_target_pairs={{0,4},{4,0},{8,12},{12,8},{1,5},{5,1},{9,13},{13,9},{2,6},{6,2},{1... | collective-permute-start | bytes 147464 | tf_op jit(solution)/shard_map/ppermute | solution.py:399
  5.6 6.1 %collective-permute-start.2 = (bf16[12,16,128]{2,1,0:T(8,128)(2,1)}, bf16[12,16,128]{2,1,0:T(8,128)(2,1)S(1)}, u32[]{:S(2)}, u32[]{:S(2)}) collective-permute-start(bf16[12,16,128]{2,1,0:T(8,128)(2,1)} %refs_4_.1), channel_id=1, source_target_pairs={{0,12},{4,8},{8,4},{12,0},{1,13},{5,9},{9,5},{13,1},{2,14},{6,10},... | collective-permute-start | bytes 147464 | tf_op jit(solution)/shard_map/ppermute | solution.py:399
  11.7 0.8 %copy-start.1 = (bf16[12,16,128]{2,1,0:T(8,128)(2,1)S(1)}, bf16[12,16,128]{2,1,0:T(8,128)(2,1)}, u32[]{:S(2)}) copy-start(bf16[12,16,128]{2,1,0:T(8,128)(2,1)} %refs_4_.1) | copy-start | bytes 147460
  12.5 2.3 %copy-start.6 = (bf16[9,128,256]{2,1,0:T(8,128)(2,1)S(1)}, bf16[9,128,256]{2,1,0:T(8,128)(2,1)}, u32[]{:S(2)}) copy-start(bf16[9,128,256]{2,1,0:T(8,128)(2,1)} %wa.1) | copy-start | bytes 1769476
  12.5 2.3 %copy-start.7 = (bf16[9,128,128]{2,1,0:T(8,128)(2,1)S(1)}, bf16[9,128,128]{2,1,0:T(8,128)(2,1)}, u32[]{:S(2)}) copy-start(bf16[9,128,128]{2,1,0:T(8,128)(2,1)} %w2.1) | copy-start | bytes 884740
  12.5 2.3 %copy-start.8 = (bf16[9,128,128]{2,1,0:T(8,128)(2,1)S(1)}, bf16[9,128,128]{2,1,0:T(8,128)(2,1)}, u32[]{:S(2)}) copy-start(bf16[9,128,128]{2,1,0:T(8,128)(2,1)} %wb.1) | copy-start | bytes 884740
  12.5 2.3 %copy-start.9 = (bf16[9,128,12]{1,2,0:T(8,128)(2,1)S(1)}, bf16[9,128,12]{1,2,0:T(8,128)(2,1)}, u32[]{:S(2)}) copy-start(bf16[9,128,12]{1,2,0:T(8,128)(2,1)} %param.14) | copy-start | bytes 82948
  12.6 6.3 %collective-permute-start.3 = (bf16[448,256]{1,0:T(8,128)(2,1)S(1)}, bf16[448,256]{1,0:T(8,128)(2,1)S(1)}, u32[]{:S(2)}, u32[]{:S(2)}) collective-permute-start(bf16[448,256]{1,0:T(8,128)(2,1)S(1)} %get-tuple-element.21.refs_7_), channel_id=1, source_target_pairs={{1,0},{0,1},{3,2},{2,3},{5,4},{4,5},{7,6},{6,7},{9,8},{8,9},{11,10... | collective-permute-start | bytes 688136 | tf_op jit(solution)/shard_map/ppermute | solution.py:470
  12.7 5.6 %collective-permute-start.5 = (bf16[64,256]{1,0:T(8,128)(2,1)S(1)}, bf16[64,256]{1,0:T(8,128)(2,1)S(1)}, u32[]{:S(2)}, u32[]{:S(2)}) collective-permute-start(bf16[64,256]{1,0:T(8,128)(2,1)S(1)} %get-tuple-element.23), channel_id=1, source_target_pairs={{3,0},{2,1},{1,2},{0,3},{7,4},{6,5},{5,6},{4,7},{11,8},{10,9},{9,1... | collective-permute-start | bytes 98312 | tf_op jit(solution)/shard_map/ppermute | solution.py:466
  14.3 4.6 %collective-permute-start.4 = (bf16[176,256]{1,0:T(8,128)(2,1)S(1)}, bf16[176,256]{1,0:T(8,128)(2,1)S(1)}, u32[]{:S(2)}, u32[]{:S(2)}) collective-permute-start(bf16[176,256]{1,0:T(8,128)(2,1)S(1)} %get-tuple-element.22), channel_id=1, source_target_pairs={{2,0},{0,2},{3,1},{1,3},{6,4},{4,6},{7,5},{5,7},{10,8},{8,10},{11,... | collective-permute-start | bytes 270344 | tf_op jit(solution)/shard_map/ppermute | solution.py:461
  14.9 4.0 %copy-start = (bf16[1,128,64,128]{3,2,1,0:T(8,128)(2,1)S(1)}, bf16[1,128,64,128]{3,2,1,0:T(8,128)(2,1)}, u32[]{:S(2)}) copy-start(bf16[1,128,64,128]{3,2,1,0:T(8,128)(2,1)} %param.11) | copy-start | bytes 6291460
  14.9 4.0 %copy-start.2 = (f32[128]{0:T(128)S(1)}, f32[128]{0:T(128)}, u32[]{:S(2)}) copy-start(f32[128]{0:T(128)} %param.15) | copy-start | bytes 1540
  14.9 4.0 %copy-start.3 = (f32[128]{0:T(128)S(1)}, f32[128]{0:T(128)}, u32[]{:S(2)}) copy-start(f32[128]{0:T(128)} %param.17) | copy-start | bytes 1540
  14.9 4.0 %copy-start.4 = (f32[128]{0:T(128)S(1)}, f32[128]{0:T(128)}, u32[]{:S(2)}) copy-start(f32[128]{0:T(128)} %param.19) | copy-start | bytes 1540
  14.9 4.0 %copy-start.5 = (f32[128]{0:T(128)S(1)}, f32[128]{0:T(128)}, u32[]{:S(2)}) copy-start(f32[128]{0:T(128)} %param.20) | copy-start | bytes 1540

commit v2 on v1

--- a/solution.py
+++ b/solution.py
@@ -20,8 +20,9 @@
 
 BASE = 8
 HALO = 4
-EDGE = 8
+EDGE = HALO
 GROUP = 8
+OUT_STRIDE = 17
 SLOT = 16
 
 
@@ -33,13 +34,16 @@
     return 1.0 / root, SIGMA_DATA * SIGMA_DATA / spread, sigma * SIGMA_DATA / root, jnp.log(sigma) / 4.0
 
 
-def prep_kernel(level_ref, field_hbm, pairs_ref, left_ref, right_ref, raw, buf, sems, *, pitch):
+def prep_kernel(level_ref, field_hbm, cond_hbm, pairs_ref, left_ref, right_ref, cond_ref, raw, buf,
+                sems, *, pitch):
     steps, chans, tall, cols = raw.shape
     gets = []
     for s in range(steps):
         get = pltpu.make_async_copy(field_hbm.at[:, pl.ds(s * tall, tall), :], raw.at[s], sems.at[s])
         get.start()
         gets.append(get)
+    get_cond = pltpu.make_async_copy(cond_hbm, cond_ref, sems.at[steps])
+    get_cond.start()
     c_in = plan(level_ref)[0]
     for s in range(steps):
         gets[s].wait()
@@ -53,6 +57,7 @@
                 pairs_ref[at * pitch + 2:at * pitch + 2 + cols, lanes] = cells
                 left_ref[2 * at:2 * at + 2, lanes] = cells[:2]
                 right_ref[2 * at:2 * at + 2, lanes] = cells[cols - 2:]
+    get_cond.wait()
 
 
 def pack_kernel(*refs, geo, block_count):
@@ -134,26 +139,37 @@
                 corner = pick(sub == 0, pair[cols - 2:], pair[:2])
             else:
                 corner = pair[:2] if left else pair[cols - 2:]
-            corner_out[:2, :] = corner
-            corner_out[16:, :] = strip_out[cols:, :]
-
-
-def conv(src, weight, at, span, pitch):
+            corner_out[:half * EDGE, :] = strip_out[cols:, :]
+            corner_out[half * EDGE:half * EDGE + 2, :] = corner
+
+
+def conv(pieces, weight):
     lo, hi = slice(0, 128), slice(128, 256)
-    parts = []
+
+    def rows_of(lanes, shift, extra):
+        return jnp.concatenate(
+            [src[at + shift(pitch):at + shift(pitch) + span + extra, lanes]
+             for src, at, span, pitch in pieces], axis=0)
+
+    inner = []
     for b in range(3):
-        parts.append(src[at + b:at + b + span, hi])
-        parts.append(src[at + pitch + b:at + pitch + b + span, lo])
+        inner.append(rows_of(hi, lambda pitch: b, 0))
+        inner.append(rows_of(lo, lambda pitch: pitch + b, 0))
     y = lax.dot_general(
-        jnp.concatenate(parts, axis=1), weight[:, :768], NT, preferred_element_type=F32)
-    more = span + 8
-    upper = jnp.concatenate([src[at + b:at + b + more, lo] for b in range(2)], axis=1)
+        jnp.concatenate(inner, axis=1), weight[:, :768], NT, preferred_element_type=F32)
+    upper = jnp.concatenate([rows_of(lo, lambda pitch: b, 8) for b in range(2)], axis=1)
     upper = lax.dot_general(upper, weight[:, 768:1024], NT, preferred_element_type=F32)
-    lower = jnp.concatenate(
-        [src[at + pitch + b:at + pitch + b + more, hi] for b in range(2)], axis=1)
+    lower = jnp.concatenate([rows_of(hi, lambda pitch: pitch + b, 8) for b in range(2)], axis=1)
     lower = lax.dot_general(lower, weight[:, 1024:], NT, preferred_element_type=F32)
-    return y + jnp.concatenate(
-        [upper[:span, lo] + upper[1:span + 1, hi], lower[:span, lo] + lower[1:span + 1, hi]], axis=1)
+    results = []
+    at = more = 0
+    for _, _, span, _ in pieces:
+        a, b = upper[more:more + span + 8], lower[more:more + span + 8]
+        outer = [a[:span, lo] + a[1:span + 1, hi], b[:span, lo] + b[1:span + 1, hi]]
+        results.append(y[at:at + span] + jnp.concatenate(outer, axis=1))
+        at += span
+        more += span + 8
+    return results
 
 
 def tiles_of(dst, src, lanes):
@@ -181,7 +197,7 @@
     tiles_of(mn, wa, slice(0, chans))
     for first, count in chunks(npair - 1, GROUP):
         part[first * pitch:(first + count) * pitch, :] = conv(
-            pairs, mn, first * pitch, count * pitch, pitch)
+            [(pairs, first * pitch, count * pitch, pitch)], mn)[0]
     tiles_of(m2, w2, slice(0, chans))
     tiles_of(mf, wa, slice(chans, 2 * chans))
     tiles_of(mb, wb, slice(0, chans))
@@ -252,7 +268,7 @@
         at = BASE - HALO + w * pitch
         lw[at + HALO:at + HALO + cols, :] = cells.astype(BF16)
     for k in range(n_sub_in):
-        fill(ch, sub_in[k], [(diag_top[k], above, True, 16), (diag_bottom[k], below, False, 16)])
+        fill(ch, sub_in[k], [(diag_top[k], above, True, 0), (diag_bottom[k], below, False, 0)])
         for w in range(windows):
             cells = ch[6 * SLOT * w:6 * SLOT * w + 8 * SLOT, :].T
             at = BASE - HALO + w * pitch
@@ -305,7 +321,7 @@
 
     bias2 = twice(b2[...])
     for first, count in chunks(npair + 2, GROUP):
-        y = conv(xe, m2, BASE + first * pitch, count * pitch, pitch) + bias2
+        y = conv([(xe, BASE + first * pitch, count * pitch, pitch)], m2)[0] + bias2
         parts = inside(y, 2, 2 + cols, first, count, 2)
         for i, cells in enumerate(parts):
             at = BASE + (first + i) * pitch
@@ -315,14 +331,15 @@
         return (keep(before, sub_in[0][2 * q:2 * q + 2, :]).astype(BF16),
                 keep(after, sub_in[-1][2 * q:2 * q + 2, :]).astype(BF16))
 
+    corner = slice(half * EDGE, half * EDGE + 2)
     strip_rows = (
         (xt, strip_top, diag_top, above, 0, pairs_top[:pitch, :], 0, 1),
         (xb, strip_bottom, diag_bottom, below, 1, pairs_bottom[pitch:, :], npair - 1, 0))
     for dst, source, corners, flag, at, inner, q, inner_at in strip_rows:
         at = BASE + at * pitch
         dst[at + 2:at + 2 + cols, :] = keep(flag, source[:cols, :]).astype(BF16)
-        dst[at:at + 2, :] = keep(flag & before, corners[0][:2, :]).astype(BF16)
-        dst[at + 2 + cols:at + 4 + cols, :] = keep(flag & after, corners[-1][:2, :]).astype(BF16)
+        dst[at:at + 2, :] = keep(flag & before, corners[0][corner, :]).astype(BF16)
+        dst[at + 2 + cols:at + 4 + cols, :] = keep(flag & after, corners[-1][corner, :]).astype(BF16)
         at = BASE + inner_at * pitch
         dst[at:at + pitch, :] = inner
         dst[at:at + 2, :], dst[at + 2 + cols:at + 4 + cols, :] = halo_cells(q)
@@ -331,18 +348,20 @@
         xc[at:at + 2, :], xc[at + 6:at + 8, :] = halo_cells(q)
         xc[at + 2:at + 4, :] = left[2 * q:2 * q + 2, :]
         xc[at + 4:at + 6, :] = right[2 * q:2 * q + 2, :]
-    yc[...] = conv(xc, mn, 0, 8 * (npair - 1), 8)
+    edge_top, edge_bottom, edge_cols = conv(
+        [(xt, BASE, pitch, pitch), (xb, BASE, pitch, pitch), (xc, 0, 8 * (npair - 1), 8)], mn)
+    yc[...] = edge_cols
 
     offset = twice(ba[...] + c_noise * gain[...])
     first_cols = lax.broadcasted_iota(jnp.int32, (8, 2 * chans), 0) < 2
     for first, count in chunks(npair + 1, GROUP):
-        y = conv(xf, mf, BASE + first * pitch, count * pitch, pitch) + offset
+        y = conv([(xf, BASE + first * pitch, count * pitch, pitch)], mf)[0] + offset
         noisy = []
         for j in range(first, first + count):
             if j == 0:
-                noisy.append(conv(xt, mn, BASE, pitch, pitch))
+                noisy.append(edge_top)
             elif j == npair:
-                noisy.append(conv(xb, mn, BASE, pitch, pitch))
+                noisy.append(edge_bottom)
             else:
                 at = (j - 1) * pitch
                 edge = yc[8 * (j - 1):8 * j, :]
@@ -356,19 +375,19 @@
             at = BASE + (first + i) * pitch
             xh[at:at + pitch, :] = cells.astype(BF16)
 
-    c_skip, c_out = c_skip.reshape(1, 1, cols), c_out.reshape(1, 1, cols)
     puts = []
     for first, count in chunks(npair, 8):
-        y = conv(xh, mb, BASE + first * pitch, count * pitch, pitch)
+        y = conv([(xh, BASE + first * pitch, count * pitch, pitch)], mb)[0]
         tall = 2 * count
         for i in range(count):
             for h in range(2):
                 cells = y[i * pitch:i * pitch + cols, h * chans:(h + 1) * chans]
-                obuf[pl.ds(2 * i + h, chans, stride=tall), :] = cells.T
-        update = obuf[...].reshape(chans, tall, cols)
+                obuf[pl.ds(2 * i + h, chans, stride=OUT_STRIDE), :] = cells.T
         r0 = 2 * first
-        skip = field[:, r0:r0 + tall, :].astype(F32)
-        out[:, r0:r0 + tall, :] = (c_skip * skip + c_out * update).astype(BF16)
+        for c in range(chans):
+            update = obuf[c * OUT_STRIDE:c * OUT_STRIDE + tall, :]
+            skip = field[c, r0:r0 + tall, :].astype(F32)
+            out[c, r0:r0 + tall, :] = (c_skip * skip + c_out * update).astype(BF16)
         put = pltpu.make_async_copy(
             out.at[:, pl.ds(r0, tall), :], out_hbm.at[:, pl.ds(r0, tall), :],
             sems.at[first // 8])
@@ -405,28 +424,32 @@
     any_spec = pl.BlockSpec(memory_space=pl.ANY)
     smem = pl.BlockSpec(memory_space=pltpu.SMEM)
     vmem = pl.BlockSpec(memory_space=pltpu.VMEM)
-    pairs, left, right = pl.pallas_call(
+    pairs, left, right, own_cond = pl.pallas_call(
         functools.partial(prep_kernel, pitch=pitch),
         out_shape=[
             jax.ShapeDtypeStruct((npair * pitch + 16, 2 * chans), BF16),
             jax.ShapeDtypeStruct((2 * npair, 2 * chans), BF16),
             jax.ShapeDtypeStruct((2 * npair, 2 * chans), BF16),
+            jax.ShapeDtypeStruct(condition.shape, BF16),
         ],
-        in_specs=[smem, pl.BlockSpec(memory_space=pltpu.HBM)],
-        out_specs=[vmem] * 3,
+        in_specs=[smem] + [pl.BlockSpec(memory_space=pltpu.HBM)] * 2,
+        out_specs=[vmem] * 4,
         scratch_shapes=[
             pltpu.VMEM((steps, chans, tall, cols), BF16),
             pltpu.VMEM((chans * tall, cols), F32),
-            pltpu.SemaphoreType.DMA((steps,)),
+            pltpu.SemaphoreType.DMA((steps + 1,)),
         ],
         compiler_params=pltpu.CompilerParams(vmem_limit_bytes=12 * 2**20),
         cost_estimate=pl.CostEstimate(flops=0, bytes_accessed=16 * 2**20, transcendentals=0),
         name="prep",
-    )(levels, pltpu.with_memory_space_constraint(field, pltpu.HBM))
+    )(levels, pltpu.with_memory_space_constraint(field, pltpu.HBM),
+      pltpu.with_memory_space_constraint(condition, pltpu.HBM))
+    if len(blocks) > 1:
+        blocks[0] = own_cond
 
     whole_shape = jax.ShapeDtypeStruct((2 * npair + cin // 2 * rows, 2 * cols), BF16)
     strip_shape = jax.ShapeDtypeStruct((cols + cin // 2 * EDGE, 2 * cols), BF16)
-    diag_shape = jax.ShapeDtypeStruct((16 + cin // 2 * EDGE, 2 * cols), BF16)
+    diag_shape = jax.ShapeDtypeStruct((cin // 2 * EDGE + 8, 2 * cols), BF16)
     n_sub_out = 1 if n_sub == 2 else 2
     n_strip_out = 1 if n_strip == 2 else 2
     out_shape = [whole_shape] * n_sub_out
@@ -510,7 +533,7 @@
             cond_scratch, cond_scratch,
             pltpu.VMEM((BASE + windows * pitch + 16, 8 * SLOT), BF16),
             whole_scratch,
-            pltpu.VMEM((chans * 16, cols), F32),
+            pltpu.VMEM((chans * OUT_STRIDE, cols), F32),
             pltpu.SemaphoreType.DMA((-(-npair // 8),)),
         ],
         compiler_params=pltpu.CompilerParams(vmem_limit_bytes=28 * 2**20),

time: 35.1 us -> 32.4 us (0.923)
  Pallas kernels: 22.3 us -> 21.1 us
  local copies, waits for them, and re-layouts: 0.84 us -> 0.05 us
  waiting for transfers between devices: 2.95 us -> 2.28 us
    pallas_call x1, Pallas kernels: 15.8 us -> 14.6 us  [local(): pl.pallas_call(functools.partial(main_kernel, geo=geo, n_strip_in=n_strip...]
    unnamed x20 -> x18, local copies, waits for them, and re-layouts: 0.84 us -> 0.05 us
    ppermute x3, waiting for transfers between devices: 2.39 us -> 1.9 us  [local(): lax.ppermute(condition, 'member', [(i, i ^ k) for i in range(n_member)])]
  transfers between devices with their start and end apart: 6 -> 6, of which waited for: 2 -> 3; matrix products, arithmetic and copies ran while one was open for 0% -> 0% of each run, Pallas kernels for 18% -> 20%
where the time goes in v2:
time: 32.4 us; the launch traced here: 32.2 us
  Pallas kernels  21.1 us (65%)
  starting transfers between devices  7.83 us (24%)
  waiting for transfers between devices  2.28 us (7%)
  between operations  0.94 us (3%)
    pallas_call x1, Pallas kernels, local(): pl.pallas_call(functools.partial(main_kernel, geo=geo, n_strip_in=n_strip...  14.6 us
    ppermute x3, starting transfers between devices, local(): lax.ppermute(condition, 'member', [(i, i ^ k) for i in range(n_member)])  5.62 us
    pallas_call x1, Pallas kernels, local(): pl.pallas_call(functools.partial(noisy_kernel, geo=geo), out_shape=[jax.S...  3.4 us
    pallas_call x1, Pallas kernels, local(): pl.pallas_call(functools.partial(prep_kernel, pitch=pitch), out_shape=[ja...  3.04 us
    ppermute x3, waiting for transfers between devices, local(): lax.ppermute(condition, 'member', [(i, i ^ k) for i in range(n_member)])  1.9 us
    ppermute x1, starting transfers between devices, local(): corners.append(lax.ppermute(rest[at], ('strip', 'sub'), pairs_of))  1.61 us
  transfers between devices with their start and end apart: 6, of which 3 were waited for; matrix products, arithmetic and copies ran while one was open for 0% of the time, Pallas kernels for 20%

profile of v2, /device:TPU:0, one launch (start us, length us, event | category | flops | bytes accessed | tf_op | source)
XLA Modules:
  0.0 32.2 jit_solution(14635795385170712552)
XLA Ops:
  0.0 3.0 %collective-permute-start = (bf16[12,16,128]{2,1,0:T(8,128)(2,1)}, bf16[12,16,128]{2,1,0:T(8,128)(2,1)S(1)}, u32[]{:S(2)}, u32[]{:S(2)}) collective-permute-start(bf16[12,16,128]{2,1,0:T(8,128)(2,1)} %cond_hbm.1), channel_id=1, source_target_pairs={{0,4},{4,0},{8,12},{12,8},{1,5},{5,1},{9,13},{13,9},{2,6},{6,2},{1... | collective-permute-start | bytes 147464 | tf_op jit(solution)/shard_map/ppermute | solution.py:418
  3.0 2.5 %collective-permute-start.2 = (bf16[12,16,128]{2,1,0:T(8,128)(2,1)}, bf16[12,16,128]{2,1,0:T(8,128)(2,1)S(1)}, u32[]{:S(2)}, u32[]{:S(2)}) collective-permute-start(bf16[12,16,128]{2,1,0:T(8,128)(2,1)} %cond_hbm.1), channel_id=1, source_target_pairs={{0,12},{4,8},{8,4},{12,0},{1,13},{5,9},{9,5},{13,1},{2,14},{6,10},... | collective-permute-start | bytes 147464 | tf_op jit(solution)/shard_map/ppermute | solution.py:418
  5.5 0.1 collective-permute-start.1
  6.3 3.0 %prep.1 = (bf16[4368,256]{1,0:T(8,128)(2,1)S(1)}, bf16[64,256]{1,0:T(8,128)(2,1)S(1)}, bf16[64,256]{1,0:T(8,128)(2,1)S(1)}, bf16[12,16,128]{2,1,0:T(8,128)(2,1)S(1)}) custom-call(s32[1]{0:T(128)S(6)} %copy.12.level_ref.refs_0_, bf16[128,64,128]{2,1,0:T(8,128)(2,1)} %bitcast.7, bf16[12,16,128]{2,1,0:T(8,128)(2,1)} %cond_hbm.1), custom_call_target="tpu_custom_call" | custom-call | bytes 16777216 | tf_op jit(solution)/shard_map/prep/pallas_call | solution.py:427
  9.3 0.0 collective-permute-done.refs_5_
  9.3 0.4 %collective-permute-done.2.refs_7_ = bf16[12,16,128]{2,1,0:T(8,128)(2,1)S(1)} collective-permute-done((bf16[12,16,128]{2,1,0:T(8,128)(2,1)}, bf16[12,16,128]{2,1,0:T(8,128)(2,1)S(1)}, u32[]{:S(2)}, u32[]{:S(2)}) %collective-permute-start.2) | collective-permute-done | bytes 49184 | tf_op jit(solution)/shard_map/ppermute | solution.py:418
  9.7 1.5 %collective-permute-done.1.refs_6_ = bf16[12,16,128]{2,1,0:T(8,128)(2,1)S(1)} collective-permute-done((bf16[12,16,128]{2,1,0:T(8,128)(2,1)}, bf16[12,16,128]{2,1,0:T(8,128)(2,1)S(1)}, u32[]{:S(2)}, u32[]{:S(2)}) %collective-permute-start.1) | collective-permute-done | bytes 49184 | tf_op jit(solution)/shard_map/ppermute | solution.py:418
  11.2 0.1 pack.1
  11.3 0.1 collective-permute-start.3
  11.4 1.6 %collective-permute-start.5 = (bf16[32,256]{1,0:T(8,128)(2,1)S(1)}, bf16[32,256]{1,0:T(8,128)(2,1)S(1)}, u32[]{:S(2)}, u32[]{:S(2)}) collective-permute-start(bf16[32,256]{1,0:T(8,128)(2,1)S(1)} %get-tuple-element.25), channel_id=1, source_target_pairs={{3,0},{2,1},{1,2},{0,3},{7,4},{6,5},{5,6},{4,7},{11,8},{10,9},{9,1... | collective-permute-start | bytes 49160 | tf_op jit(solution)/shard_map/ppermute | solution.py:489
  13.0 0.5 %collective-permute-start.4 = (bf16[152,256]{1,0:T(8,128)(2,1)S(1)}, bf16[152,256]{1,0:T(8,128)(2,1)S(1)}, u32[]{:S(2)}, u32[]{:S(2)}) collective-permute-start(bf16[152,256]{1,0:T(8,128)(2,1)S(1)} %get-tuple-element.24), channel_id=1, source_target_pairs={{2,0},{0,2},{3,1},{1,3},{6,4},{4,6},{7,5},{5,7},{10,8},{8,10},{11,... | collective-permute-start | bytes 233480 | tf_op jit(solution)/shard_map/ppermute | solution.py:484
  13.6 0.0 copy-done.5
  13.6 0.0 copy-done.6
  13.6 0.0 copy-start
  13.6 0.0 copy-start.1
  13.6 0.0 copy-start.2
  13.6 0.0 copy-start.3
  13.6 0.0 copy-start.4
  13.6 3.4 %noisy.1 = (f32[4216,256]{1,0:T(8,128)S(1)}, bf16[384,768]{1,0:T(8,128)(2,1)S(1)}, bf16[256,1280]{1,0:T(8,128)(2,1)S(1)}, bf16[256,1280]{1,0:T(8,128)(2,1)S(1)},...) custom-call(bf16[4368,256]{1,0:T(8,128)(2,1)S(1)} %get-tuple-element.18.pairs.refs_0_.refs_1_.refs_3_.refs_4_, ...), custom_call_target="tpu_custom_call" | custom-call | flops 2415919104 | bytes 8388608 | tf_op jit(solution)/shard_map/noisy/pallas_call | solution.py:496
  17.0 0.0 collective-permute-done.5.refs_10_
  17.1 0.4 %collective-permute-done.4.refs_9_ = bf16[152,256]{1,0:T(8,128)(2,1)S(1)} collective-permute-done((bf16[152,256]{1,0:T(8,128)(2,1)S(1)}, bf16[152,256]{1,0:T(8,128)(2,1)S(1)}, u32[]{:S(2)}, u32[]{:S(2)}) %collective-permute-start.4) | collective-permute-done | bytes 77856 | tf_op jit(solution)/shard_map/ppermute | solution.py:484
  17.4 0.0 collective-permute-done.3.refs_8_
  17.4 0.0 copy-done
  17.5 14.6 %denoise.1 = bf16[128,64,128]{2,1,0:T(8,128)(2,1)} custom-call(s32[1]{0:T(128)S(6)} %copy.12.level_ref.refs_0_, bf16[128,64,128]{2,1,0:T(8,128)(2,1)S(1)} %bitcast.8, f32[4216,256]{1,0:T(8,128)S(1)} %get-tuple-element.19.refs_2_, bf16[4368,256]{1,0:T(8,128)(2,1)S(1)} %get-tuple-element.18.pairs.refs_0_.refs_1_.refs_3_.refs_4_, ...), custom_call_target="tpu_custom_call" | custom-call | tf_op jit(solution)/shard_map/denoise/pallas_call | solution.py:522
  (10 shorter events, 0.0 us)
Async XLA Ops:
  0.0 9.3 %collective-permute-start = (bf16[12,16,128]{2,1,0:T(8,128)(2,1)}, bf16[12,16,128]{2,1,0:T(8,128)(2,1)S(1)}, u32[]{:S(2)}, u32[]{:S(2)}) collective-permute-start(bf16[12,16,128]{2,1,0:T(8,128)(2,1)} %cond_hbm.1), channel_id=1, source_target_pairs={{0,4},{4,0},{8,12},{12,8},{1,5},{5,1},{9,13},{13,9},{2,6},{6,2},{1... | collective-permute-start | bytes 147464 | tf_op jit(solution)/shard_map/ppermute | solution.py:418
  3.0 6.7 %collective-permute-start.2 = (bf16[12,16,128]{2,1,0:T(8,128)(2,1)}, bf16[12,16,128]{2,1,0:T(8,128)(2,1)S(1)}, u32[]{:S(2)}, u32[]{:S(2)}) collective-permute-start(bf16[12,16,128]{2,1,0:T(8,128)(2,1)} %cond_hbm.1), channel_id=1, source_target_pairs={{0,12},{4,8},{8,4},{12,0},{1,13},{5,9},{9,5},{13,1},{2,14},{6,10},... | collective-permute-start | bytes 147464 | tf_op jit(solution)/shard_map/ppermute | solution.py:418
  5.5 5.7 %collective-permute-start.1 = (bf16[12,16,128]{2,1,0:T(8,128)(2,1)}, bf16[12,16,128]{2,1,0:T(8,128)(2,1)S(1)}, u32[]{:S(2)}, u32[]{:S(2)}) collective-permute-start(bf16[12,16,128]{2,1,0:T(8,128)(2,1)} %cond_hbm.1), channel_id=1, source_target_pairs={{0,8},{4,12},{8,0},{12,4},{1,9},{5,13},{9,1},{13,5},{2,10},{6,14},... | collective-permute-start | bytes 147464 | tf_op jit(solution)/shard_map/ppermute | solution.py:418
  11.2 2.3 %copy-start.5 = (bf16[9,128,256]{2,1,0:T(8,128)(2,1)S(1)}, bf16[9,128,256]{2,1,0:T(8,128)(2,1)}, u32[]{:S(2)}) copy-start(bf16[9,128,256]{2,1,0:T(8,128)(2,1)} %wa.1) | copy-start | bytes 1769476
  11.2 2.3 %copy-start.6 = (bf16[9,128,128]{2,1,0:T(8,128)(2,1)S(1)}, bf16[9,128,128]{2,1,0:T(8,128)(2,1)}, u32[]{:S(2)}) copy-start(bf16[9,128,128]{2,1,0:T(8,128)(2,1)} %w2.1) | copy-start | bytes 884740
  11.2 2.3 %copy-start.7 = (bf16[9,128,128]{2,1,0:T(8,128)(2,1)S(1)}, bf16[9,128,128]{2,1,0:T(8,128)(2,1)}, u32[]{:S(2)}) copy-start(bf16[9,128,128]{2,1,0:T(8,128)(2,1)} %wb.1) | copy-start | bytes 884740
  11.2 2.3 %copy-start.8 = (bf16[9,128,12]{1,2,0:T(8,128)(2,1)S(1)}, bf16[9,128,12]{1,2,0:T(8,128)(2,1)}, u32[]{:S(2)}) copy-start(bf16[9,128,12]{1,2,0:T(8,128)(2,1)} %param.14) | copy-start | bytes 82948
  11.3 6.1 %collective-permute-start.3 = (bf16[448,256]{1,0:T(8,128)(2,1)S(1)}, bf16[448,256]{1,0:T(8,128)(2,1)S(1)}, u32[]{:S(2)}, u32[]{:S(2)}) collective-permute-start(bf16[448,256]{1,0:T(8,128)(2,1)S(1)} %get-tuple-element.23.refs_7_), channel_id=1, source_target_pairs={{1,0},{0,1},{3,2},{2,3},{5,4},{4,5},{7,6},{6,7},{9,8},{8,9},{11,10... | collective-permute-start | bytes 688136 | tf_op jit(solution)/shard_map/ppermute | solution.py:493
  11.4 5.6 %collective-permute-start.5 = (bf16[32,256]{1,0:T(8,128)(2,1)S(1)}, bf16[32,256]{1,0:T(8,128)(2,1)S(1)}, u32[]{:S(2)}, u32[]{:S(2)}) collective-permute-start(bf16[32,256]{1,0:T(8,128)(2,1)S(1)} %get-tuple-element.25), channel_id=1, source_target_pairs={{3,0},{2,1},{1,2},{0,3},{7,4},{6,5},{5,6},{4,7},{11,8},{10,9},{9,1... | collective-permute-start | bytes 49160 | tf_op jit(solution)/shard_map/ppermute | solution.py:489
  13.0 4.4 %collective-permute-start.4 = (bf16[152,256]{1,0:T(8,128)(2,1)S(1)}, bf16[152,256]{1,0:T(8,128)(2,1)S(1)}, u32[]{:S(2)}, u32[]{:S(2)}) collective-permute-start(bf16[152,256]{1,0:T(8,128)(2,1)S(1)} %get-tuple-element.24), channel_id=1, source_target_pairs={{2,0},{0,2},{3,1},{1,3},{6,4},{4,6},{7,5},{5,7},{10,8},{8,10},{11,... | collective-permute-start | bytes 233480 | tf_op jit(solution)/shard_map/ppermute | solution.py:484
  13.6 3.9 %copy-start = (bf16[1,128,64,128]{3,2,1,0:T(8,128)(2,1)S(1)}, bf16[1,128,64,128]{3,2,1,0:T(8,128)(2,1)}, u32[]{:S(2)}) copy-start(bf16[1,128,64,128]{3,2,1,0:T(8,128)(2,1)} %param.11) | copy-start | bytes 6291460
  13.6 3.8 %copy-start.1 = (f32[128]{0:T(128)S(1)}, f32[128]{0:T(128)}, u32[]{:S(2)}) copy-start(f32[128]{0:T(128)} %param.15) | copy-start | bytes 1540
  13.6 3.8 %copy-start.2 = (f32[128]{0:T(128)S(1)}, f32[128]{0:T(128)}, u32[]{:S(2)}) copy-start(f32[128]{0:T(128)} %param.17) | copy-start | bytes 1540
  13.6 3.8 %copy-start.3 = (f32[128]{0:T(128)S(1)}, f32[128]{0:T(128)}, u32[]{:S(2)}) copy-start(f32[128]{0:T(128)} %param.19) | copy-start | bytes 1540
  13.6 3.8 %copy-start.4 = (f32[128]{0:T(128)S(1)}, f32[128]{0:T(128)}, u32[]{:S(2)}) copy-start(f32[128]{0:T(128)} %param.20) | copy-start | bytes 1540

commit v3 on v2

--- a/solution.py
+++ b/solution.py
@@ -21,21 +21,23 @@
 BASE = 8
 HALO = 4
 EDGE = HALO
+EARLY = 4
 GROUP = 8
 OUT_STRIDE = 17
+HALO_ORDER = ("strip", "diag", "sub")
 SLOT = 16
 
 
 def plan(level_ref):
-    level = jnp.full((1, 128), level_ref[0].astype(F32))
+    level = level_ref[0:1, :]
     sigma = SIG_LOW * jnp.exp(level * (math.log(SIG_HIGH / SIG_LOW) / (LEVELS - 1)))
     spread = sigma * sigma + SIGMA_DATA * SIGMA_DATA
     root = jnp.sqrt(spread)
     return 1.0 / root, SIGMA_DATA * SIGMA_DATA / spread, sigma * SIGMA_DATA / root, jnp.log(sigma) / 4.0
 
 
-def prep_kernel(level_ref, field_hbm, cond_hbm, pairs_ref, left_ref, right_ref, cond_ref, raw, buf,
-                sems, *, pitch):
+def prep_kernel(level_ref, field_hbm, cond_hbm, pairs_ref, left_ref, right_ref, cond_ref, scale_ref,
+                raw, buf, sems, *, pitch):
     steps, chans, tall, cols = raw.shape
     gets = []
     for s in range(steps):
@@ -44,7 +46,9 @@
         gets.append(get)
     get_cond = pltpu.make_async_copy(cond_hbm, cond_ref, sems.at[steps])
     get_cond.start()
-    c_in = plan(level_ref)[0]
+    c_in, c_skip, c_out, c_noise = plan(level_ref)
+    scale_ref[...] = jnp.concatenate(
+        [c_skip, c_out, c_noise, jnp.zeros((5, 128), F32)], axis=0)
     for s in range(steps):
         gets[s].wait()
         buf[...] = raw[s].astype(F32).reshape(chans * tall, cols)
@@ -60,10 +64,11 @@
     get_cond.wait()
 
 
-def pack_kernel(*refs, geo, block_count):
+def pack_kernel(*refs, geo, order):
+    block_count = len(order)
     top_ref, bottom_ref, left_ref, right_ref = refs[:4]
-    blocks = refs[4:4 + block_count]
-    outs = list(refs[4 + block_count:])
+    blocks = [refs[4 + order.index(k)] for k in range(block_count)]
+    outs = list(refs[4 + block_count + 1:])
     n_strip, n_sub, n_member = geo["n_strip"], geo["n_sub"], geo["n_member"]
     pitch, cols, rows, cin = geo["pitch"], geo["cols"], geo["rows"], geo["cin"]
     half = cin // 2
@@ -71,8 +76,9 @@
     strip = lax.axis_index("strip")
     sub = lax.axis_index("sub")
 
-    whole = outs[0]
-    edge_rows = rows
+    n_sub_out = 1 if n_sub == 2 else 2
+    rest, subs = outs[:-n_sub_out], outs[-n_sub_out:]
+    whole = subs[0]
     for k, block in enumerate(blocks):
         tall = block.shape[1]
         if block_count == 1:
@@ -106,13 +112,11 @@
 
     if n_sub == 2:
         whole[:noisy_rows, :] = pick(sub == 0, whole_right, whole_left)
-        rest = outs[1:]
     else:
         whole[:noisy_rows, :] = whole_left
-        other = outs[1]
+        other = subs[1]
         other[noisy_rows:, :] = whole[noisy_rows:, :]
         other[:noisy_rows, :] = whole_right
-        rest = outs[2:]
     tops = [None] if n_strip == 2 else [True, False]
     lefts = [None] if n_sub == 2 else [True, False]
     at = 0
@@ -191,13 +195,19 @@
     return [(at, min(size, total - at)) for at in range(0, total, size)]
 
 
-def noisy_kernel(pairs, w1, w2, wa, wb, part, m1, m2, mn, mf, mb, *, geo):
-    pitch, npair, cin = geo["pitch"], geo["rows"] // 2, geo["cin"]
-    chans = 128
-    tiles_of(mn, wa, slice(0, chans))
-    for first, count in chunks(npair - 1, GROUP):
+def first_kernel(pairs, wa, part, mn, *, pitch):
+    tiles_of(mn, wa, slice(0, 128))
+    for first, count in chunks(part.shape[0] // pitch, GROUP):
         part[first * pitch:(first + count) * pitch, :] = conv(
             [(pairs, first * pitch, count * pitch, pitch)], mn)[0]
+
+
+def second_kernel(pairs, mn, w1, w2, wa, wb, part, m1, m2, mf, mb, *, geo, skip):
+    pitch, cin = geo["pitch"], geo["cin"]
+    chans = 128
+    for first, count in chunks(part.shape[0] // pitch, GROUP):
+        part[first * pitch:(first + count) * pitch, :] = conv(
+            [(pairs, (skip + first) * pitch, count * pitch, pitch)], mn)[0]
     tiles_of(m2, w2, slice(0, chans))
     tiles_of(mf, wa, slice(chans, 2 * chans))
     tiles_of(mb, wb, slice(0, chans))
@@ -211,15 +221,16 @@
 
 def main_kernel(*refs, geo, n_strip_in, n_sub_in):
     it = iter(refs)
-    level_ref = next(it)
+    scales = next(it)
     field = next(it)
-    part, pairs_top, pairs_bottom, left, right, own = [next(it) for _ in range(6)]
-    sub_in = [next(it) for _ in range(n_sub_in)]
-    strip_in = []
-    diag_in = []
-    for _ in range(n_strip_in):
-        strip_in.append(next(it))
-        diag_in.append([next(it) for _ in range(n_sub_in)])
+    part_a, part_b, pairs_top, pairs_bottom, left, right, own = [next(it) for _ in range(7)]
+    split = part_a.shape[0] // geo["pitch"]
+    got = {}
+    for kind in HALO_ORDER:
+        count = dict(strip=n_strip_in, sub=n_sub_in, diag=n_strip_in * n_sub_in)[kind]
+        got[kind] = [next(it) for _ in range(count)]
+    strip_in, sub_in = got["strip"], got["sub"]
+    diag_in = [got["diag"][k * n_sub_in:(k + 1) * n_sub_in] for k in range(n_strip_in)]
     m1, m2, mn, mf, mb, b1, b2, ba, gain = [next(it) for _ in range(9)]
     out_hbm = next(it)
     (xe, xf, xh, xt, xb, xc, yc, cr, ch, lw, out, obuf, sems) = list(it)
@@ -235,7 +246,7 @@
     above, below = strip > 0, strip < n_strip - 1
     before, after = sub > 0, sub < n_sub - 1
 
-    _, c_skip, c_out, c_noise = plan(level_ref)
+    c_skip, c_out, c_noise = scales[0:1, :], scales[1:2, :], scales[2:3, :]
 
     def keep(flag, cells):
         return jnp.where(flag, cells.astype(F32), 0.0)
@@ -363,7 +374,8 @@
             elif j == npair:
                 noisy.append(edge_bottom)
             else:
-                at = (j - 1) * pitch
+                part, at = (part_a, j - 1) if j - 1 < split else (part_b, j - 1 - split)
+                at *= pitch
                 edge = yc[8 * (j - 1):8 * j, :]
                 noisy.append(jnp.where(first_cols, edge, part[at:at + 8, :]))
                 noisy.append(part[at + 8:at + cols, :])
@@ -422,18 +434,18 @@
     tall = 16
     steps = rows // tall
     any_spec = pl.BlockSpec(memory_space=pl.ANY)
-    smem = pl.BlockSpec(memory_space=pltpu.SMEM)
     vmem = pl.BlockSpec(memory_space=pltpu.VMEM)
-    pairs, left, right, own_cond = pl.pallas_call(
+    pairs, left, right, own_cond, scales = pl.pallas_call(
         functools.partial(prep_kernel, pitch=pitch),
         out_shape=[
             jax.ShapeDtypeStruct((npair * pitch + 16, 2 * chans), BF16),
             jax.ShapeDtypeStruct((2 * npair, 2 * chans), BF16),
             jax.ShapeDtypeStruct((2 * npair, 2 * chans), BF16),
             jax.ShapeDtypeStruct(condition.shape, BF16),
+            jax.ShapeDtypeStruct((8, 128), F32),
         ],
-        in_specs=[smem] + [pl.BlockSpec(memory_space=pltpu.HBM)] * 2,
-        out_specs=[vmem] * 4,
+        in_specs=[vmem] + [pl.BlockSpec(memory_space=pltpu.HBM)] * 2,
+        out_specs=[vmem] * 5,
         scratch_shapes=[
             pltpu.VMEM((steps, chans, tall, cols), BF16),
             pltpu.VMEM((chans * tall, cols), F32),
@@ -442,32 +454,44 @@
         compiler_params=pltpu.CompilerParams(vmem_limit_bytes=12 * 2**20),
         cost_estimate=pl.CostEstimate(flops=0, bytes_accessed=16 * 2**20, transcendentals=0),
         name="prep",
-    )(levels, pltpu.with_memory_space_constraint(field, pltpu.HBM),
-      pltpu.with_memory_space_constraint(condition, pltpu.HBM))
+    )(jnp.broadcast_to(levels.astype(F32)[:, None], (8, 128)), *[pltpu.with_memory_space_constraint(x, pltpu.HBM) for x in (field, condition)])
     if len(blocks) > 1:
         blocks[0] = own_cond
+
+    mat = jax.ShapeDtypeStruct((2 * chans, 10 * chans), BF16)
+    work = 2 * 9 * chans * chans * 2 * cols
+    split = EARLY
+    part_a, mn = pl.pallas_call(
+        functools.partial(first_kernel, pitch=pitch),
+        out_shape=[jax.ShapeDtypeStruct((split * pitch, 2 * chans), F32), mat],
+        in_specs=[vmem] * 2,
+        out_specs=[vmem] * 2,
+        compiler_params=pltpu.CompilerParams(vmem_limit_bytes=16 * 2**20),
+        cost_estimate=pl.CostEstimate(
+            flops=work * split, bytes_accessed=4 * 2**20, transcendentals=0),
+        name="noisy_first",
+    )(pairs, den_wa)
 
     whole_shape = jax.ShapeDtypeStruct((2 * npair + cin // 2 * rows, 2 * cols), BF16)
     strip_shape = jax.ShapeDtypeStruct((cols + cin // 2 * EDGE, 2 * cols), BF16)
     diag_shape = jax.ShapeDtypeStruct((cin // 2 * EDGE + 8, 2 * cols), BF16)
     n_sub_out = 1 if n_sub == 2 else 2
     n_strip_out = 1 if n_strip == 2 else 2
-    out_shape = [whole_shape] * n_sub_out
-    for _ in range(n_strip_out):
-        out_shape += [strip_shape] + [diag_shape] * n_sub_out
+    out_shape = ([strip_shape] + [diag_shape] * n_sub_out) * n_strip_out + [whole_shape] * n_sub_out
     last = npair // 2 - 1
+    order = sorted(range(len(blocks)), key=lambda k: (0, 3, 1, 2).index(k))
     packed = pl.pallas_call(
-        functools.partial(pack_kernel, geo=geo, block_count=len(blocks)),
+        functools.partial(pack_kernel, geo=geo, order=order),
         grid=(1,),
         out_shape=out_shape,
         in_specs=[
             pl.BlockSpec((2 * pitch, 2 * chans), lambda i: (0, 0)),
             pl.BlockSpec((2 * pitch, 2 * chans), lambda i: (last, 0)),
-        ] + [vmem] * (2 + len(blocks)),
+        ] + [vmem] * (2 + len(blocks)) + [any_spec],
         out_specs=[vmem] * len(out_shape),
         compiler_params=pltpu.CompilerParams(vmem_limit_bytes=8 * 2**20),
         name="pack",
-    )(pairs, pairs, left, right, *blocks)
+    )(pairs, pairs, left, right, *[blocks[k] for k in order], part_a)
 
     def up(n):
         return [(i, i - 1) for i in range(1, n)]
@@ -477,36 +501,35 @@
 
     sub_moves = [up(n_sub) + down(n_sub)] if n_sub == 2 else [up(n_sub), down(n_sub)]
     strip_moves = [up(n_strip) + down(n_strip)] if n_strip == 2 else [up(n_strip), down(n_strip)]
-    rest = packed[n_sub_out:]
-    strip_in = []
-    at = 0
-    for move in strip_moves:
-        got = [lax.ppermute(rest[at], "strip", move)]
-        at += 1
+    rest, subs = packed[:-n_sub_out], packed[-n_sub_out:]
+    sub_in = [lax.ppermute(x, "sub", move) for x, move in zip(subs, sub_moves)]
+    diag_in = []
+    for k, move in enumerate(strip_moves):
         corners = []
-        for side in sub_moves:
-            pairs_of = [(i * n_sub + j, k * n_sub + l) for i, k in move for j, l in side]
-            corners.append(lax.ppermute(rest[at], ("strip", "sub"), pairs_of))
-            at += 1
-        strip_in.append(got + corners[::-1])
-    strip_in = [x for one in strip_in[::-1] for x in one]
-    sub_in = [lax.ppermute(x, "sub", move) for x, move in zip(packed[:n_sub_out], sub_moves)][::-1]
-
-    mat = jax.ShapeDtypeStruct((2 * chans, 10 * chans), BF16)
-    part, *mats = pl.pallas_call(
-        functools.partial(noisy_kernel, geo=geo),
+        for n, side in enumerate(sub_moves):
+            pairs_of = [(i * n_sub + j, p * n_sub + q) for i, p in move for j, q in side]
+            corners.append(lax.ppermute(rest[k * (1 + n_sub_out) + 1 + n], ("strip", "sub"), pairs_of))
+        diag_in.append(corners[::-1])
+    strip_in = [
+        lax.ppermute(rest[k * (1 + n_sub_out)], "strip", move) for k, move in enumerate(strip_moves)]
+    got = dict(strip=strip_in[::-1], sub=sub_in[::-1], diag=[x for y in diag_in[::-1] for x in y])
+    halos = [x for kind in HALO_ORDER for x in got[kind]]
+
+    part_b, m1, m2, mf, mb = pl.pallas_call(
+        functools.partial(second_kernel, geo=geo, skip=split),
         out_shape=[
-            jax.ShapeDtypeStruct(((npair - 1) * pitch, 2 * chans), F32),
+            jax.ShapeDtypeStruct(((npair - 1 - split) * pitch, 2 * chans), F32),
             jax.ShapeDtypeStruct((3 * 8 * SLOT, 6 * chans), BF16),
-            mat, mat, mat, mat,
+            mat, mat, mat,
         ],
-        in_specs=[vmem] * 5,
-        out_specs=[vmem] * 6,
+        in_specs=[vmem] * 6,
+        out_specs=[vmem] * 5,
         compiler_params=pltpu.CompilerParams(vmem_limit_bytes=16 * 2**20),
         cost_estimate=pl.CostEstimate(
-            flops=2 * 9 * chans * chans * rows * cols, bytes_accessed=8 * 2**20, transcendentals=0),
-        name="noisy",
-    )(pairs, jnp.swapaxes(enc_w1, 1, 2), enc_w2, den_wa, den_wb)
+            flops=work * (npair - 1 - split), bytes_accessed=8 * 2**20, transcendentals=0),
+        name="noisy_second",
+    )(pairs, mn, jnp.swapaxes(enc_w1, 1, 2), enc_w2, den_wa, den_wb)
+    mats = [m1, m2, mn, mf, mb]
 
     flat = BASE + (npair + 3) * pitch + 16
     windows = geo["windows"]
@@ -514,16 +537,16 @@
     edge_scratch = pltpu.VMEM((BASE + 2 * pitch + 16, 2 * chans), BF16)
     cond_scratch = pltpu.VMEM(((6 * windows + 2) * SLOT, cols), F32)
     whole_scratch = pltpu.VMEM((chans, rows, cols), BF16)
-    inputs = [part, pairs, pairs, left, right, packed[0], *sub_in, *strip_in, *mats,
+    inputs = [part_a, part_b, pairs, pairs, left, right, subs[0], *halos, *mats,
               enc_b1[None], enc_b2[None], den_ba[None], noise_gain[None]]
     in_specs = [vmem] * len(inputs)
-    in_specs[1] = pl.BlockSpec((2 * pitch, 2 * chans), lambda i: (0, 0))
-    in_specs[2] = pl.BlockSpec((2 * pitch, 2 * chans), lambda i: (last, 0))
+    in_specs[2] = pl.BlockSpec((2 * pitch, 2 * chans), lambda i: (0, 0))
+    in_specs[3] = pl.BlockSpec((2 * pitch, 2 * chans), lambda i: (last, 0))
     result = pl.pallas_call(
         functools.partial(main_kernel, geo=geo, n_strip_in=n_strip_out, n_sub_in=n_sub_out),
         grid=(1,),
         out_shape=jax.ShapeDtypeStruct((chans, rows, cols), BF16),
-        in_specs=[smem, vmem] + in_specs,
+        in_specs=[vmem, vmem] + in_specs,
         out_specs=any_spec,
         scratch_shapes=[
             field_scratch, field_scratch, field_scratch,
@@ -538,7 +561,7 @@
         ],
         compiler_params=pltpu.CompilerParams(vmem_limit_bytes=28 * 2**20),
         name="denoise",
-    )(levels, field, *inputs)
+    )(scales, field, *inputs)
     return result[None]
 
 

time: 32.4 us -> 31.5 us (0.972)
  waiting for transfers between devices: 2.28 us -> 1.08 us
    ppermute x3, waiting for transfers between devices: 1.9 us -> 0.24 us  [local(): lax.ppermute(condition, 'member', [(i, i ^ k) for i in range(n_member)])]
    ppermute x3, waiting for transfers between devices: 0.38 us -> 0.84 us  [the longest x1 0.83 us: local(): lax.ppermute(rest[k * (1 + n_sub_out)], 'strip', move)]
    pallas_call x2 -> x3, Pallas kernels: 3.5 us -> 3.64 us  [the longest x1 2.95 us: local(): pl.pallas_call(functools.partial(second_kernel, geo=geo, skip=split), out...]
  transfers between devices with their start and end apart: 6 -> 6, of which waited for: 3 -> 2; matrix products, arithmetic and copies ran while one was open for 0% -> 0% of each run, Pallas kernels for 20% -> 21%
where the time goes in v3:
time: 31.5 us; the launch traced here: 31.3 us
  Pallas kernels  21.3 us (68%)
  starting transfers between devices  7.89 us (25%)
  waiting for transfers between devices  1.08 us (3%)
  between operations  0.96 us (3%)
    pallas_call x1, Pallas kernels, local(): pl.pallas_call(functools.partial(main_kernel, geo=geo, n_strip_in=n_strip...  14.7 us
    ppermute x3, starting transfers between devices, local(): lax.ppermute(condition, 'member', [(i, i ^ k) for i in range(n_member)])  5.68 us
    pallas_call x1, Pallas kernels, local(): pl.pallas_call(functools.partial(prep_kernel, pitch=pitch), out_shape=[ja...  3.04 us
    pallas_call x1, Pallas kernels, local(): pl.pallas_call(functools.partial(second_kernel, geo=geo, skip=split), out...  2.95 us
    ppermute x1, starting transfers between devices, local(): lax.ppermute(rest[k * (1 + n_sub_out) + 1 + n], ('strip', 'sub'), pairs_of)  1.61 us
    ppermute x1, waiting for transfers between devices, local(): lax.ppermute(rest[k * (1 + n_sub_out)], 'strip', move)  0.83 us
  transfers between devices with their start and end apart: 6, of which 2 were waited for; matrix products, arithmetic and copies ran while one was open for 0% of the time, Pallas kernels for 21%

profile of v3, /device:TPU:0, one launch (start us, length us, event | category | flops | bytes accessed | tf_op | source)
XLA Modules:
  0.0 31.3 jit_solution(596070135525009797)
XLA Ops:
  0.0 5.0 %collective-permute-start = (bf16[12,16,128]{2,1,0:T(8,128)(2,1)}, bf16[12,16,128]{2,1,0:T(8,128)(2,1)S(1)}, u32[]{:S(2)}, u32[]{:S(2)}) collective-permute-start(bf16[12,16,128]{2,1,0:T(8,128)(2,1)} %cond_hbm.1), channel_id=1, source_target_pairs={{0,12},{4,8},{8,4},{12,0},{1,13},{5,9},{9,5},{13,1},{2,14},{6,10},... | collective-permute-start | bytes 147464 | tf_op jit(solution)/shard_map/ppermute | solution.py:430
  5.1 0.0 collective-permute-start.2
  5.1 0.6 %collective-permute-start.1 = (bf16[12,16,128]{2,1,0:T(8,128)(2,1)}, bf16[12,16,128]{2,1,0:T(8,128)(2,1)S(1)}, u32[]{:S(2)}, u32[]{:S(2)}) collective-permute-start(bf16[12,16,128]{2,1,0:T(8,128)(2,1)} %cond_hbm.1), channel_id=1, source_target_pairs={{0,4},{4,0},{8,12},{12,8},{1,5},{5,1},{9,13},{13,9},{2,6},{6,2},{1... | collective-permute-start | bytes 147464 | tf_op jit(solution)/shard_map/ppermute | solution.py:430
  6.3 3.0 %prep.1 = (bf16[4368,256]{1,0:T(8,128)(2,1)S(1)}, bf16[64,256]{1,0:T(8,128)(2,1)S(1)}, bf16[64,256]{1,0:T(8,128)(2,1)S(1)}, bf16[12,16,128]{2,1,0:T(8,128)(2,1)S(1)}, f32[8,128]{1,0:T(8,128)S(1)}) custom-call(f32[8,128]{1,0:T(8,128)S(1)} %broadcast_in_dim.24.level_ref, bf16[128,64,128]{2,1,0:T(8,128)(2,1)} %bitcast.8, bf16[12,16,128]{2,1,0:T(8,128)(2,1)} %cond_hbm.1), custom_call_target="tpu_custom_call" | custom-call | bytes 16777216 | tf_op jit(solution)/shard_map/prep/pallas_call | solution.py:438
  9.4 0.0 copy-done.1
  9.4 0.6 %noisy_first.1 = (f32[544,256]{1,0:T(8,128)S(1)}, bf16[256,1280]{1,0:T(8,128)(2,1)S(1)}) custom-call(bf16[4368,256]{1,0:T(8,128)(2,1)S(1)} %get-tuple-element.21.pairs.refs_0_.refs_1_.refs_4_.refs_5_, bf16[9,128,256]{2,1,0:T(8,128)(2,1)S(1)} %copy-done.1), custom_call_target="tpu_custom_call" | custom-call | flops 301989888 | bytes 4194304 | tf_op jit(solution)/shard_map/noisy_first/pallas_call | solution.py:464
  10.0 0.0 collective-permute-done.refs_5_
  10.0 0.2 collective-permute-done.2.refs_7_
  10.3 0.0 collective-permute-done.1.refs_6_
  10.3 0.1 pack.1
  10.4 0.1 collective-permute-start.5
  10.4 1.6 %collective-permute-start.4 = (bf16[32,256]{1,0:T(8,128)(2,1)S(1)}, bf16[32,256]{1,0:T(8,128)(2,1)S(1)}, u32[]{:S(2)}, u32[]{:S(2)}) collective-permute-start(bf16[32,256]{1,0:T(8,128)(2,1)S(1)} %get-tuple-element.30), channel_id=1, source_target_pairs={{3,0},{2,1},{1,2},{0,3},{7,4},{6,5},{5,6},{4,7},{11,8},{10,9},{9,1... | collective-permute-start | bytes 49160 | tf_op jit(solution)/shard_map/ppermute | solution.py:511
  12.1 0.5 %collective-permute-start.3 = (bf16[152,256]{1,0:T(8,128)(2,1)S(1)}, bf16[152,256]{1,0:T(8,128)(2,1)S(1)}, u32[]{:S(2)}, u32[]{:S(2)}) collective-permute-start(bf16[152,256]{1,0:T(8,128)(2,1)S(1)} %get-tuple-element.29), channel_id=1, source_target_pairs={{2,0},{0,2},{3,1},{1,3},{6,4},{4,6},{7,5},{5,7},{10,8},{8,10},{11,... | collective-permute-start | bytes 233480 | tf_op jit(solution)/shard_map/ppermute | solution.py:514
  12.6 0.0 copy-done.6
  12.6 0.0 copy-done.7
  12.6 0.0 copy-start.2
  12.6 0.0 copy-start.3
  12.6 0.0 copy-start.4
  12.6 0.0 copy-start.5
  12.7 2.9 %noisy_second.1 = (f32[3672,256]{1,0:T(8,128)S(1)}, bf16[384,768]{1,0:T(8,128)(2,1)S(1)}, bf16[256,1280]{1,0:T(8,128)(2,1)S(1)}, bf16[256,1280]{1,0:T(8,128)(2,1)S(1)}, bf16[256,1280]{1,0:T(8,128)(2,1)S(1)}) custom-call(bf16[4368,256]{1,0:T(8,128)(2,1)S(1)} %get-tuple-element.21.pairs.refs_0_.refs_1_.refs_4_.refs_5_, ...), custom_call_target="tpu_custom_call" | custom-call | flops 2038431744 | bytes 8388608 | tf_op jit(solution)/shard_map/noisy_second/pallas_call | solution.py:518
  15.6 0.0 collective-permute-done.4.refs_10_
  15.6 0.8 %collective-permute-done.3.refs_9_ = bf16[152,256]{1,0:T(8,128)(2,1)S(1)} collective-permute-done((bf16[152,256]{1,0:T(8,128)(2,1)S(1)}, bf16[152,256]{1,0:T(8,128)(2,1)S(1)}, u32[]{:S(2)}, u32[]{:S(2)}) %collective-permute-start.3) | collective-permute-done | bytes 77856 | tf_op jit(solution)/shard_map/ppermute | solution.py:514
  16.5 0.0 collective-permute-done.5.refs_11_
  16.5 14.7 %denoise.1 = bf16[128,64,128]{2,1,0:T(8,128)(2,1)} custom-call(f32[8,128]{1,0:T(8,128)S(1)} %get-tuple-element.20.refs_0_, bf16[128,64,128]{2,1,0:T(8,128)(2,1)S(1)} %bitcast.9, f32[544,256]{1,0:T(8,128)S(1)} %get-tuple-element.22.refs_8_.refs_2_, f32[3672,256]{1,0:T(8,128)S(1)} %get-tuple-element.24.refs_3_, ...), custom_call_target="tpu_custom_call" | custom-call | tf_op jit(solution)/shard_map/denoise/pallas_call | solution.py:545
  (12 shorter events, 0.0 us)
Async XLA Ops:
  0.0 9.4 %copy-start.1 = (bf16[9,128,256]{2,1,0:T(8,128)(2,1)S(1)}, bf16[9,128,256]{2,1,0:T(8,128)(2,1)}, u32[]{:S(2)}) copy-start(bf16[9,128,256]{2,1,0:T(8,128)(2,1)} %wa.3) | copy-start | bytes 1769476
  0.0 10.0 %collective-permute-start = (bf16[12,16,128]{2,1,0:T(8,128)(2,1)}, bf16[12,16,128]{2,1,0:T(8,128)(2,1)S(1)}, u32[]{:S(2)}, u32[]{:S(2)}) collective-permute-start(bf16[12,16,128]{2,1,0:T(8,128)(2,1)} %cond_hbm.1), channel_id=1, source_target_pairs={{0,12},{4,8},{8,4},{12,0},{1,13},{5,9},{9,5},{13,1},{2,14},{6,10},... | collective-permute-start | bytes 147464 | tf_op jit(solution)/shard_map/ppermute | solution.py:430
  5.1 5.2 %collective-permute-start.2 = (bf16[12,16,128]{2,1,0:T(8,128)(2,1)}, bf16[12,16,128]{2,1,0:T(8,128)(2,1)S(1)}, u32[]{:S(2)}, u32[]{:S(2)}) collective-permute-start(bf16[12,16,128]{2,1,0:T(8,128)(2,1)} %cond_hbm.1), channel_id=1, source_target_pairs={{0,8},{4,12},{8,0},{12,4},{1,9},{5,13},{9,1},{13,5},{2,10},{6,14},... | collective-permute-start | bytes 147464 | tf_op jit(solution)/shard_map/ppermute | solution.py:430
  5.1 5.2 %collective-permute-start.1 = (bf16[12,16,128]{2,1,0:T(8,128)(2,1)}, bf16[12,16,128]{2,1,0:T(8,128)(2,1)S(1)}, u32[]{:S(2)}, u32[]{:S(2)}) collective-permute-start(bf16[12,16,128]{2,1,0:T(8,128)(2,1)} %cond_hbm.1), channel_id=1, source_target_pairs={{0,4},{4,0},{8,12},{12,8},{1,5},{5,1},{9,13},{13,9},{2,6},{6,2},{1... | collective-permute-start | bytes 147464 | tf_op jit(solution)/shard_map/ppermute | solution.py:430
  10.3 2.3 %copy-start.6 = (bf16[9,128,128]{2,1,0:T(8,128)(2,1)S(1)}, bf16[9,128,128]{2,1,0:T(8,128)(2,1)}, u32[]{:S(2)}) copy-start(bf16[9,128,128]{2,1,0:T(8,128)(2,1)} %w2.1) | copy-start | bytes 884740
  10.3 2.3 %copy-start.7 = (bf16[9,128,128]{2,1,0:T(8,128)(2,1)S(1)}, bf16[9,128,128]{2,1,0:T(8,128)(2,1)}, u32[]{:S(2)}) copy-start(bf16[9,128,128]{2,1,0:T(8,128)(2,1)} %wb.1) | copy-start | bytes 884740
  10.3 2.3 %copy-start.8 = (bf16[9,128,12]{1,2,0:T(8,128)(2,1)S(1)}, bf16[9,128,12]{1,2,0:T(8,128)(2,1)}, u32[]{:S(2)}) copy-start(bf16[9,128,12]{1,2,0:T(8,128)(2,1)} %param.14) | copy-start | bytes 82948
  10.4 6.1 %collective-permute-start.5 = (bf16[448,256]{1,0:T(8,128)(2,1)S(1)}, bf16[448,256]{1,0:T(8,128)(2,1)S(1)}, u32[]{:S(2)}, u32[]{:S(2)}) collective-permute-start(bf16[448,256]{1,0:T(8,128)(2,1)S(1)} %get-tuple-element.28.refs_8_), channel_id=1, source_target_pairs={{1,0},{0,1},{3,2},{2,3},{5,4},{4,5},{7,6},{6,7},{9,8},{8,9},{11,10... | collective-permute-start | bytes 688136 | tf_op jit(solution)/shard_map/ppermute | solution.py:505
  10.4 5.2 %collective-permute-start.4 = (bf16[32,256]{1,0:T(8,128)(2,1)S(1)}, bf16[32,256]{1,0:T(8,128)(2,1)S(1)}, u32[]{:S(2)}, u32[]{:S(2)}) collective-permute-start(bf16[32,256]{1,0:T(8,128)(2,1)S(1)} %get-tuple-element.30), channel_id=1, source_target_pairs={{3,0},{2,1},{1,2},{0,3},{7,4},{6,5},{5,6},{4,7},{11,8},{10,9},{9,1... | collective-permute-start | bytes 49160 | tf_op jit(solution)/shard_map/ppermute | solution.py:511
  12.1 4.4 %collective-permute-start.3 = (bf16[152,256]{1,0:T(8,128)(2,1)S(1)}, bf16[152,256]{1,0:T(8,128)(2,1)S(1)}, u32[]{:S(2)}, u32[]{:S(2)}) collective-permute-start(bf16[152,256]{1,0:T(8,128)(2,1)S(1)} %get-tuple-element.29), channel_id=1, source_target_pairs={{2,0},{0,2},{3,1},{1,3},{6,4},{4,6},{7,5},{5,7},{10,8},{8,10},{11,... | collective-permute-start | bytes 233480 | tf_op jit(solution)/shard_map/ppermute | solution.py:514
  12.6 3.9 %copy-start = (bf16[1,128,64,128]{3,2,1,0:T(8,128)(2,1)S(1)}, bf16[1,128,64,128]{3,2,1,0:T(8,128)(2,1)}, u32[]{:S(2)}) copy-start(bf16[1,128,64,128]{3,2,1,0:T(8,128)(2,1)} %param.11) | copy-start | bytes 6291460
  12.6 3.9 %copy-start.2 = (f32[128]{0:T(128)S(1)}, f32[128]{0:T(128)}, u32[]{:S(2)}) copy-start(f32[128]{0:T(128)} %param.15) | copy-start | bytes 1540
  12.6 3.8 %copy-start.3 = (f32[128]{0:T(128)S(1)}, f32[128]{0:T(128)}, u32[]{:S(2)}) copy-start(f32[128]{0:T(128)} %param.17) | copy-start | bytes 1540
  12.6 3.8 %copy-start.4 = (f32[128]{0:T(128)S(1)}, f32[128]{0:T(128)}, u32[]{:S(2)}) copy-start(f32[128]{0:T(128)} %param.19) | copy-start | bytes 1540
  12.6 3.8 %copy-start.5 = (f32[128]{0:T(128)S(1)}, f32[128]{0:T(128)}, u32[]{:S(2)}) copy-start(f32[128]{0:T(128)} %param.20) | copy-start | bytes 1540

commit v4 on v3

--- a/solution.py
+++ b/solution.py
@@ -25,7 +25,7 @@
 GROUP = 8
 OUT_STRIDE = 17
 HALO_ORDER = ("strip", "diag", "sub")
-SLOT = 16
+TALL = 6
 
 
 def plan(level_ref):
@@ -118,15 +118,12 @@
         other[noisy_rows:, :] = whole[noisy_rows:, :]
         other[:noisy_rows, :] = whole_right
     tops = [None] if n_strip == 2 else [True, False]
-    lefts = [None] if n_sub == 2 else [True, False]
-    at = 0
-    for top in tops:
+    for at, top in enumerate(tops):
         if top is None:
             pair = pick(strip == 0, pair_edge(False), pair_edge(True))
         else:
             pair = pair_edge(top)
         strip_out = rest[at]
-        at += 1
         strip_out[:cols, :] = pair
         for c in range(cin):
             lanes = slice((c // half) * cols, (c // half + 1) * cols)
@@ -136,15 +133,19 @@
                 cells = cond_edge(c, top)
             start = cols + (c % half) * EDGE
             strip_out[start:start + EDGE, lanes] = cells
-        for left in lefts:
-            corner_out = rest[at]
-            at += 1
-            if left is None:
-                corner = pick(sub == 0, pair[cols - 2:], pair[:2])
-            else:
-                corner = pair[:2] if left else pair[cols - 2:]
-            corner_out[:half * EDGE, :] = strip_out[cols:, :]
-            corner_out[half * EDGE:half * EDGE + 2, :] = corner
+
+
+def corner_kernel(strip_ref, *outs, cols):
+    cond_rows = strip_ref.shape[0] - cols
+    for out in outs:
+        out[:cond_rows, :] = strip_ref[cols:, :]
+    if len(outs) == 1:
+        first = lax.axis_index("sub") == 0
+        cells = jnp.where(first, strip_ref[cols - 2:cols, :].astype(F32), strip_ref[:2, :].astype(F32))
+        outs[0][cond_rows:cond_rows + 2, :] = cells.astype(BF16)
+    else:
+        outs[0][cond_rows:cond_rows + 2, :] = strip_ref[:2, :]
+        outs[1][cond_rows:cond_rows + 2, :] = strip_ref[cols - 2:cols, :]
 
 
 def conv(pieces, weight):
@@ -213,9 +214,9 @@
     tiles_of(mb, wb, slice(0, chans))
     m1[...] = jnp.zeros_like(m1)
     for b in range(3):
-        for n in range(6):
+        for n in range(TALL - 2):
             for a in range(3):
-                at = b * 8 * SLOT + (n + a) * SLOT
+                at = (b * TALL + n + a) * cin
                 m1[at:at + cin, n * chans:(n + 1) * chans] = w1[3 * a + b]
 
 
@@ -251,92 +252,8 @@
     def keep(flag, cells):
         return jnp.where(flag, cells.astype(F32), 0.0)
 
-    cr[...] = jnp.zeros_like(cr)
-    ch[...] = jnp.zeros_like(ch)
-
-    def lanes_of(c):
-        return slice((c // half) * cols, (c // half + 1) * cols)
-
-    def fill(dst, body, tops):
-        for c in range(cin):
-            at = noisy_rows + (c % half) * rows
-            dst[pl.ds(HALO * SLOT + c, rows, stride=SLOT), :] = (
-                body[at:at + rows, lanes_of(c)].astype(F32))
-            for source, flag, is_top, first in tops:
-                at = first + (c % half) * EDGE
-                cells = source[at:at + EDGE, lanes_of(c)].astype(F32)
-                if is_top:
-                    dst[pl.ds(c, HALO, stride=SLOT), :] = keep(flag, cells[EDGE - HALO:])
-                else:
-                    dst[pl.ds((HALO + rows) * SLOT + c, HALO, stride=SLOT), :] = keep(flag, cells[:HALO])
-
     strip_top, strip_bottom = strip_in[0], strip_in[-1]
     diag_top, diag_bottom = diag_in[0], diag_in[-1]
-    fill(cr, own, [(strip_top, above, True, cols), (strip_bottom, below, False, cols)])
-    windows = geo["windows"]
-    for w in range(windows):
-        cells = cr[6 * SLOT * w:6 * SLOT * w + 8 * SLOT, :].T
-        at = BASE - HALO + w * pitch
-        lw[at + HALO:at + HALO + cols, :] = cells.astype(BF16)
-    for k in range(n_sub_in):
-        fill(ch, sub_in[k], [(diag_top[k], above, True, 0), (diag_bottom[k], below, False, 0)])
-        for w in range(windows):
-            cells = ch[6 * SLOT * w:6 * SLOT * w + 8 * SLOT, :].T
-            at = BASE - HALO + w * pitch
-            if k == 0:
-                lw[at:at + HALO, :] = keep(before, cells[cols - HALO:]).astype(BF16)
-            if k == n_sub_in - 1:
-                lw[at + HALO + cols:at + 2 * HALO + cols, :] = keep(after, cells[:HALO]).astype(BF16)
-
-    def inside(y, left, right, first, count, low_row):
-        y = y.reshape(count, pitch, 2 * chans)
-        col = lax.broadcasted_iota(jnp.int32, (count, 8, 2 * chans), 1)
-        head = jnp.where((col >= left) | before, y[:, :8], 0.0)
-        tail = jnp.where((col < right - (pitch - 8)) | after, y[:, pitch - 8:], 0.0)
-        y = jnp.concatenate([head, y[:, 8:pitch - 8], tail], axis=1)
-        parts = []
-        for i in range(count):
-            halves = []
-            for h in range(2):
-                row = 2 * (first + i) + h - low_row
-                cells = y[i, :, h * chans:(h + 1) * chans]
-                if row < 0:
-                    cells = jnp.where(above, cells, 0.0)
-                elif row >= rows:
-                    cells = jnp.where(below, cells, 0.0)
-                halves.append(cells)
-            parts.append(jnp.concatenate(halves, axis=1))
-        return parts
-
-    def silu(v):
-        return v * (0.5 * jnp.tanh(0.5 * v) + 0.5)
-
-    def twice(v):
-        return jnp.concatenate([v, v], axis=1)
-
-    bias1 = twice(b1[...])
-    per = 4
-    for w0 in range(0, windows, per):
-        count = min(per, windows - w0)
-        span = count * pitch
-        at = BASE - HALO + w0 * pitch
-        lhs = jnp.concatenate([lw[at + b:at + b + span, :] for b in range(3)], axis=1)
-        y = lax.dot_general(lhs, m1[...], NN, preferred_element_type=F32)
-        for p in range(3):
-            z = silu(y[:, p * 2 * chans:(p + 1) * 2 * chans] + bias1)
-            for i in range(count):
-                j = 3 * (w0 + i) + p
-                if j < npair + 3:
-                    cells = inside(z[i * pitch:(i + 1) * pitch], 3, 3 + cols, j, 1, 3)[0]
-                    xe[BASE + j * pitch:BASE + (j + 1) * pitch, :] = cells.astype(BF16)
-
-    bias2 = twice(b2[...])
-    for first, count in chunks(npair + 2, GROUP):
-        y = conv([(xe, BASE + first * pitch, count * pitch, pitch)], m2)[0] + bias2
-        parts = inside(y, 2, 2 + cols, first, count, 2)
-        for i, cells in enumerate(parts):
-            at = BASE + (first + i) * pitch
-            xf[at:at + pitch, :] = cells.astype(BF16)
 
     def halo_cells(q):
         return (keep(before, sub_in[0][2 * q:2 * q + 2, :]).astype(BF16),
@@ -362,6 +279,97 @@
     edge_top, edge_bottom, edge_cols = conv(
         [(xt, BASE, pitch, pitch), (xb, BASE, pitch, pitch), (xc, 0, 8 * (npair - 1), 8)], mn)
     yc[...] = edge_cols
+
+    cr[...] = jnp.zeros_like(cr)
+    ch[...] = jnp.zeros_like(ch)
+
+    def lanes_of(c):
+        return slice((c // half) * cols, (c // half + 1) * cols)
+
+    def fill(dst, body, tops):
+        for c in range(cin):
+            at = noisy_rows + (c % half) * rows
+            dst[pl.ds(HALO * cin + c, rows, stride=cin), :] = (
+                body[at:at + rows, lanes_of(c)].astype(F32))
+            for source, flag, is_top, first in tops:
+                at = first + (c % half) * EDGE
+                cells = source[at:at + EDGE, lanes_of(c)].astype(F32)
+                if is_top:
+                    dst[pl.ds(c, HALO, stride=cin), :] = keep(flag, cells[EDGE - HALO:])
+                else:
+                    dst[pl.ds((HALO + rows) * cin + c, HALO, stride=cin), :] = keep(flag, cells[:HALO])
+
+    fill(cr, own, [(strip_top, above, True, cols), (strip_bottom, below, False, cols)])
+    windows = geo["windows"]
+    step = (TALL - 2) * cin
+    for w in range(windows):
+        at = BASE - HALO + w * pitch
+        lw[at + HALO:at + HALO + cols, :] = cr[step * w:step * w + chans, :].T
+    for k in range(n_sub_in):
+        fill(ch, sub_in[k], [(diag_top[k], above, True, 0), (diag_bottom[k], below, False, 0)])
+        for w in range(windows):
+            cells = ch[step * w:step * w + chans, :].T
+            at = BASE - HALO + w * pitch
+            if k == 0:
+                lw[at:at + HALO, :] = keep(before, cells[cols - HALO:])
+            if k == n_sub_in - 1:
+                lw[at + HALO + cols:at + 2 * HALO + cols, :] = keep(after, cells[:HALO])
+
+    def inside(y, left, right, first, count, low_row):
+        y = y.reshape(count, pitch, 2 * chans)
+        col = lax.broadcasted_iota(jnp.int32, (count, 8, 2 * chans), 1)
+        head = jnp.where((col >= left) | before, y[:, :8], 0.0)
+        tail = jnp.where((col < right - (pitch - 8)) | after, y[:, pitch - 8:], 0.0)
+        y = jnp.concatenate([head, y[:, 8:pitch - 8], tail], axis=1)
+        parts = []
+        for i in range(count):
+            halves = []
+            for h in range(2):
+                row = 2 * (first + i) + h - low_row
+                cells = y[i, :, h * chans:(h + 1) * chans]
+                if row < 0:
+                    cells = jnp.where(above, cells, 0.0)
+                elif row >= rows:
+                    cells = jnp.where(below, cells, 0.0)
+                halves.append(cells)
+            parts.append(jnp.concatenate(halves, axis=1))
+        return parts
+
+    def silu(v):
+        return v * (0.5 * jnp.tanh(0.5 * v) + 0.5)
+
+    def twice(v):
+        return jnp.concatenate([v, v], axis=1)
+
+    bias1 = twice(b1[...])
+    wide = TALL * cin
+    lane = lax.broadcasted_iota(jnp.int32, (1, chans), 1)
+    per = 5
+    for w0 in range(0, windows, per):
+        count = min(per, windows - w0)
+        span = count * pitch
+        at = BASE - HALO + w0 * pitch
+        middle = pltpu.roll(lw[at + 1:at + 1 + span, :], wide, 1)
+        last = pltpu.roll(lw[at + 2:at + 2 + span, :], 2 * wide - chans, 1)
+        lhs = jnp.concatenate(
+            [jnp.where(lane < wide, lw[at:at + span, :], middle),
+             jnp.where(lane < 2 * wide - chans, middle, last)], axis=1).astype(BF16)
+        y = lax.dot_general(lhs, m1[...], NN, preferred_element_type=F32)
+        for p in range((TALL - 2) // 2):
+            z = silu(y[:, p * 2 * chans:(p + 1) * 2 * chans] + bias1)
+            for i in range(count):
+                j = (TALL - 2) // 2 * (w0 + i) + p
+                if j < npair + 3:
+                    cells = inside(z[i * pitch:(i + 1) * pitch], 3, 3 + cols, j, 1, 3)[0]
+                    xe[BASE + j * pitch:BASE + (j + 1) * pitch, :] = cells.astype(BF16)
+
+    bias2 = twice(b2[...])
+    for first, count in chunks(npair + 2, GROUP):
+        y = conv([(xe, BASE + first * pitch, count * pitch, pitch)], m2)[0] + bias2
+        parts = inside(y, 2, 2 + cols, first, count, 2)
+        for i, cells in enumerate(parts):
+            at = BASE + (first + i) * pitch
+            xf[at:at + pitch, :] = cells.astype(BF16)
 
     offset = twice(ba[...] + c_noise * gain[...])
     first_cols = lax.broadcasted_iota(jnp.int32, (8, 2 * chans), 0) < 2
@@ -421,7 +429,7 @@
     pitch = cols + 2 * HALO
     npair = rows // 2
     geo = dict(n_strip=n_strip, n_sub=n_sub, n_member=n_member, pitch=pitch, cols=cols, rows=rows,
-               cin=cin, windows=-(-(rows + 6) // 6))
+               cin=cin, windows=-(-(rows + 6) // (TALL - 2)))
 
     if n_member in (1, 2, 4):
         blocks = [condition]
@@ -477,7 +485,7 @@
     diag_shape = jax.ShapeDtypeStruct((cin // 2 * EDGE + 8, 2 * cols), BF16)
     n_sub_out = 1 if n_sub == 2 else 2
     n_strip_out = 1 if n_strip == 2 else 2
-    out_shape = ([strip_shape] + [diag_shape] * n_sub_out) * n_strip_out + [whole_shape] * n_sub_out
+    out_shape = [strip_shape] * n_strip_out + [whole_shape] * n_sub_out
     last = npair // 2 - 1
     order = sorted(range(len(blocks)), key=lambda k: (0, 3, 1, 2).index(k))
     packed = pl.pallas_call(
@@ -501,17 +509,27 @@
 
     sub_moves = [up(n_sub) + down(n_sub)] if n_sub == 2 else [up(n_sub), down(n_sub)]
     strip_moves = [up(n_strip) + down(n_strip)] if n_strip == 2 else [up(n_strip), down(n_strip)]
-    rest, subs = packed[:-n_sub_out], packed[-n_sub_out:]
+    strips, subs = packed[:-n_sub_out], packed[-n_sub_out:]
+    diags = [
+        pl.pallas_call(
+            functools.partial(corner_kernel, cols=cols),
+            out_shape=[diag_shape] * n_sub_out,
+            in_specs=[vmem],
+            out_specs=[vmem] * n_sub_out,
+            compiler_params=pltpu.CompilerParams(vmem_limit_bytes=8 * 2**20),
+            name="corners",
+        )(strip)
+        for strip in strips
+    ]
     sub_in = [lax.ppermute(x, "sub", move) for x, move in zip(subs, sub_moves)]
     diag_in = []
     for k, move in enumerate(strip_moves):
         corners = []
         for n, side in enumerate(sub_moves):
             pairs_of = [(i * n_sub + j, p * n_sub + q) for i, p in move for j, q in side]
-            corners.append(lax.ppermute(rest[k * (1 + n_sub_out) + 1 + n], ("strip", "sub"), pairs_of))
+            corners.append(lax.ppermute(diags[k][n], ("strip", "sub"), pairs_of))
         diag_in.append(corners[::-1])
-    strip_in = [
-        lax.ppermute(rest[k * (1 + n_sub_out)], "strip", move) for k, move in enumerate(strip_moves)]
+    strip_in = [lax.ppermute(x, "strip", move) for x, move in zip(strips, strip_moves)]
     got = dict(strip=strip_in[::-1], sub=sub_in[::-1], diag=[x for y in diag_in[::-1] for x in y])
     halos = [x for kind in HALO_ORDER for x in got[kind]]
 
@@ -519,7 +537,7 @@
         functools.partial(second_kernel, geo=geo, skip=split),
         out_shape=[
             jax.ShapeDtypeStruct(((npair - 1 - split) * pitch, 2 * chans), F32),
-            jax.ShapeDtypeStruct((3 * 8 * SLOT, 6 * chans), BF16),
+            jax.ShapeDtypeStruct((2 * chans, (TALL - 2) * chans), BF16),
             mat, mat, mat,
         ],
         in_specs=[vmem] * 6,
@@ -535,7 +553,7 @@
     windows = geo["windows"]
     field_scratch = pltpu.VMEM((flat, 2 * chans), BF16)
     edge_scratch = pltpu.VMEM((BASE + 2 * pitch + 16, 2 * chans), BF16)
-    cond_scratch = pltpu.VMEM(((6 * windows + 2) * SLOT, cols), F32)
+    cond_scratch = pltpu.VMEM(((TALL - 2) * cin * (windows - 1) + chans, cols), F32)
     whole_scratch = pltpu.VMEM((chans, rows, cols), BF16)
     inputs = [part_a, part_b, pairs, pairs, left, right, subs[0], *halos, *mats,
               enc_b1[None], enc_b2[None], den_ba[None], noise_gain[None]]
@@ -554,7 +572,7 @@
             pltpu.VMEM((8 * npair + 16, 2 * chans), BF16),
             pltpu.VMEM((8 * (npair - 1), 2 * chans), F32),
             cond_scratch, cond_scratch,
-            pltpu.VMEM((BASE + windows * pitch + 16, 8 * SLOT), BF16),
+            pltpu.VMEM((BASE + windows * pitch + 16, chans), F32),
             whole_scratch,
             pltpu.VMEM((chans * OUT_STRIDE, cols), F32),
             pltpu.SemaphoreType.DMA((-(-npair // 8),)),

time: 31.5 us -> 30.2 us (0.959)
  waiting for transfers between devices: 1.08 us -> 0.33 us
    ppermute x2, waiting for transfers between devices: 0.84 us -> 0.09 us  [the longest x1 0.06 us: local(): lax.ppermute(x, 'strip', move)]
  transfers between devices with their start and end apart: 6 -> 6, of which waited for: 2 -> 2; matrix products, arithmetic and copies ran while one was open for 0% -> 0% of each run, Pallas kernels for 21% -> 22%
where the time goes in v4:
time: 30.2 us; the launch traced here: 30 us
  Pallas kernels  21.1 us (70%)
  starting transfers between devices  7.6 us (25%)
  between operations  0.96 us (3%)
  waiting for transfers between devices  0.33 us (1%)
    pallas_call x1, Pallas kernels, local(): pl.pallas_call(functools.partial(main_kernel, geo=geo, n_strip_in=n_strip...  14.4 us
    ppermute x3, starting transfers between devices, local(): lax.ppermute(condition, 'member', [(i, i ^ k) for i in range(n_member)])  5.68 us
    pallas_call x1, Pallas kernels, local(): pl.pallas_call(functools.partial(prep_kernel, pitch=pitch), out_shape=[ja...  3.04 us
    pallas_call x1, Pallas kernels, local(): pl.pallas_call(functools.partial(second_kernel, geo=geo, skip=split), out...  2.92 us
    ppermute x1, starting transfers between devices, local(): lax.ppermute(x, 'strip', move)  1.56 us
  transfers between devices with their start and end apart: 6, of which 2 were waited for; matrix products, arithmetic and copies ran while one was open for 0% of the time, Pallas kernels for 22%

profile of v4, /device:TPU:0, one launch (start us, length us, event | category | flops | bytes accessed | tf_op | source)
XLA Modules:
  0.0 30.0 jit_solution(7044282562430284510)
XLA Ops:
  0.0 5.0 %collective-permute-start = (bf16[12,16,128]{2,1,0:T(8,128)(2,1)}, bf16[12,16,128]{2,1,0:T(8,128)(2,1)S(1)}, u32[]{:S(2)}, u32[]{:S(2)}) collective-permute-start(bf16[12,16,128]{2,1,0:T(8,128)(2,1)} %cond_hbm.1), channel_id=1, source_target_pairs={{0,12},{4,8},{8,4},{12,0},{1,13},{5,9},{9,5},{13,1},{2,14},{6,10},... | collective-permute-start | bytes 147464 | tf_op jit(solution)/shard_map/ppermute | solution.py:438
  5.1 0.0 collective-permute-start.2
  5.1 0.6 %collective-permute-start.1 = (bf16[12,16,128]{2,1,0:T(8,128)(2,1)}, bf16[12,16,128]{2,1,0:T(8,128)(2,1)S(1)}, u32[]{:S(2)}, u32[]{:S(2)}) collective-permute-start(bf16[12,16,128]{2,1,0:T(8,128)(2,1)} %cond_hbm.1), channel_id=1, source_target_pairs={{0,4},{4,0},{8,12},{12,8},{1,5},{5,1},{9,13},{13,9},{2,6},{6,2},{1... | collective-permute-start | bytes 147464 | tf_op jit(solution)/shard_map/ppermute | solution.py:438
  6.3 3.0 %prep.1 = (bf16[4368,256]{1,0:T(8,128)(2,1)S(1)}, bf16[64,256]{1,0:T(8,128)(2,1)S(1)}, bf16[64,256]{1,0:T(8,128)(2,1)S(1)}, bf16[12,16,128]{2,1,0:T(8,128)(2,1)S(1)}, f32[8,128]{1,0:T(8,128)S(1)}) custom-call(f32[8,128]{1,0:T(8,128)S(1)} %broadcast_in_dim.24.level_ref, bf16[128,64,128]{2,1,0:T(8,128)(2,1)} %bitcast.8, bf16[12,16,128]{2,1,0:T(8,128)(2,1)} %cond_hbm.1), custom_call_target="tpu_custom_call" | custom-call | bytes 16777216 | tf_op jit(solution)/shard_map/prep/pallas_call | solution.py:446
  9.4 0.0 copy-done.1
  9.4 0.6 %noisy_first.1 = (f32[544,256]{1,0:T(8,128)S(1)}, bf16[256,1280]{1,0:T(8,128)(2,1)S(1)}) custom-call(bf16[4368,256]{1,0:T(8,128)(2,1)S(1)} %get-tuple-element.20.pairs.refs_0_.refs_1_.refs_4_.refs_5_, bf16[9,128,256]{2,1,0:T(8,128)(2,1)S(1)} %copy-done.1), custom_call_target="tpu_custom_call" | custom-call | flops 301989888 | bytes 4194304 | tf_op jit(solution)/shard_map/noisy_first/pallas_call | solution.py:472
  10.0 0.0 collective-permute-done.refs_5_
  10.0 0.2 collective-permute-done.2.refs_7_
  10.3 0.0 collective-permute-done.1.refs_6_
  10.3 0.1 pack.1
  10.4 0.1 collective-permute-start.5
  10.5 1.6 %collective-permute-start.3 = (bf16[152,256]{1,0:T(8,128)(2,1)S(1)}, bf16[152,256]{1,0:T(8,128)(2,1)S(1)}, u32[]{:S(2)}, u32[]{:S(2)}) collective-permute-start(bf16[152,256]{1,0:T(8,128)(2,1)S(1)} %get-tuple-element.28.strip_ref), channel_id=1, source_target_pairs={{2,0},{0,2},{3,1},{1,3},{6,4},{4,6},{7,5},{5,7},{10,8},{8,10},{11,... | collective-permute-start | bytes 233480 | tf_op jit(solution)/shard_map/ppermute | solution.py:532
  12.0 0.3 collective-permute-start.4
  12.3 0.0 copy-done.8
  12.3 0.0 copy-start.2
  12.3 0.0 copy-start.3
  12.4 0.0 copy-start.4
  12.4 0.0 copy-start.5
  12.4 2.9 %noisy_second.1 = (f32[3672,256]{1,0:T(8,128)S(1)}, bf16[256,512]{1,0:T(8,128)(2,1)S(1)}, bf16[256,1280]{1,0:T(8,128)(2,1)S(1)}, bf16[256,1280]{1,0:T(8,128)(2,1)S(1)}, bf16[256,1280]{1,0:T(8,128)(2,1)S(1)}) custom-call(bf16[4368,256]{1,0:T(8,128)(2,1)S(1)} %get-tuple-element.20.pairs.refs_0_.refs_1_.refs_4_.refs_5_, ...), custom_call_target="tpu_custom_call" | custom-call | flops 2038431744 | bytes 8388608 | tf_op jit(solution)/shard_map/noisy_second/pallas_call | solution.py:536
  15.3 0.0 collective-permute-done.4.refs_10_
  15.3 0.1 collective-permute-done.3.refs_9_
  15.4 0.0 collective-permute-done.5.refs_11_
  15.4 0.0 copy-done
  15.4 14.4 %denoise.1 = bf16[128,64,128]{2,1,0:T(8,128)(2,1)} custom-call(f32[8,128]{1,0:T(8,128)S(1)} %get-tuple-element.19.refs_0_, bf16[128,64,128]{2,1,0:T(8,128)(2,1)S(1)} %bitcast.9, f32[544,256]{1,0:T(8,128)S(1)} %get-tuple-element.21.refs_8_.refs_2_, f32[3672,256]{1,0:T(8,128)S(1)} %get-tuple-element.23.refs_3_, ...), custom_call_target="tpu_custom_call" | custom-call | tf_op jit(solution)/shard_map/denoise/pallas_call | solution.py:563
  (13 shorter events, 0.0 us)
Async XLA Ops:
  0.0 9.4 %copy-start.1 = (bf16[9,128,256]{2,1,0:T(8,128)(2,1)S(1)}, bf16[9,128,256]{2,1,0:T(8,128)(2,1)}, u32[]{:S(2)}) copy-start(bf16[9,128,256]{2,1,0:T(8,128)(2,1)} %wa.3) | copy-start | bytes 1769476
  0.0 10.0 %collective-permute-start = (bf16[12,16,128]{2,1,0:T(8,128)(2,1)}, bf16[12,16,128]{2,1,0:T(8,128)(2,1)S(1)}, u32[]{:S(2)}, u32[]{:S(2)}) collective-permute-start(bf16[12,16,128]{2,1,0:T(8,128)(2,1)} %cond_hbm.1), channel_id=1, source_target_pairs={{0,12},{4,8},{8,4},{12,0},{1,13},{5,9},{9,5},{13,1},{2,14},{6,10},... | collective-permute-start | bytes 147464 | tf_op jit(solution)/shard_map/ppermute | solution.py:438
  5.1 5.2 %collective-permute-start.2 = (bf16[12,16,128]{2,1,0:T(8,128)(2,1)}, bf16[12,16,128]{2,1,0:T(8,128)(2,1)S(1)}, u32[]{:S(2)}, u32[]{:S(2)}) collective-permute-start(bf16[12,16,128]{2,1,0:T(8,128)(2,1)} %cond_hbm.1), channel_id=1, source_target_pairs={{0,8},{4,12},{8,0},{12,4},{1,9},{5,13},{9,1},{13,5},{2,10},{6,14},... | collective-permute-start | bytes 147464 | tf_op jit(solution)/shard_map/ppermute | solution.py:438
  5.1 5.2 %collective-permute-start.1 = (bf16[12,16,128]{2,1,0:T(8,128)(2,1)}, bf16[12,16,128]{2,1,0:T(8,128)(2,1)S(1)}, u32[]{:S(2)}, u32[]{:S(2)}) collective-permute-start(bf16[12,16,128]{2,1,0:T(8,128)(2,1)} %cond_hbm.1), channel_id=1, source_target_pairs={{0,4},{4,0},{8,12},{12,8},{1,5},{5,1},{9,13},{13,9},{2,6},{6,2},{1... | collective-permute-start | bytes 147464 | tf_op jit(solution)/shard_map/ppermute | solution.py:438
  10.3 2.1 %copy-start.6 = (bf16[9,128,128]{2,1,0:T(8,128)(2,1)S(1)}, bf16[9,128,128]{2,1,0:T(8,128)(2,1)}, u32[]{:S(2)}) copy-start(bf16[9,128,128]{2,1,0:T(8,128)(2,1)} %w2.1) | copy-start | bytes 884740
  10.3 2.1 %copy-start.7 = (bf16[9,128,128]{2,1,0:T(8,128)(2,1)S(1)}, bf16[9,128,128]{2,1,0:T(8,128)(2,1)}, u32[]{:S(2)}) copy-start(bf16[9,128,128]{2,1,0:T(8,128)(2,1)} %wb.1) | copy-start | bytes 884740
  10.3 2.1 %copy-start.8 = (bf16[9,128,12]{1,2,0:T(8,128)(2,1)S(1)}, bf16[9,128,12]{1,2,0:T(8,128)(2,1)}, u32[]{:S(2)}) copy-start(bf16[9,128,12]{1,2,0:T(8,128)(2,1)} %param.14) | copy-start | bytes 82948
  10.4 5.0 %collective-permute-start.5 = (bf16[448,256]{1,0:T(8,128)(2,1)S(1)}, bf16[448,256]{1,0:T(8,128)(2,1)S(1)}, u32[]{:S(2)}, u32[]{:S(2)}) collective-permute-start(bf16[448,256]{1,0:T(8,128)(2,1)S(1)} %get-tuple-element.27.refs_8_), channel_id=1, source_target_pairs={{1,0},{0,1},{3,2},{2,3},{5,4},{4,5},{7,6},{6,7},{9,8},{8,9},{11,10... | collective-permute-start | bytes 688136 | tf_op jit(solution)/shard_map/ppermute | solution.py:524
  10.5 4.9 %collective-permute-start.3 = (bf16[152,256]{1,0:T(8,128)(2,1)S(1)}, bf16[152,256]{1,0:T(8,128)(2,1)S(1)}, u32[]{:S(2)}, u32[]{:S(2)}) collective-permute-start(bf16[152,256]{1,0:T(8,128)(2,1)S(1)} %get-tuple-element.28.strip_ref), channel_id=1, source_target_pairs={{2,0},{0,2},{3,1},{1,3},{6,4},{4,6},{7,5},{5,7},{10,8},{8,10},{11,... | collective-permute-start | bytes 233480 | tf_op jit(solution)/shard_map/ppermute | solution.py:532
  12.0 3.3 %collective-permute-start.4 = (bf16[32,256]{1,0:T(8,128)(2,1)S(1)}, bf16[32,256]{1,0:T(8,128)(2,1)S(1)}, u32[]{:S(2)}, u32[]{:S(2)}) collective-permute-start(bf16[32,256]{1,0:T(8,128)(2,1)S(1)} %corners.1), channel_id=1, source_target_pairs={{3,0},{2,1},{1,2},{0,3},{7,4},{6,5},{5,6},{4,7},{11,8},{10,9},{9,1... | collective-permute-start | bytes 49160 | tf_op jit(solution)/shard_map/ppermute | solution.py:530
  12.3 3.1 %copy-start = (bf16[1,128,64,128]{3,2,1,0:T(8,128)(2,1)S(1)}, bf16[1,128,64,128]{3,2,1,0:T(8,128)(2,1)}, u32[]{:S(2)}) copy-start(bf16[1,128,64,128]{3,2,1,0:T(8,128)(2,1)} %param.11) | copy-start | bytes 6291460
  12.3 3.1 %copy-start.2 = (f32[128]{0:T(128)S(1)}, f32[128]{0:T(128)}, u32[]{:S(2)}) copy-start(f32[128]{0:T(128)} %param.15) | copy-start | bytes 1540
  12.3 3.1 %copy-start.3 = (f32[128]{0:T(128)S(1)}, f32[128]{0:T(128)}, u32[]{:S(2)}) copy-start(f32[128]{0:T(128)} %param.17) | copy-start | bytes 1540
  12.4 3.1 %copy-start.4 = (f32[128]{0:T(128)S(1)}, f32[128]{0:T(128)}, u32[]{:S(2)}) copy-start(f32[128]{0:T(128)} %param.19) | copy-start | bytes 1540
  12.4 3.1 %copy-start.5 = (f32[128]{0:T(128)S(1)}, f32[128]{0:T(128)}, u32[]{:S(2)}) copy-start(f32[128]{0:T(128)} %param.20) | copy-start | bytes 1540

commit v5 on v4

--- a/solution.py
+++ b/solution.py
@@ -336,7 +336,7 @@
         return parts
 
     def silu(v):
-        return v * (0.5 * jnp.tanh(0.5 * v) + 0.5)
+        return v * jax.nn.sigmoid(v)
 
     def twice(v):
         return jnp.concatenate([v, v], axis=1)
@@ -397,11 +397,11 @@
 
     puts = []
     for first, count in chunks(npair, 8):
-        y = conv([(xh, BASE + first * pitch, count * pitch, pitch)], mb)[0]
+        y = conv([(xh, BASE + j * pitch, cols, pitch) for j in range(first, first + count)], mb)
         tall = 2 * count
         for i in range(count):
             for h in range(2):
-                cells = y[i * pitch:i * pitch + cols, h * chans:(h + 1) * chans]
+                cells = y[i][:, h * chans:(h + 1) * chans]
                 obuf[pl.ds(2 * i + h, chans, stride=OUT_STRIDE), :] = cells.T
         r0 = 2 * first
         for c in range(chans):

time: 30.2 us -> 29.3 us (0.970)
  Pallas kernels: 21.1 us -> 20.2 us
    pallas_call x1, Pallas kernels: 14.4 us -> 13.5 us  [local(): pl.pallas_call(functools.partial(main_kernel, geo=geo, n_strip_in=n_strip...]
  transfers between devices with their start and end apart: 6 -> 6, of which waited for: 2 -> 2; matrix products, arithmetic and copies ran while one was open for 0% -> 0% of each run, Pallas kernels for 22% -> 23%
where the time goes in v5:
time: 29.3 us; the launch traced here: 29.1 us
  Pallas kernels  20.2 us (69%)
  starting transfers between devices  7.6 us (26%)
  between operations  0.96 us (3%)
  waiting for transfers between devices  0.33 us (1%)
    pallas_call x1, Pallas kernels, local(): pl.pallas_call(functools.partial(main_kernel, geo=geo, n_strip_in=n_strip...  13.5 us
    ppermute x3, starting transfers between devices, local(): lax.ppermute(condition, 'member', [(i, i ^ k) for i in range(n_member)])  5.68 us
    pallas_call x1, Pallas kernels, local(): pl.pallas_call(functools.partial(prep_kernel, pitch=pitch), out_shape=[ja...  3.04 us
    pallas_call x1, Pallas kernels, local(): pl.pallas_call(functools.partial(second_kernel, geo=geo, skip=split), out...  2.92 us
    ppermute x1, starting transfers between devices, local(): lax.ppermute(x, 'strip', move)  1.56 us
    pallas_call x1, Pallas kernels, local(): pl.pallas_call(functools.partial(first_kernel, pitch=pitch), out_shape=[j...  0.6 us
  transfers between devices with their start and end apart: 6, of which 2 were waited for; matrix products, arithmetic and copies ran while one was open for 0% of the time, Pallas kernels for 23%

profile of v5, /device:TPU:0, one launch (start us, length us, event | category | flops | bytes accessed | tf_op | source)
XLA Modules:
  0.0 29.1 jit_solution(13991558124721472169)
XLA Ops:
  0.0 5.0 %collective-permute-start = (bf16[12,16,128]{2,1,0:T(8,128)(2,1)}, bf16[12,16,128]{2,1,0:T(8,128)(2,1)S(1)}, u32[]{:S(2)}, u32[]{:S(2)}) collective-permute-start(bf16[12,16,128]{2,1,0:T(8,128)(2,1)} %cond_hbm.1), channel_id=1, source_target_pairs={{0,12},{4,8},{8,4},{12,0},{1,13},{5,9},{9,5},{13,1},{2,14},{6,10},... | collective-permute-start | bytes 147464 | tf_op jit(solution)/shard_map/ppermute | solution.py:438
  5.1 0.0 collective-permute-start.2
  5.1 0.6 %collective-permute-start.1 = (bf16[12,16,128]{2,1,0:T(8,128)(2,1)}, bf16[12,16,128]{2,1,0:T(8,128)(2,1)S(1)}, u32[]{:S(2)}, u32[]{:S(2)}) collective-permute-start(bf16[12,16,128]{2,1,0:T(8,128)(2,1)} %cond_hbm.1), channel_id=1, source_target_pairs={{0,4},{4,0},{8,12},{12,8},{1,5},{5,1},{9,13},{13,9},{2,6},{6,2},{1... | collective-permute-start | bytes 147464 | tf_op jit(solution)/shard_map/ppermute | solution.py:438
  6.3 3.0 %prep.1 = (bf16[4368,256]{1,0:T(8,128)(2,1)S(1)}, bf16[64,256]{1,0:T(8,128)(2,1)S(1)}, bf16[64,256]{1,0:T(8,128)(2,1)S(1)}, bf16[12,16,128]{2,1,0:T(8,128)(2,1)S(1)}, f32[8,128]{1,0:T(8,128)S(1)}) custom-call(f32[8,128]{1,0:T(8,128)S(1)} %broadcast_in_dim.24.level_ref, bf16[128,64,128]{2,1,0:T(8,128)(2,1)} %bitcast.8, bf16[12,16,128]{2,1,0:T(8,128)(2,1)} %cond_hbm.1), custom_call_target="tpu_custom_call" | custom-call | bytes 16777216 | tf_op jit(solution)/shard_map/prep/pallas_call | solution.py:446
  9.4 0.0 copy-done.1
  9.4 0.6 %noisy_first.1 = (f32[544,256]{1,0:T(8,128)S(1)}, bf16[256,1280]{1,0:T(8,128)(2,1)S(1)}) custom-call(bf16[4368,256]{1,0:T(8,128)(2,1)S(1)} %get-tuple-element.20.pairs.refs_0_.refs_1_.refs_4_.refs_5_, bf16[9,128,256]{2,1,0:T(8,128)(2,1)S(1)} %copy-done.1), custom_call_target="tpu_custom_call" | custom-call | flops 301989888 | bytes 4194304 | tf_op jit(solution)/shard_map/noisy_first/pallas_call | solution.py:472
  10.0 0.0 collective-permute-done.refs_5_
  10.0 0.2 collective-permute-done.2.refs_7_
  10.3 0.0 collective-permute-done.1.refs_6_
  10.3 0.1 pack.1
  10.4 0.1 collective-permute-start.5
  10.5 1.6 %collective-permute-start.3 = (bf16[152,256]{1,0:T(8,128)(2,1)S(1)}, bf16[152,256]{1,0:T(8,128)(2,1)S(1)}, u32[]{:S(2)}, u32[]{:S(2)}) collective-permute-start(bf16[152,256]{1,0:T(8,128)(2,1)S(1)} %get-tuple-element.28.strip_ref), channel_id=1, source_target_pairs={{2,0},{0,2},{3,1},{1,3},{6,4},{4,6},{7,5},{5,7},{10,8},{8,10},{11,... | collective-permute-start | bytes 233480 | tf_op jit(solution)/shard_map/ppermute | solution.py:532
  12.0 0.3 %collective-permute-start.4 = (bf16[32,256]{1,0:T(8,128)(2,1)S(1)}, bf16[32,256]{1,0:T(8,128)(2,1)S(1)}, u32[]{:S(2)}, u32[]{:S(2)}) collective-permute-start(bf16[32,256]{1,0:T(8,128)(2,1)S(1)} %corners.1), channel_id=1, source_target_pairs={{3,0},{2,1},{1,2},{0,3},{7,4},{6,5},{5,6},{4,7},{11,8},{10,9},{9,1... | collective-permute-start | bytes 49160 | tf_op jit(solution)/shard_map/ppermute | solution.py:530
  12.3 0.0 copy-done.8
  12.3 0.0 copy-start.2
  12.3 0.0 copy-start.3
  12.4 0.0 copy-start.4
  12.4 0.0 copy-start.5
  12.4 2.9 %noisy_second.1 = (f32[3672,256]{1,0:T(8,128)S(1)}, bf16[256,512]{1,0:T(8,128)(2,1)S(1)}, bf16[256,1280]{1,0:T(8,128)(2,1)S(1)}, bf16[256,1280]{1,0:T(8,128)(2,1)S(1)}, bf16[256,1280]{1,0:T(8,128)(2,1)S(1)}) custom-call(bf16[4368,256]{1,0:T(8,128)(2,1)S(1)} %get-tuple-element.20.pairs.refs_0_.refs_1_.refs_4_.refs_5_, ...), custom_call_target="tpu_custom_call" | custom-call | flops 2038431744 | bytes 8388608 | tf_op jit(solution)/shard_map/noisy_second/pallas_call | solution.py:536
  15.3 0.0 collective-permute-done.4.refs_10_
  15.3 0.1 collective-permute-done.3.refs_9_
  15.4 0.0 collective-permute-done.5.refs_11_
  15.4 0.0 copy-done
  15.4 13.5 %denoise.1 = bf16[128,64,128]{2,1,0:T(8,128)(2,1)} custom-call(f32[8,128]{1,0:T(8,128)S(1)} %get-tuple-element.19.refs_0_, bf16[128,64,128]{2,1,0:T(8,128)(2,1)S(1)} %bitcast.9, f32[544,256]{1,0:T(8,128)S(1)} %get-tuple-element.21.refs_8_.refs_2_, f32[3672,256]{1,0:T(8,128)S(1)} %get-tuple-element.23.refs_3_, ...), custom_call_target="tpu_custom_call" | custom-call | tf_op jit(solution)/shard_map/denoise/pallas_call | solution.py:563
  (13 shorter events, 0.0 us)
Async XLA Ops:
  0.0 9.4 %copy-start.1 = (bf16[9,128,256]{2,1,0:T(8,128)(2,1)S(1)}, bf16[9,128,256]{2,1,0:T(8,128)(2,1)}, u32[]{:S(2)}) copy-start(bf16[9,128,256]{2,1,0:T(8,128)(2,1)} %wa.3) | copy-start | bytes 1769476
  0.0 10.0 %collective-permute-start = (bf16[12,16,128]{2,1,0:T(8,128)(2,1)}, bf16[12,16,128]{2,1,0:T(8,128)(2,1)S(1)}, u32[]{:S(2)}, u32[]{:S(2)}) collective-permute-start(bf16[12,16,128]{2,1,0:T(8,128)(2,1)} %cond_hbm.1), channel_id=1, source_target_pairs={{0,12},{4,8},{8,4},{12,0},{1,13},{5,9},{9,5},{13,1},{2,14},{6,10},... | collective-permute-start | bytes 147464 | tf_op jit(solution)/shard_map/ppermute | solution.py:438
  5.1 5.2 %collective-permute-start.2 = (bf16[12,16,128]{2,1,0:T(8,128)(2,1)}, bf16[12,16,128]{2,1,0:T(8,128)(2,1)S(1)}, u32[]{:S(2)}, u32[]{:S(2)}) collective-permute-start(bf16[12,16,128]{2,1,0:T(8,128)(2,1)} %cond_hbm.1), channel_id=1, source_target_pairs={{0,8},{4,12},{8,0},{12,4},{1,9},{5,13},{9,1},{13,5},{2,10},{6,14},... | collective-permute-start | bytes 147464 | tf_op jit(solution)/shard_map/ppermute | solution.py:438
  5.1 5.2 %collective-permute-start.1 = (bf16[12,16,128]{2,1,0:T(8,128)(2,1)}, bf16[12,16,128]{2,1,0:T(8,128)(2,1)S(1)}, u32[]{:S(2)}, u32[]{:S(2)}) collective-permute-start(bf16[12,16,128]{2,1,0:T(8,128)(2,1)} %cond_hbm.1), channel_id=1, source_target_pairs={{0,4},{4,0},{8,12},{12,8},{1,5},{5,1},{9,13},{13,9},{2,6},{6,2},{1... | collective-permute-start | bytes 147464 | tf_op jit(solution)/shard_map/ppermute | solution.py:438
  10.3 2.1 %copy-start.6 = (bf16[9,128,128]{2,1,0:T(8,128)(2,1)S(1)}, bf16[9,128,128]{2,1,0:T(8,128)(2,1)}, u32[]{:S(2)}) copy-start(bf16[9,128,128]{2,1,0:T(8,128)(2,1)} %w2.1) | copy-start | bytes 884740
  10.3 2.1 %copy-start.7 = (bf16[9,128,128]{2,1,0:T(8,128)(2,1)S(1)}, bf16[9,128,128]{2,1,0:T(8,128)(2,1)}, u32[]{:S(2)}) copy-start(bf16[9,128,128]{2,1,0:T(8,128)(2,1)} %wb.1) | copy-start | bytes 884740
  10.3 2.1 %copy-start.8 = (bf16[9,128,12]{1,2,0:T(8,128)(2,1)S(1)}, bf16[9,128,12]{1,2,0:T(8,128)(2,1)}, u32[]{:S(2)}) copy-start(bf16[9,128,12]{1,2,0:T(8,128)(2,1)} %param.14) | copy-start | bytes 82948
  10.4 5.0 %collective-permute-start.5 = (bf16[448,256]{1,0:T(8,128)(2,1)S(1)}, bf16[448,256]{1,0:T(8,128)(2,1)S(1)}, u32[]{:S(2)}, u32[]{:S(2)}) collective-permute-start(bf16[448,256]{1,0:T(8,128)(2,1)S(1)} %get-tuple-element.27.refs_8_), channel_id=1, source_target_pairs={{1,0},{0,1},{3,2},{2,3},{5,4},{4,5},{7,6},{6,7},{9,8},{8,9},{11,10... | collective-permute-start | bytes 688136 | tf_op jit(solution)/shard_map/ppermute | solution.py:524
  10.5 4.9 %collective-permute-start.3 = (bf16[152,256]{1,0:T(8,128)(2,1)S(1)}, bf16[152,256]{1,0:T(8,128)(2,1)S(1)}, u32[]{:S(2)}, u32[]{:S(2)}) collective-permute-start(bf16[152,256]{1,0:T(8,128)(2,1)S(1)} %get-tuple-element.28.strip_ref), channel_id=1, source_target_pairs={{2,0},{0,2},{3,1},{1,3},{6,4},{4,6},{7,5},{5,7},{10,8},{8,10},{11,... | collective-permute-start | bytes 233480 | tf_op jit(solution)/shard_map/ppermute | solution.py:532
  12.0 3.3 %collective-permute-start.4 = (bf16[32,256]{1,0:T(8,128)(2,1)S(1)}, bf16[32,256]{1,0:T(8,128)(2,1)S(1)}, u32[]{:S(2)}, u32[]{:S(2)}) collective-permute-start(bf16[32,256]{1,0:T(8,128)(2,1)S(1)} %corners.1), channel_id=1, source_target_pairs={{3,0},{2,1},{1,2},{0,3},{7,4},{6,5},{5,6},{4,7},{11,8},{10,9},{9,1... | collective-permute-start | bytes 49160 | tf_op jit(solution)/shard_map/ppermute | solution.py:530
  12.3 3.1 %copy-start = (bf16[1,128,64,128]{3,2,1,0:T(8,128)(2,1)S(1)}, bf16[1,128,64,128]{3,2,1,0:T(8,128)(2,1)}, u32[]{:S(2)}) copy-start(bf16[1,128,64,128]{3,2,1,0:T(8,128)(2,1)} %param.11) | copy-start | bytes 6291460
  12.3 3.1 %copy-start.2 = (f32[128]{0:T(128)S(1)}, f32[128]{0:T(128)}, u32[]{:S(2)}) copy-start(f32[128]{0:T(128)} %param.15) | copy-start | bytes 1540
  12.3 3.1 %copy-start.3 = (f32[128]{0:T(128)S(1)}, f32[128]{0:T(128)}, u32[]{:S(2)}) copy-start(f32[128]{0:T(128)} %param.17) | copy-start | bytes 1540
  12.4 3.1 %copy-start.4 = (f32[128]{0:T(128)S(1)}, f32[128]{0:T(128)}, u32[]{:S(2)}) copy-start(f32[128]{0:T(128)} %param.19) | copy-start | bytes 1540
  12.4 3.1 %copy-start.5 = (f32[128]{0:T(128)S(1)}, f32[128]{0:T(128)}, u32[]{:S(2)}) copy-start(f32[128]{0:T(128)} %param.20) | copy-start | bytes 1540

commit v6 on v5

--- a/solution.py
+++ b/solution.py
@@ -344,7 +344,7 @@
     bias1 = twice(b1[...])
     wide = TALL * cin
     lane = lax.broadcasted_iota(jnp.int32, (1, chans), 1)
-    per = 5
+    per = 9
     for w0 in range(0, windows, per):
         count = min(per, windows - w0)
         span = count * pitch

time: 29.3 us -> 29.1 us (level)
  no operation moved by 1% of the time
where the time goes in v6:
time: 29.1 us; the launch traced here: 29 us
  Pallas kernels  20.1 us (69%)
  starting transfers between devices  7.6 us (26%)
  between operations  0.96 us (3%)
  waiting for transfers between devices  0.33 us (1%)
    pallas_call x1, Pallas kernels, local(): pl.pallas_call(functools.partial(main_kernel, geo=geo, n_strip_in=n_strip...  13.4 us
    ppermute x3, starting transfers between devices, local(): lax.ppermute(condition, 'member', [(i, i ^ k) for i in range(n_member)])  5.68 us
    pallas_call x1, Pallas kernels, local(): pl.pallas_call(functools.partial(prep_kernel, pitch=pitch), out_shape=[ja...  3.04 us
    pallas_call x1, Pallas kernels, local(): pl.pallas_call(functools.partial(second_kernel, geo=geo, skip=split), out...  2.92 us
    ppermute x1, starting transfers between devices, local(): lax.ppermute(x, 'strip', move)  1.56 us
    pallas_call x1, Pallas kernels, local(): pl.pallas_call(functools.partial(first_kernel, pitch=pitch), out_shape=[j...  0.6 us
  transfers between devices with their start and end apart: 6, of which 2 were waited for; matrix products, arithmetic and copies ran while one was open for 0% of the time, Pallas kernels for 23%

profile of v6, /device:TPU:0, one launch (start us, length us, event | category | flops | bytes accessed | tf_op | source)
XLA Modules:
  0.0 29.0 jit_solution(365117515378499581)
XLA Ops:
  0.0 5.0 %collective-permute-start = (bf16[12,16,128]{2,1,0:T(8,128)(2,1)}, bf16[12,16,128]{2,1,0:T(8,128)(2,1)S(1)}, u32[]{:S(2)}, u32[]{:S(2)}) collective-permute-start(bf16[12,16,128]{2,1,0:T(8,128)(2,1)} %cond_hbm.1), channel_id=1, source_target_pairs={{0,12},{4,8},{8,4},{12,0},{1,13},{5,9},{9,5},{13,1},{2,14},{6,10},... | collective-permute-start | bytes 147464 | tf_op jit(solution)/shard_map/ppermute | solution.py:438
  5.1 0.0 collective-permute-start.2
  5.1 0.6 %collective-permute-start.1 = (bf16[12,16,128]{2,1,0:T(8,128)(2,1)}, bf16[12,16,128]{2,1,0:T(8,128)(2,1)S(1)}, u32[]{:S(2)}, u32[]{:S(2)}) collective-permute-start(bf16[12,16,128]{2,1,0:T(8,128)(2,1)} %cond_hbm.1), channel_id=1, source_target_pairs={{0,4},{4,0},{8,12},{12,8},{1,5},{5,1},{9,13},{13,9},{2,6},{6,2},{1... | collective-permute-start | bytes 147464 | tf_op jit(solution)/shard_map/ppermute | solution.py:438
  6.3 3.0 %prep.1 = (bf16[4368,256]{1,0:T(8,128)(2,1)S(1)}, bf16[64,256]{1,0:T(8,128)(2,1)S(1)}, bf16[64,256]{1,0:T(8,128)(2,1)S(1)}, bf16[12,16,128]{2,1,0:T(8,128)(2,1)S(1)}, f32[8,128]{1,0:T(8,128)S(1)}) custom-call(f32[8,128]{1,0:T(8,128)S(1)} %broadcast_in_dim.24.level_ref, bf16[128,64,128]{2,1,0:T(8,128)(2,1)} %bitcast.8, bf16[12,16,128]{2,1,0:T(8,128)(2,1)} %cond_hbm.1), custom_call_target="tpu_custom_call" | custom-call | bytes 16777216 | tf_op jit(solution)/shard_map/prep/pallas_call | solution.py:446
  9.4 0.0 copy-done.1
  9.4 0.6 %noisy_first.1 = (f32[544,256]{1,0:T(8,128)S(1)}, bf16[256,1280]{1,0:T(8,128)(2,1)S(1)}) custom-call(bf16[4368,256]{1,0:T(8,128)(2,1)S(1)} %get-tuple-element.20.pairs.refs_0_.refs_1_.refs_4_.refs_5_, bf16[9,128,256]{2,1,0:T(8,128)(2,1)S(1)} %copy-done.1), custom_call_target="tpu_custom_call" | custom-call | flops 301989888 | bytes 4194304 | tf_op jit(solution)/shard_map/noisy_first/pallas_call | solution.py:472
  10.0 0.0 collective-permute-done.refs_5_
  10.0 0.2 collective-permute-done.2.refs_7_
  10.3 0.0 collective-permute-done.1.refs_6_
  10.3 0.1 pack.1
  10.4 0.1 collective-permute-start.5
  10.5 1.6 %collective-permute-start.3 = (bf16[152,256]{1,0:T(8,128)(2,1)S(1)}, bf16[152,256]{1,0:T(8,128)(2,1)S(1)}, u32[]{:S(2)}, u32[]{:S(2)}) collective-permute-start(bf16[152,256]{1,0:T(8,128)(2,1)S(1)} %get-tuple-element.28.strip_ref), channel_id=1, source_target_pairs={{2,0},{0,2},{3,1},{1,3},{6,4},{4,6},{7,5},{5,7},{10,8},{8,10},{11,... | collective-permute-start | bytes 233480 | tf_op jit(solution)/shard_map/ppermute | solution.py:532
  12.0 0.3 %collective-permute-start.4 = (bf16[32,256]{1,0:T(8,128)(2,1)S(1)}, bf16[32,256]{1,0:T(8,128)(2,1)S(1)}, u32[]{:S(2)}, u32[]{:S(2)}) collective-permute-start(bf16[32,256]{1,0:T(8,128)(2,1)S(1)} %corners.1), channel_id=1, source_target_pairs={{3,0},{2,1},{1,2},{0,3},{7,4},{6,5},{5,6},{4,7},{11,8},{10,9},{9,1... | collective-permute-start | bytes 49160 | tf_op jit(solution)/shard_map/ppermute | solution.py:530
  12.3 0.0 copy-done.8
  12.3 0.0 copy-start.2
  12.3 0.0 copy-start.3
  12.4 0.0 copy-start.4
  12.4 0.0 copy-start.5
  12.4 2.9 %noisy_second.1 = (f32[3672,256]{1,0:T(8,128)S(1)}, bf16[256,512]{1,0:T(8,128)(2,1)S(1)}, bf16[256,1280]{1,0:T(8,128)(2,1)S(1)}, bf16[256,1280]{1,0:T(8,128)(2,1)S(1)}, bf16[256,1280]{1,0:T(8,128)(2,1)S(1)}) custom-call(bf16[4368,256]{1,0:T(8,128)(2,1)S(1)} %get-tuple-element.20.pairs.refs_0_.refs_1_.refs_4_.refs_5_, ...), custom_call_target="tpu_custom_call" | custom-call | flops 2038431744 | bytes 8388608 | tf_op jit(solution)/shard_map/noisy_second/pallas_call | solution.py:536
  15.3 0.0 collective-permute-done.4.refs_10_
  15.3 0.1 collective-permute-done.3.refs_9_
  15.4 0.0 collective-permute-done.5.refs_11_
  15.4 0.0 copy-done
  15.4 13.4 %denoise.1 = bf16[128,64,128]{2,1,0:T(8,128)(2,1)} custom-call(f32[8,128]{1,0:T(8,128)S(1)} %get-tuple-element.19.refs_0_, bf16[128,64,128]{2,1,0:T(8,128)(2,1)S(1)} %bitcast.9, f32[544,256]{1,0:T(8,128)S(1)} %get-tuple-element.21.refs_8_.refs_2_, f32[3672,256]{1,0:T(8,128)S(1)} %get-tuple-element.23.refs_3_, ...), custom_call_target="tpu_custom_call" | custom-call | tf_op jit(solution)/shard_map/denoise/pallas_call | solution.py:563
  (13 shorter events, 0.0 us)
Async XLA Ops:
  0.0 9.4 %copy-start.1 = (bf16[9,128,256]{2,1,0:T(8,128)(2,1)S(1)}, bf16[9,128,256]{2,1,0:T(8,128)(2,1)}, u32[]{:S(2)}) copy-start(bf16[9,128,256]{2,1,0:T(8,128)(2,1)} %wa.3) | copy-start | bytes 1769476
  0.0 10.0 %collective-permute-start = (bf16[12,16,128]{2,1,0:T(8,128)(2,1)}, bf16[12,16,128]{2,1,0:T(8,128)(2,1)S(1)}, u32[]{:S(2)}, u32[]{:S(2)}) collective-permute-start(bf16[12,16,128]{2,1,0:T(8,128)(2,1)} %cond_hbm.1), channel_id=1, source_target_pairs={{0,12},{4,8},{8,4},{12,0},{1,13},{5,9},{9,5},{13,1},{2,14},{6,10},... | collective-permute-start | bytes 147464 | tf_op jit(solution)/shard_map/ppermute | solution.py:438
  5.1 5.2 %collective-permute-start.2 = (bf16[12,16,128]{2,1,0:T(8,128)(2,1)}, bf16[12,16,128]{2,1,0:T(8,128)(2,1)S(1)}, u32[]{:S(2)}, u32[]{:S(2)}) collective-permute-start(bf16[12,16,128]{2,1,0:T(8,128)(2,1)} %cond_hbm.1), channel_id=1, source_target_pairs={{0,8},{4,12},{8,0},{12,4},{1,9},{5,13},{9,1},{13,5},{2,10},{6,14},... | collective-permute-start | bytes 147464 | tf_op jit(solution)/shard_map/ppermute | solution.py:438
  5.1 5.2 %collective-permute-start.1 = (bf16[12,16,128]{2,1,0:T(8,128)(2,1)}, bf16[12,16,128]{2,1,0:T(8,128)(2,1)S(1)}, u32[]{:S(2)}, u32[]{:S(2)}) collective-permute-start(bf16[12,16,128]{2,1,0:T(8,128)(2,1)} %cond_hbm.1), channel_id=1, source_target_pairs={{0,4},{4,0},{8,12},{12,8},{1,5},{5,1},{9,13},{13,9},{2,6},{6,2},{1... | collective-permute-start | bytes 147464 | tf_op jit(solution)/shard_map/ppermute | solution.py:438
  10.3 2.1 %copy-start.6 = (bf16[9,128,128]{2,1,0:T(8,128)(2,1)S(1)}, bf16[9,128,128]{2,1,0:T(8,128)(2,1)}, u32[]{:S(2)}) copy-start(bf16[9,128,128]{2,1,0:T(8,128)(2,1)} %w2.1) | copy-start | bytes 884740
  10.3 2.1 %copy-start.7 = (bf16[9,128,128]{2,1,0:T(8,128)(2,1)S(1)}, bf16[9,128,128]{2,1,0:T(8,128)(2,1)}, u32[]{:S(2)}) copy-start(bf16[9,128,128]{2,1,0:T(8,128)(2,1)} %wb.1) | copy-start | bytes 884740
  10.3 2.1 %copy-start.8 = (bf16[9,128,12]{1,2,0:T(8,128)(2,1)S(1)}, bf16[9,128,12]{1,2,0:T(8,128)(2,1)}, u32[]{:S(2)}) copy-start(bf16[9,128,12]{1,2,0:T(8,128)(2,1)} %param.14) | copy-start | bytes 82948
  10.4 5.0 %collective-permute-start.5 = (bf16[448,256]{1,0:T(8,128)(2,1)S(1)}, bf16[448,256]{1,0:T(8,128)(2,1)S(1)}, u32[]{:S(2)}, u32[]{:S(2)}) collective-permute-start(bf16[448,256]{1,0:T(8,128)(2,1)S(1)} %get-tuple-element.27.refs_8_), channel_id=1, source_target_pairs={{1,0},{0,1},{3,2},{2,3},{5,4},{4,5},{7,6},{6,7},{9,8},{8,9},{11,10... | collective-permute-start | bytes 688136 | tf_op jit(solution)/shard_map/ppermute | solution.py:524
  10.5 4.9 %collective-permute-start.3 = (bf16[152,256]{1,0:T(8,128)(2,1)S(1)}, bf16[152,256]{1,0:T(8,128)(2,1)S(1)}, u32[]{:S(2)}, u32[]{:S(2)}) collective-permute-start(bf16[152,256]{1,0:T(8,128)(2,1)S(1)} %get-tuple-element.28.strip_ref), channel_id=1, source_target_pairs={{2,0},{0,2},{3,1},{1,3},{6,4},{4,6},{7,5},{5,7},{10,8},{8,10},{11,... | collective-permute-start | bytes 233480 | tf_op jit(solution)/shard_map/ppermute | solution.py:532
  12.0 3.3 %collective-permute-start.4 = (bf16[32,256]{1,0:T(8,128)(2,1)S(1)}, bf16[32,256]{1,0:T(8,128)(2,1)S(1)}, u32[]{:S(2)}, u32[]{:S(2)}) collective-permute-start(bf16[32,256]{1,0:T(8,128)(2,1)S(1)} %corners.1), channel_id=1, source_target_pairs={{3,0},{2,1},{1,2},{0,3},{7,4},{6,5},{5,6},{4,7},{11,8},{10,9},{9,1... | collective-permute-start | bytes 49160 | tf_op jit(solution)/shard_map/ppermute | solution.py:530
  12.3 3.1 %copy-start = (bf16[1,128,64,128]{3,2,1,0:T(8,128)(2,1)S(1)}, bf16[1,128,64,128]{3,2,1,0:T(8,128)(2,1)}, u32[]{:S(2)}) copy-start(bf16[1,128,64,128]{3,2,1,0:T(8,128)(2,1)} %param.11) | copy-start | bytes 6291460
  12.3 3.1 %copy-start.2 = (f32[128]{0:T(128)S(1)}, f32[128]{0:T(128)}, u32[]{:S(2)}) copy-start(f32[128]{0:T(128)} %param.15) | copy-start | bytes 1540
  12.3 3.1 %copy-start.3 = (f32[128]{0:T(128)S(1)}, f32[128]{0:T(128)}, u32[]{:S(2)}) copy-start(f32[128]{0:T(128)} %param.17) | copy-start | bytes 1540
  12.4 3.1 %copy-start.4 = (f32[128]{0:T(128)S(1)}, f32[128]{0:T(128)}, u32[]{:S(2)}) copy-start(f32[128]{0:T(128)} %param.19) | copy-start | bytes 1540
  12.4 3.1 %copy-start.5 = (f32[128]{0:T(128)S(1)}, f32[128]{0:T(128)}, u32[]{:S(2)}) copy-start(f32[128]{0:T(128)} %param.20) | copy-start | bytes 1540
